TPU v7x, 32 devices: a whole 2x2x4 slice. The times are simulated.
32 devices in a mesh: ctx: 8 (over y, x, core), fsdp: 4 (over z).
Axes of the slice: x: 2, y: 2, z: 4, core: 2. Of those that a mesh axis runs over, the one named last changes fastest.
Arguments:
- hidden_in: bfloat16 [4, 1024, 2048], P('fsdp', 'ctx'), may hold values from -6 to 6
- out_grad: bfloat16 [4, 1024, 2048], P('fsdp', 'ctx'), may hold values from -6 to 6
- doc_ids: int32 [4, 1024], P('fsdp', 'ctx'), may hold values from 0 to 2, as said below
- norm_gain: bfloat16 [2048], P(('ctx', 'fsdp')), may hold values from 0.5 to 1.5
- query_weight: bfloat16 [2048, 1024], P(('ctx', 'fsdp')), may hold values from -0.125 to 0.125
- key_matrix: bfloat16 [2048, 256], P(('ctx', 'fsdp')), may hold values from -0.125 to 0.125
- value_matrix: bfloat16 [2048, 256], P(('ctx', 'fsdp')), may hold values from -0.125 to 0.125
- attn_out_weight: bfloat16 [1024, 2048], P(('ctx', 'fsdp')), may hold values from -2 to 2
- mixer_gate_weight: bfloat16 [2048, 3072], P(('ctx', 'fsdp')), may hold values from -0.125 to 0.125
- conv_in_weight: bfloat16 [2048, 3584], P(('ctx', 'fsdp')), may hold values from -0.125 to 0.125
- step_weight: bfloat16 [2048, 48], P(('ctx', 'fsdp')), may hold values from -0.125 to 0.125
- conv_weight: bfloat16 [4, 3584], P(None, ('ctx', 'fsdp')), may hold values from -3 to 3
- conv_bias: bfloat16 [3584], P(('ctx', 'fsdp')), may hold values from -3 to 3
- step_bias: float32 [48], replicated, may hold values from -5 to -1
- log_decay: float32 [48], replicated, may hold values from -7 to 1
- skip_gain: float32 [48], replicated, may hold values from 0.5 to 1.5
- mixer_gain: bfloat16 [3072], P(('ctx', 'fsdp')), may hold values from 0.5 to 1.5
- mamba_out_weight: bfloat16 [3072, 2048], P(('ctx', 'fsdp')), may hold values from -0.109375 to 0.109375
- ffn_gain: bfloat16 [2048], P(('ctx', 'fsdp')), may hold values from 0.5 to 1.5
- gate_weight: bfloat16 [2048, 4096], P(('ctx', 'fsdp')), may hold values from -0.125 to 0.125
- up_weight: bfloat16 [2048, 4096], P(('ctx', 'fsdp')), may hold values from -0.125 to 0.125
- down_weight: bfloat16 [4096, 2048], P(('ctx', 'fsdp')), may hold values from -0.09375 to 0.09375
Outputs:
- block_out: bfloat16 [4, 1024, 2048], P('fsdp', 'ctx')
- input_grad: bfloat16 [4, 1024, 2048], P('fsdp', 'ctx')
- norm_gain_grad: float32 [2048], P(('ctx', 'fsdp'))
- query_weight_grad: float32 [2048, 1024], P(('ctx', 'fsdp'))
- key_weight_grad: float32 [2048, 256], P(('ctx', 'fsdp'))
- value_weight_grad: float32 [2048, 256], P(('ctx', 'fsdp'))
- attn_out_weight_grad: float32 [1024, 2048], P(('ctx', 'fsdp'))
- mixer_gate_weight_grad: float32 [2048, 3072], P(('ctx', 'fsdp'))
- conv_in_weight_grad: float32 [2048, 3584], P(('ctx', 'fsdp'))
- step_weight_grad: float32 [2048, 48], P(('ctx', 'fsdp'))
- conv_weight_grad: float32 [4, 3584], P(None, ('ctx', 'fsdp'))
- conv_bias_grad: float32 [3584], P(('ctx', 'fsdp'))
- step_bias_grad: float32 [48], replicated
- log_decay_grad: float32 [48], replicated
- skip_gain_grad: float32 [48], replicated
- mixer_gain_grad: float32 [3072], P(('ctx', 'fsdp'))
- mamba_out_weight_grad: float32 [3072, 2048], P(('ctx', 'fsdp'))
- ffn_gain_grad: float32 [2048], P(('ctx', 'fsdp'))
- gate_weight_grad: float32 [2048, 4096], P(('ctx', 'fsdp'))
- up_weight_grad: float32 [2048, 4096], P(('ctx', 'fsdp'))
- down_weight_grad: float32 [4096, 2048], P(('ctx', 'fsdp'))
Inputs may be any that keep to these rules, and one draw needn't show every extreme that they name: `doc_ids`: each row never falls and holds three documents: the first starts the sequence and ends within its first 64 places, the last begins within its last 64 places.
All inputs are finite; a program needn't handle non-finite values.
Results may differ from a plain program's by a relative error of at most 0.023.
Values may be sent and summed in bfloat16 or wider, within the bound.
A program may use at most 448 MiB of HBM per device.

v0:
```python
from functools import partial
import math

import jax
import jax.numpy as jnp
from jax import lax
from jax.sharding import PartitionSpec as P

QUERY_HEADS = 8
KEY_VALUE_HEADS = 2
HEAD_SIZE = 128
HS = 48
HP = 64
STATE = 256
CONV = 4


EPSILON = 1e-05
ROPE_BASE = 100000000000.0
NEGATIVE_FLOOR = -1e30
HIGHEST = lax.Precision.HIGHEST


def shifted(value, axis, steps):
    count = lax.axis_size(axis)
    leading, last = (max(0, -steps), min(count, count - steps))
    return lax.ppermute(value, axis, [(source, source + steps) for source in range(leading, last)])


def prefix(shard, axis, combine, identity):
    devices, position = (lax.axis_size(axis), lax.axis_index(axis))
    everything = jax.tree.map(
        lambda part, kind: lax.all_gather(part.astype(kind), axis),
        shard,
        (jnp.bfloat16, jnp.bfloat16),
    )
    start = jax.tree.map(
        lambda part, zero: jnp.broadcast_to(jnp.asarray(zero, part.dtype), part.shape),
        shard,
        identity,
    )

    def step(k, before):
        reached = k < position
        new = combine(
            before, jax.tree.map(lambda part, own: part[k].astype(own.dtype), everything, shard)
        )
        return jax.tree.map(lambda a, b: jnp.where(reached, a, b), new, before)

    return lax.fori_loop(0, devices, step, start)


def carried_in(shard, axis, join, neutral):
    count = lax.axis_size(axis)
    place = lax.axis_index(axis)
    ahead = count - 1 - place
    gathered = jax.tree.map(
        lambda a, kind: lax.all_gather(a.astype(kind), axis),
        shard,
        jax.tree.map(lambda a: jnp.bfloat16 if a.dtype == jnp.float32 else a.dtype, shard),
    )
    state = jax.tree.map(lambda a, e: jnp.zeros_like(a) + jnp.asarray(e, a.dtype), shard, neutral)

    def one(step, state):
        source = count - 1 - step
        return join(
            state,
            jax.tree.map(
                lambda a, own: lax.dynamic_index_in_dim(a, source, 0, False).astype(own.dtype),
                gathered,
                shard,
            ),
        )

    return lax.fori_loop(0, ahead, one, state)


def rms_scale(values, gain):
    return values * lax.rsqrt(jnp.mean(values * values, axis=-1, keepdims=True) + EPSILON) * gain


def rotate(values, places):
    half_size = values.shape[-1] // 2
    freqs = ROPE_BASE ** (-jnp.arange(half_size).astype(jnp.float32) / half_size)
    angles = places[:, None] * freqs[None, :]
    cosine = jnp.cos(angles)[:, None, :]
    sine = jnp.sin(angles)[:, None, :]
    first = values[..., :half_size]
    second = values[..., half_size:]
    return jnp.concatenate(
        [first * cosine - second * sine, second * cosine + first * sine], axis=-1
    )


def conv_part(widened, taps_weight, bias, widened_docs, documents):
    row_length_total = documents.shape[0]
    total = bias[None, :]
    for tap_index in range(taps_weight.shape[0]):
        same_doc = (widened_docs[tap_index : tap_index + row_length_total] == documents)[:, None]
        total = total + jnp.where(
            same_doc,
            widened[tap_index : tap_index + row_length_total] * taps_weight[tap_index][None, :],
            0.0,
        )
    return jax.nn.silu(total)


def step_part(step_lin, step_bias, log_decay):
    return (jax.nn.softplus(step_lin + step_bias), -jnp.exp(log_decay))


def block_stats(mixer_in, write_proj, step_size, decay_rate, documents, prior_doc):
    decay_log = jnp.cumsum(step_size * decay_rate[None, :], axis=0)
    last_doc = documents[-1]
    tail_weight = (
        jnp.where(
            (documents == last_doc)[:, None], jnp.exp(decay_log[-1][None, :] - decay_log), 0.0
        )
        * step_size
    )
    state_loc = jnp.einsum(
        "thp,tn->hpn", mixer_in * tail_weight[:, :, None], write_proj, precision=HIGHEST
    )
    carry_decay = jnp.exp(decay_log[-1]) * (last_doc == prior_doc).astype(jnp.float32)
    return (state_loc, carry_decay)


def block_mix(
    mixer_in,
    write_proj,
    read_proj,
    step_size,
    decay_rate,
    skip_gain,
    state_in,
    documents,
    prior_doc,
):
    decay_log = jnp.cumsum(step_size * decay_rate[None, :], axis=0)
    positions = jnp.arange(documents.shape[0])
    visible = (documents[:, None] == documents[None, :]) & (
        positions[:, None] >= positions[None, :]
    )
    spread = decay_log.T[:, :, None] - decay_log.T[:, None, :]
    decay_pair = jnp.where(visible[None], jnp.exp(jnp.where(visible[None], spread, 0.0)), 0.0)
    gram = jnp.dot(read_proj, write_proj.T, precision=HIGHEST)
    mixing = decay_pair * gram[None] * step_size.T[:, None, :]
    inner = jnp.einsum("htu,uhp->thp", mixing, mixer_in, precision=HIGHEST)
    entry = jnp.where((documents == prior_doc)[:, None], jnp.exp(decay_log), 0.0)
    carried = jnp.einsum("tn,hpn->thp", read_proj, state_in, precision=HIGHEST) * entry[:, :, None]
    return inner + carried + skip_gain[None, :, None] * mixer_in


def gated_norm(flat_mixed, mixer_gate, gain):
    return rms_scale(flat_mixed * jax.nn.silu(mixer_gate), gain)


def chain_combine(earlier, later):
    decay_early, state_early = earlier
    decay_late, state_late = later
    return (decay_early * decay_late, decay_late[:, None, None] * state_early + state_late)


def piece_scores(piece, start, query_group, query_docs, query_places):
    key_segment, value_segment, docs_piece = piece
    segment_rows = key_segment.shape[0]
    heads_of_key = key_segment.reshape(segment_rows, KEY_VALUE_HEADS, HEAD_SIZE).transpose(1, 0, 2)
    heads_of_value = value_segment.reshape(segment_rows, KEY_VALUE_HEADS, HEAD_SIZE).transpose(
        1, 0, 2
    )
    key_places = (start + jnp.arange(segment_rows)).astype(jnp.float32)
    visible = (docs_piece.astype(jnp.float32)[None, :] == query_docs[:, None]) & (
        key_places[None, :] <= query_places[:, None]
    )
    scores = jnp.einsum(
        "gqd,gkd->gqk", query_group, heads_of_key, preferred_element_type=jnp.float32
    ) * HEAD_SIZE ** (-0.5)
    return (heads_of_key, heads_of_value, visible, jnp.where(visible[None], scores, NEGATIVE_FLOOR))


def fold_local(step_fn, whole, start_carry):
    row_length_total = whole[0].shape[0]
    tile_block = math.gcd(row_length_total, 512)

    def advance(block_index, carry):
        start = block_index * tile_block
        piece = tuple((lax.dynamic_slice_in_dim(member, start, tile_block, 0) for member in whole))
        return step_fn(carry, piece, start)

    return lax.fori_loop(0, row_length_total // tile_block, advance, start_carry)


def on_device(
    hidden_in,
    out_grad,
    doc_ids,
    norm_gain,
    query_weight,
    key_matrix,
    value_matrix,
    attn_out_weight,
    mixer_gate_weight,
    conv_in_weight,
    step_weight,
    conv_weight,
    conv_bias,
    step_bias,
    log_decay,
    skip_gain,
    mixer_gain,
    mamba_out_weight,
    ffn_gain,
    gate_weight,
    up_weight,
    down_weight,
):
    single_float = jnp.float32
    brain_float_half = jnp.bfloat16
    (
        norm_full,
        query_full,
        complete_key,
        value_full,
        attn_out_full,
        mixer_gate_full,
        conv_in_full,
        step_full,
        conv_full,
        conv_bias_full,
        mixer_gain_full,
        mamba_out_full,
    ) = (
        lax.all_gather(norm_gain, ("ctx", "fsdp"), axis=0, tiled=True),
        lax.all_gather(query_weight, ("ctx", "fsdp"), axis=0, tiled=True),
        lax.all_gather(key_matrix, ("ctx", "fsdp"), axis=0, tiled=True),
        lax.all_gather(value_matrix, ("ctx", "fsdp"), axis=0, tiled=True),
        lax.all_gather(attn_out_weight, ("ctx", "fsdp"), axis=0, tiled=True),
        lax.all_gather(mixer_gate_weight, ("ctx", "fsdp"), axis=0, tiled=True),
        lax.all_gather(conv_in_weight, ("ctx", "fsdp"), axis=0, tiled=True),
        lax.all_gather(step_weight, ("ctx", "fsdp"), axis=0, tiled=True),
        lax.all_gather(conv_weight, ("ctx", "fsdp"), axis=1, tiled=True),
        lax.all_gather(conv_bias, ("ctx", "fsdp"), axis=0, tiled=True),
        lax.all_gather(mixer_gain, ("ctx", "fsdp"), axis=0, tiled=True),
        lax.all_gather(mamba_out_weight, ("ctx", "fsdp"), axis=0, tiled=True),
    )
    tokens_per_worker = hidden_in.shape[1]
    head_cluster = QUERY_HEADS // KEY_VALUE_HEADS
    dssm = HS * HP
    taps = CONV - 1
    resid = hidden_in[0].astype(single_float)
    documents = doc_ids[0]
    places = (lax.axis_index("ctx") * tokens_per_worker + jnp.arange(tokens_per_worker)).astype(
        single_float
    )
    norm_one, norm_one_back = jax.vjp(rms_scale, resid, norm_full.astype(single_float))
    normalized_input = norm_one.astype(brain_float_half)
    query_lin = jnp.dot(normalized_input, query_full, preferred_element_type=single_float).reshape(
        tokens_per_worker, QUERY_HEADS, HEAD_SIZE
    )
    key_linear = jnp.dot(
        normalized_input, complete_key, preferred_element_type=single_float
    ).reshape(tokens_per_worker, KEY_VALUE_HEADS, HEAD_SIZE)
    query_turned, unturn_query = jax.vjp(partial(rotate, places=places), query_lin)
    rotated_key, unrotate_key = jax.vjp(partial(rotate, places=places), key_linear)
    rotated_query = query_turned.astype(brain_float_half)
    flattened_key = rotated_key.astype(brain_float_half).reshape(
        tokens_per_worker, KEY_VALUE_HEADS * HEAD_SIZE
    )
    value_lowered = jnp.dot(
        normalized_input, value_full, preferred_element_type=single_float
    ).astype(brain_float_half)
    docs_low = documents.astype(brain_float_half)
    query_group = (
        rotated_query.reshape(tokens_per_worker, KEY_VALUE_HEADS, head_cluster, HEAD_SIZE)
        .transpose(1, 2, 0, 3)
        .reshape(KEY_VALUE_HEADS, head_cluster * tokens_per_worker, HEAD_SIZE)
    )
    query_places = jnp.tile(places, head_cluster)
    query_docs = jnp.tile(documents.astype(single_float), head_cluster)

    def attend_piece(carry, piece, start):
        previous_maximum, total_old, summed_old = carry
        heads_of_key, heads_of_value, visible, scores = piece_scores(
            piece, start, query_group, query_docs, query_places
        )
        peak_new = jnp.maximum(previous_maximum, jnp.max(scores, axis=-1))
        weights = jnp.where(visible[None], jnp.exp(scores - peak_new[:, :, None]), 0.0)
        factor = jnp.exp(previous_maximum - peak_new)
        total_new = total_old * factor + jnp.sum(weights, axis=-1)
        summed_new = summed_old * factor[:, :, None] + jnp.einsum(
            "gqk,gkd->gqd",
            weights.astype(brain_float_half),
            heads_of_value,
            preferred_element_type=single_float,
        )
        return (peak_new, total_new, summed_new)

    rows_of_query = head_cluster * tokens_per_worker
    start_forward = (
        jnp.full((KEY_VALUE_HEADS, rows_of_query), NEGATIVE_FLOOR, single_float),
        jnp.zeros((KEY_VALUE_HEADS, rows_of_query), single_float),
        jnp.zeros((KEY_VALUE_HEADS, rows_of_query, HEAD_SIZE), single_float),
    )
    kv_whole = (
        lax.all_gather(flattened_key, "ctx", axis=0, tiled=True),
        lax.all_gather(value_lowered, "ctx", axis=0, tiled=True),
        lax.all_gather(docs_low, "ctx", axis=0, tiled=True),
    )
    peak, total, summed = fold_local(attend_piece, kv_whole, start_forward)
    attention_cluster = summed / total[:, :, None]
    log_total = peak + jnp.log(total)
    attn_low = (
        attention_cluster.reshape(KEY_VALUE_HEADS, head_cluster, tokens_per_worker, HEAD_SIZE)
        .transpose(2, 0, 1, 3)
        .reshape(tokens_per_worker, QUERY_HEADS * HEAD_SIZE)
        .astype(brain_float_half)
    )
    attn_out = jnp.dot(attn_low, attn_out_full, preferred_element_type=single_float)
    mixer_gate = jnp.dot(normalized_input, mixer_gate_full, preferred_element_type=single_float)
    conv_lin = jnp.dot(normalized_input, conv_in_full, preferred_element_type=single_float).astype(
        brain_float_half
    )
    step_lin = jnp.dot(normalized_input, step_full, preferred_element_type=single_float)
    rim_rows, rim_docs = shifted(
        (conv_lin[tokens_per_worker - taps :], docs_low[tokens_per_worker - taps :]), "ctx", 1
    )
    widened = jnp.concatenate([rim_rows, conv_lin], axis=0).astype(single_float)
    widened_docs = jnp.concatenate([rim_docs.astype(jnp.int32), documents])
    prior_doc = widened_docs[taps - 1]
    conv_act, conv_back = jax.vjp(
        partial(conv_part, widened_docs=widened_docs, documents=documents),
        widened,
        conv_full.astype(single_float),
        conv_bias_full.astype(single_float),
    )
    conv_vals = conv_act.astype(brain_float_half).astype(single_float)
    mixer_in = conv_vals[:, :dssm].reshape(tokens_per_worker, HS, HP)
    write_proj = conv_vals[:, dssm : dssm + STATE]
    read_proj = conv_vals[:, dssm + STATE :]
    (step_size, decay_rate), step_back = jax.vjp(step_part, step_lin, step_bias, log_decay)
    (state_loc, carry_decay), stats_back = jax.vjp(
        partial(block_stats, documents=documents, prior_doc=prior_doc),
        mixer_in,
        write_proj,
        step_size,
        decay_rate,
    )
    chain_identity = (jnp.ones_like(carry_decay), jnp.zeros_like(state_loc))
    _, state_in = prefix((carry_decay, state_loc), "ctx", chain_combine, chain_identity)
    mixed, mix_back = jax.vjp(
        partial(block_mix, documents=documents, prior_doc=prior_doc),
        mixer_in,
        write_proj,
        read_proj,
        step_size,
        decay_rate,
        skip_gain,
        state_in,
    )
    ymix_vals, gate_back = jax.vjp(
        gated_norm,
        mixed.reshape(tokens_per_worker, dssm),
        mixer_gate,
        mixer_gain_full.astype(single_float),
    )
    ymix_low = ymix_vals.astype(brain_float_half)
    mamba_out = jnp.dot(ymix_low, mamba_out_full, preferred_element_type=single_float)
    ffn_gain_full, gate_full, up_full, down_full = (
        lax.all_gather(ffn_gain, ("ctx", "fsdp"), axis=0, tiled=True),
        lax.all_gather(gate_weight, ("ctx", "fsdp"), axis=0, tiled=True),
        lax.all_gather(up_weight, ("ctx", "fsdp"), axis=0, tiled=True),
        lax.all_gather(down_weight, ("ctx", "fsdp"), axis=0, tiled=True),
    )
    mid = resid + attn_out + mamba_out
    norm_two, norm_two_back = jax.vjp(rms_scale, mid, ffn_gain_full.astype(single_float))
    normed_two = norm_two.astype(brain_float_half)
    gate_lin = jnp.dot(normed_two, gate_full, preferred_element_type=single_float)
    up_lin = jnp.dot(normed_two, up_full, preferred_element_type=single_float)
    sigmoid_gate = jax.nn.sigmoid(gate_lin)
    silu_gate = gate_lin * sigmoid_gate
    hidden = (silu_gate * up_lin).astype(brain_float_half)
    block_out = (mid + jnp.dot(hidden, down_full, preferred_element_type=single_float)).astype(
        brain_float_half
    )
    grad_out = out_grad[0]
    down_grad_w = jnp.einsum("tf,td->fd", hidden, grad_out, preferred_element_type=single_float)
    grad_hidden = jnp.einsum("td,fd->tf", grad_out, down_full, preferred_element_type=single_float)
    grad_gate = (grad_hidden * up_lin * (sigmoid_gate + silu_gate * (1.0 - sigmoid_gate))).astype(
        brain_float_half
    )
    grad_up = (grad_hidden * silu_gate).astype(brain_float_half)
    gate_grad_w = jnp.einsum(
        "td,tf->df", normed_two, grad_gate, preferred_element_type=single_float
    )
    up_grad_w = jnp.einsum("td,tf->df", normed_two, grad_up, preferred_element_type=single_float)
    grad_normed_two = jnp.einsum(
        "tf,df->td", grad_gate, gate_full, preferred_element_type=single_float
    ) + jnp.einsum("tf,df->td", grad_up, up_full, preferred_element_type=single_float)
    grad_mid_norm, ffn_gain_grad = norm_two_back(grad_normed_two)
    grad_mid = grad_out.astype(single_float) + grad_mid_norm
    ffn_sums = (
        lax.psum_scatter(ffn_gain_grad, ("ctx", "fsdp"), scatter_dimension=0, tiled=True),
        lax.psum_scatter(gate_grad_w, ("ctx", "fsdp"), scatter_dimension=0, tiled=True),
        lax.psum_scatter(up_grad_w, ("ctx", "fsdp"), scatter_dimension=0, tiled=True),
        lax.psum_scatter(down_grad_w, ("ctx", "fsdp"), scatter_dimension=0, tiled=True),
    )
    branch_grad = grad_mid.astype(brain_float_half)
    attn_out_grad_w = jnp.einsum(
        "ti,td->id", attn_low, branch_grad, preferred_element_type=single_float
    )
    attention_gradient = jnp.einsum(
        "td,id->ti", branch_grad, attn_out_full, preferred_element_type=single_float
    ).astype(brain_float_half)
    grad_group = (
        attention_gradient.reshape(tokens_per_worker, KEY_VALUE_HEADS, head_cluster, HEAD_SIZE)
        .transpose(1, 2, 0, 3)
        .reshape(KEY_VALUE_HEADS, rows_of_query, HEAD_SIZE)
    )
    row_delta = jnp.sum(grad_group.astype(single_float) * attention_cluster, axis=-1)

    def attend_back(carry, piece, start):
        query_acc, kv_grad = carry
        heads_of_key, heads_of_value, visible, scores = piece_scores(
            piece, start, query_group, query_docs, query_places
        )
        segment_rows = heads_of_key.shape[1]
        probs = jnp.where(visible[None], jnp.exp(scores - log_total[:, :, None]), 0.0)
        prob_grad = jnp.einsum(
            "gqd,gkd->gqk", grad_group, heads_of_value, preferred_element_type=single_float
        )
        score_grad = (probs * (prob_grad - row_delta[:, :, None])).astype(brain_float_half)
        query_acc = query_acc + jnp.einsum(
            "gqk,gkd->gqd", score_grad, heads_of_key, preferred_element_type=single_float
        )
        key_portion = jnp.einsum(
            "gqk,gqd->kgd", score_grad, query_group, preferred_element_type=single_float
        ) * HEAD_SIZE ** (-0.5)
        value_portion = jnp.einsum(
            "gqk,gqd->kgd",
            probs.astype(brain_float_half),
            grad_group,
            preferred_element_type=single_float,
        )
        term = jnp.concatenate(
            [
                key_portion.reshape(segment_rows, KEY_VALUE_HEADS * HEAD_SIZE),
                value_portion.reshape(segment_rows, KEY_VALUE_HEADS * HEAD_SIZE),
            ],
            axis=1,
        )
        current = lax.dynamic_slice_in_dim(kv_grad, start, segment_rows, 0)
        kv_grad = lax.dynamic_update_slice_in_dim(kv_grad, current + term, start, 0)
        return (query_acc, kv_grad)

    start_back = (
        jnp.zeros((KEY_VALUE_HEADS, rows_of_query, HEAD_SIZE), single_float),
        jnp.zeros(
            (tokens_per_worker * lax.axis_size("ctx"), 2 * KEY_VALUE_HEADS * HEAD_SIZE),
            single_float,
        ),
    )
    query_acc, kv_grad = fold_local(attend_back, kv_whole, start_back)
    local_key_value = lax.psum_scatter(
        kv_grad.astype(jnp.bfloat16), "ctx", scatter_dimension=0, tiled=True
    ).astype(jnp.float32)
    query_turn_grad = (
        (query_acc * HEAD_SIZE ** (-0.5))
        .reshape(KEY_VALUE_HEADS, head_cluster, tokens_per_worker, HEAD_SIZE)
        .transpose(2, 0, 1, 3)
        .reshape(tokens_per_worker, QUERY_HEADS, HEAD_SIZE)
    )
    query_lin_grad = (
        unturn_query(query_turn_grad)[0]
        .reshape(tokens_per_worker, QUERY_HEADS * HEAD_SIZE)
        .astype(brain_float_half)
    )
    key_lin_grad = (
        unrotate_key(
            local_key_value[:, : KEY_VALUE_HEADS * HEAD_SIZE].reshape(
                tokens_per_worker, KEY_VALUE_HEADS, HEAD_SIZE
            )
        )[0]
        .reshape(tokens_per_worker, KEY_VALUE_HEADS * HEAD_SIZE)
        .astype(brain_float_half)
    )
    value_linear_gradient = local_key_value[:, KEY_VALUE_HEADS * HEAD_SIZE :].astype(
        brain_float_half
    )
    mamba_grad_w = jnp.einsum(
        "ti,td->id", ymix_low, branch_grad, preferred_element_type=single_float
    )
    grad_ymix = jnp.einsum(
        "td,id->ti", branch_grad, mamba_out_full, preferred_element_type=single_float
    )
    grad_mixed, grad_zgate, mixer_gain_grad = gate_back(grad_ymix)
    zgate_low = grad_zgate.astype(brain_float_half)
    (
        grad_in_mix,
        grad_write_mix,
        grad_read,
        grad_step_mix,
        grad_rate_mix,
        skip_grad,
        grad_state_in,
    ) = mix_back(grad_mixed.reshape(tokens_per_worker, HS, HP))
    _, state_later = carried_in((carry_decay, grad_state_in), "ctx", chain_combine, chain_identity)
    decay_grad = jnp.sum(state_in * state_later, axis=(1, 2))
    grad_in_stats, grad_write_stats, grad_step_stats, grad_rate_stats = stats_back(
        (state_later, decay_grad)
    )
    grad_conv = jnp.concatenate(
        [
            (grad_in_mix + grad_in_stats).reshape(tokens_per_worker, dssm),
            grad_write_mix + grad_write_stats,
            grad_read,
        ],
        axis=1,
    )
    grad_widened, conv_weight_grad, conv_bias_grad = conv_back(grad_conv)
    rim_grad = shifted(grad_widened[:taps].astype(jnp.bfloat16), "ctx", -1).astype(jnp.float32)
    conv_lin_grad = (
        grad_widened[taps:].at[tokens_per_worker - taps :].add(rim_grad).astype(brain_float_half)
    )
    step_lin_grad, step_bias_grad, log_decay_grad = step_back(
        (grad_step_mix + grad_step_stats, grad_rate_mix + grad_rate_stats)
    )
    step_lin_low = step_lin_grad.astype(brain_float_half)
    query_grad_w = jnp.einsum(
        "td,ti->di", normalized_input, query_lin_grad, preferred_element_type=single_float
    )
    key_grad_w = jnp.einsum(
        "td,ti->di", normalized_input, key_lin_grad, preferred_element_type=single_float
    )
    value_grad_w = jnp.einsum(
        "td,ti->di", normalized_input, value_linear_gradient, preferred_element_type=single_float
    )
    zgate_grad_w = jnp.einsum(
        "td,ti->di", normalized_input, zgate_low, preferred_element_type=single_float
    )
    conv_in_grad_w = jnp.einsum(
        "td,ti->di", normalized_input, conv_lin_grad, preferred_element_type=single_float
    )
    step_grad_w = jnp.einsum(
        "td,ti->di", normalized_input, step_lin_low, preferred_element_type=single_float
    )
    grad_normed = (
        jnp.einsum("ti,di->td", query_lin_grad, query_full, preferred_element_type=single_float)
        + jnp.einsum("ti,di->td", key_lin_grad, complete_key, preferred_element_type=single_float)
        + jnp.einsum(
            "ti,di->td", value_linear_gradient, value_full, preferred_element_type=single_float
        )
        + jnp.einsum("ti,di->td", zgate_low, mixer_gate_full, preferred_element_type=single_float)
        + jnp.einsum("ti,di->td", conv_lin_grad, conv_in_full, preferred_element_type=single_float)
        + jnp.einsum("ti,di->td", step_lin_low, step_full, preferred_element_type=single_float)
    )
    grad_resid_norm, norm_gain_grad = norm_one_back(grad_normed)
    input_grad = (grad_mid + grad_resid_norm).astype(brain_float_half)
    mixer_sums = (
        lax.psum_scatter(norm_gain_grad, ("ctx", "fsdp"), scatter_dimension=0, tiled=True),
        lax.psum_scatter(query_grad_w, ("ctx", "fsdp"), scatter_dimension=0, tiled=True),
        lax.psum_scatter(key_grad_w, ("ctx", "fsdp"), scatter_dimension=0, tiled=True),
        lax.psum_scatter(value_grad_w, ("ctx", "fsdp"), scatter_dimension=0, tiled=True),
        lax.psum_scatter(attn_out_grad_w, ("ctx", "fsdp"), scatter_dimension=0, tiled=True),
        lax.psum_scatter(zgate_grad_w, ("ctx", "fsdp"), scatter_dimension=0, tiled=True),
        lax.psum_scatter(conv_in_grad_w, ("ctx", "fsdp"), scatter_dimension=0, tiled=True),
        lax.psum_scatter(step_grad_w, ("ctx", "fsdp"), scatter_dimension=0, tiled=True),
        lax.psum_scatter(conv_weight_grad, ("ctx", "fsdp"), scatter_dimension=1, tiled=True),
        lax.psum_scatter(conv_bias_grad, ("ctx", "fsdp"), scatter_dimension=0, tiled=True),
        lax.psum_scatter(mixer_gain_grad, ("ctx", "fsdp"), scatter_dimension=0, tiled=True),
        lax.psum_scatter(mamba_grad_w, ("ctx", "fsdp"), scatter_dimension=0, tiled=True),
    )
    summed_grads = tuple(mixer_sums) + tuple(ffn_sums)
    step_bias_sum, log_decay_sum, skip_sum = lax.psum(
        (step_bias_grad, log_decay_grad, skip_grad), ("ctx", "fsdp")
    )
    return (
        block_out[None],
        input_grad[None],
        summed_grads[0],
        summed_grads[1],
        summed_grads[2],
        summed_grads[3],
        summed_grads[4],
        summed_grads[5],
        summed_grads[6],
        summed_grads[7],
        summed_grads[8],
        summed_grads[9],
        step_bias_sum,
        log_decay_sum,
        skip_sum,
        summed_grads[10],
        summed_grads[11],
        summed_grads[12],
        summed_grads[13],
        summed_grads[14],
        summed_grads[15],
    )


def solution(mesh):
    placed = (
        P("fsdp", "ctx", None),
        P("fsdp", "ctx", None),
        P("fsdp", "ctx"),
        P(("ctx", "fsdp")),
        P(("ctx", "fsdp"), None),
        P(("ctx", "fsdp"), None),
        P(("ctx", "fsdp"), None),
        P(("ctx", "fsdp"), None),
        P(("ctx", "fsdp"), None),
        P(("ctx", "fsdp"), None),
        P(("ctx", "fsdp"), None),
        P(None, ("ctx", "fsdp")),
        P(("ctx", "fsdp")),
        P(),
        P(),
        P(),
        P(("ctx", "fsdp")),
        P(("ctx", "fsdp"), None),
        P(("ctx", "fsdp")),
        P(("ctx", "fsdp"), None),
        P(("ctx", "fsdp"), None),
        P(("ctx", "fsdp"), None),
    )
    return jax.shard_map(
        on_device,
        mesh=mesh,
        in_specs=placed,
        out_specs=(
            P("fsdp", "ctx", None),
            P("fsdp", "ctx", None),
            P(("ctx", "fsdp")),
            P(("ctx", "fsdp"), None),
            P(("ctx", "fsdp"), None),
            P(("ctx", "fsdp"), None),
            P(("ctx", "fsdp"), None),
            P(("ctx", "fsdp"), None),
            P(("ctx", "fsdp"), None),
            P(("ctx", "fsdp"), None),
            P(None, ("ctx", "fsdp")),
            P(("ctx", "fsdp")),
            P(),
            P(),
            P(),
            P(("ctx", "fsdp")),
            P(("ctx", "fsdp"), None),
            P(("ctx", "fsdp")),
            P(("ctx", "fsdp"), None),
            P(("ctx", "fsdp"), None),
            P(("ctx", "fsdp"), None),
        ),
        check_vma=False,
    )
```

profile of v0, /device:TPU:0, one launch (start us, length us, event | category | flops | bytes accessed | tf_op | source)
XLA Modules:
  0.0 5363.3 jit_solution(4275195375064017872)
XLA Ops:
  18.4 43.1 all-reduce.23
  61.4 73.7 %all-gather.4 = bf16[32,64,48]{1,2,0:T(8,128)(2,1)S(1)} all-gather(bf16[1,64,48]{1,2,0:T(8,128)(2,1)} %bitcast.437), channel_id=1, replica_groups=mesh['ctx'=8,'fsdp'=4] {'ctx','fsdp'}, dimensions={0}, use_global_device_ids=true | all-gather | bytes 202752 | tf_op jit(solution)/shard_map/all_gather | solution.py:240
  136.7 63.5 %all-gather.3 = bf16[32,112,4]{1,2,0:T(4,128)(2,1)S(1)} all-gather(bf16[1,112,4]{1,2,0:T(4,128)(2,1)S(1)} %bitcast.441), channel_id=1, replica_groups=mesh['ctx'=8,'fsdp'=4] {'ctx','fsdp'}, dimensions={0}, use_global_device_ids=true | all-gather | bytes 29568 | tf_op jit(solution)/shard_map/all_gather | solution.py:241
  202.8 7.4 convolution_convert_fusion
  226.7 12.7 all-gather.2
  242.6 7.5 all-gather.5
  253.2 10.3 all_gather.81
  265.1 10.1 all_gather.78
  275.1 24.2 all-gather.21.cloned.1.call-done
  299.3 6.5 copy.260
  312.6 13.7 while.64
  330.6 41.2 all-gather.39.cloned.1.call-done
  371.8 37.7 while.65
  375.6 4.8 fusion.289
  380.4 4.9 fusion.289
  385.3 4.8 fusion.289
  390.1 4.8 fusion.289
  394.9 4.8 fusion.289
  399.7 4.8 fusion.289
  404.5 4.8 fusion.289
  419.0 51.6 all-gather.29.cloned.1.call-done
  470.6 8.3 multiply_reduce_fusion.12
  478.9 88.9 %all-gather.31.cloned.1.call-done = bf16[3072,2048]{1,0:T(8,128)(2,1)} async-done(((bf16[96,2048]{1,0:T(8,128)(2,1)}), bf16[3072,2048]{1,0:T(8,128)(2,1)}) %all-gather.31.cloned.1.call-update) | async-done | bytes 12582928 | tf_op jit(solution)/shard_map/all_gather | solution.py:244
  567.8 7.4 fusion.164
  575.2 56.0 %all-gather.25.cloned.1.call-done = bf16[1024,2048]{1,0:T(8,128)(2,1)} async-done(((bf16[32,2048]{1,0:T(8,128)(2,1)}), bf16[1024,2048]{1,0:T(8,128)(2,1)}) %all-gather.25.cloned.1.call-update) | async-done | bytes 4194320 | tf_op jit(solution)/shard_map/all_gather | solution.py:237
  634.7 112.9 %all-gather.33.cloned.1.call-done = bf16[2048,4096]{1,0:T(8,128)(2,1)} async-done(((bf16[64,4096]{1,0:T(8,128)(2,1)}), bf16[2048,4096]{1,0:T(8,128)(2,1)}) %all-gather.33.cloned.1.call-update) | async-done | bytes 16777232 | tf_op jit(solution)/shard_map/all_gather | solution.py:370
  747.6 10.0 fusion.187
  757.6 105.9 %all-gather.35.cloned.1.call-done = bf16[2048,4096]{1,0:T(8,128)(2,1)} async-done(((bf16[64,4096]{1,0:T(8,128)(2,1)}), bf16[2048,4096]{1,0:T(8,128)(2,1)}) %all-gather.35.cloned.1.call-update) | async-done | bytes 16777232 | tf_op jit(solution)/shard_map/all_gather | solution.py:371
  863.5 9.4 fusion.188
  873.0 106.7 %all-gather.37.cloned.1.call-done = bf16[4096,2048]{1,0:T(8,128)(2,1)} async-done(((bf16[128,2048]{1,0:T(8,128)(2,1)}), bf16[4096,2048]{1,0:T(8,128)(2,1)}) %all-gather.37.cloned.1.call-update) | async-done | bytes 16777232 | tf_op jit(solution)/shard_map/all_gather | solution.py:372
  979.6 14.6 multiply_convert_fusion
  994.3 12.8 fusion.189
  1007.0 13.9 multiply_reduce_fusion.13
  1022.6 9.8 multiply_reduce_fusion.7
  1047.4 24.7 while.66
  1078.2 4.3 fusion.89
  1082.5 5.9 fusion.50
  1089.6 22.1 all-gather.41.cloned.1.call-done
  1112.0 19.3 while.63
  1138.0 4.9 fusion.54
  1147.2 7.6 multiply_reduce_fusion.6
  1169.7 4.5 fusion.192
  1175.6 4.7 fusion.117
  1181.8 10.2 fusion.163
  1193.2 10.4 fusion.172
  1205.0 13.2 fusion.193
  1219.4 13.1 fusion.194
  1233.9 13.3 fusion.107
  1254.1 11.8 fusion.119
  1266.8 9.2 fusion.191
  1276.1 9.1 fusion.46
  1289.1 10.0 convolution_add_fusion.5
  1300.7 40.9 all-reduce.22
  1348.0 86.2 %reduce-scatter.42.cloned.1.call-done = f32[64,48]{1,0:T(8,128)} async-done(((f32[2048,48]{1,0:T(8,128)}), f32[64,48]{1,0:T(8,128)}) %reduce-scatter.42.cloned.1.call-update) | async-done | bytes 12304
  1435.7 135.8 %reduce-scatter.22.cloned.1.call-done = f32[64,256]{1,0:T(8,128)} async-done(((f32[2048,256]{1,0:T(8,128)}), f32[64,256]{1,0:T(8,128)}) %reduce-scatter.22.cloned.1.call-update) | async-done | bytes 65552 | tf_op jit(solution)/shard_map/reduce_scatter | solution.py:561
  1571.5 138.8 %reduce-scatter.24.cloned.1.call-done = f32[64,256]{1,0:T(8,128)} async-done(((f32[2048,256]{1,0:T(8,128)}), f32[64,256]{1,0:T(8,128)}) %reduce-scatter.24.cloned.1.call-update) | async-done | bytes 65552 | tf_op jit(solution)/shard_map/reduce_scatter | solution.py:562
  1710.3 186.4 %reduce-scatter.26.cloned.1.call-done = f32[32,2048]{1,0:T(8,128)} async-done(((f32[1024,2048]{1,0:T(8,128)}), f32[32,2048]{1,0:T(8,128)}) %reduce-scatter.26.cloned.1.call-update) | async-done | bytes 262160 | tf_op jit(solution)/shard_map/reduce_scatter | solution.py:563
  1896.7 186.4 %reduce-scatter.20.cloned.1.call-done = f32[64,1024]{1,0:T(8,128)} async-done(((f32[2048,1024]{1,0:T(8,128)}), f32[64,1024]{1,0:T(8,128)}) %reduce-scatter.20.cloned.1.call-update) | async-done | bytes 262160 | tf_op jit(solution)/shard_map/reduce_scatter | solution.py:560
  2083.0 250.0 %reduce-scatter.32.cloned.1.call-done = f32[96,2048]{1,0:T(8,128)} async-done(((f32[3072,2048]{1,0:T(8,128)}), f32[96,2048]{1,0:T(8,128)}) %reduce-scatter.32.cloned.1.call-update) | async-done | bytes 786448 | tf_op jit(solution)/shard_map/reduce_scatter | solution.py:570
  2333.0 253.2 %reduce-scatter.28.cloned.1.call-done = f32[64,3072]{1,0:T(8,128)} async-done(((f32[2048,3072]{1,0:T(8,128)}), f32[64,3072]{1,0:T(8,128)}) %reduce-scatter.28.cloned.1.call-update) | async-done | bytes 786448 | tf_op jit(solution)/shard_map/reduce_scatter | solution.py:564
  2586.3 714.4 %reduce-scatter.34.cloned.1.call-done = f32[64,4096]{1,0:T(8,128)} async-done(((f32[2048,4096]{1,0:T(8,128)}), f32[64,4096]{1,0:T(8,128)}) %reduce-scatter.34.cloned.1.call-update) | async-done | bytes 1048592 | tf_op jit(solution)/shard_map/reduce_scatter | solution.py:403
  3300.6 714.2 %reduce-scatter.36.cloned.1.call-done = f32[64,4096]{1,0:T(8,128)} async-done(((f32[2048,4096]{1,0:T(8,128)}), f32[64,4096]{1,0:T(8,128)}) %reduce-scatter.36.cloned.1.call-update) | async-done | bytes 1048592 | tf_op jit(solution)/shard_map/reduce_scatter | solution.py:404
  4014.8 714.0 %reduce-scatter.38.cloned.1.call-done = f32[128,2048]{1,0:T(8,128)} async-done(((f32[4096,2048]{1,0:T(8,128)}), f32[128,2048]{1,0:T(8,128)}) %reduce-scatter.38.cloned.1.call-update) | async-done | bytes 1048592 | tf_op jit(solution)/shard_map/reduce_scatter | solution.py:405
  4728.9 627.4 %reduce-scatter.30.cloned.1.call-done = f32[64,3584]{1,0:T(8,128)} async-done(((f32[2048,3584]{1,0:T(8,128)}), f32[64,3584]{1,0:T(8,128)}) %reduce-scatter.30.cloned.1.call-update) | async-done | bytes 917520 | tf_op jit(solution)/shard_map/reduce_scatter | solution.py:565
  (555 shorter events, 200.1 us)
Async XLA Ops:
  7.2 128.5 %copy-start.2 = (bf16[1,128,2048]{2,1,0:T(8,128)(2,1)S(1)}, bf16[1,128,2048]{2,1,0:T(8,128)(2,1)}, u32[]{:S(2)}) copy-start(bf16[1,128,2048]{2,1,0:T(8,128)(2,1)} %param.32) | copy-start | bytes 1572868
  7.2 128.7 %copy-start.126 = (f32[48]{0:T(128)S(1)}, f32[48]{0:T(128)}, u32[]{:S(2)}) copy-start(f32[48]{0:T(128)} %param.46) | copy-start | bytes 580
  7.2 128.7 %copy-start.128 = (f32[48]{0:T(128)S(1)}, f32[48]{0:T(128)}, u32[]{:S(2)}) copy-start(f32[48]{0:T(128)} %param.45) | copy-start | bytes 580
  7.2 195.6 %all-gather.27.cloned.1.call-start = ((), (), s32[]{:S(2)}) async-start(), calls=%async_computation.17 | async-start | bytes 15138816 | tf_op jit(solution)/shard_map/all_gather | solution.py:239
  8.0 128.8 %copy-start.121 = (bf16[4,112]{1,0:T(4,128)(2,1)S(1)}, bf16[4,112]{1,0:T(4,128)(2,1)}, u32[]{:S(2)}) copy-start(bf16[4,112]{1,0:T(4,128)(2,1)} %param.43) | copy-start | bytes 2692
  8.0 242.1 %all-gather.19.cloned.1.call-start = ((), (), s32[]{:S(2)}) async-start(), calls=%async_computation.13 | async-start | bytes 1081344 | tf_op jit(solution)/shard_map/all_gather | solution.py:235
  8.7 242.9 %all-gather.23.cloned.1.call-start = ((), (), s32[]{:S(2)}) async-start(), calls=%async_computation.15 | async-start | bytes 1081344 | tf_op jit(solution)/shard_map/all_gather | solution.py:236
  9.5 289.9 %all-gather.21.cloned.1.call-start = ((), (), s32[]{:S(2)}) async-start(), calls=%async_computation.14 | async-start | bytes 4325376 | tf_op jit(solution)/shard_map/all_gather | solution.py:234
  10.0 361.7 %all-gather.39.cloned.1.call-start = ((), (), s32[]{:S(2)}) async-start(), calls=%async_computation.33 | async-start | bytes 14155776 | tf_op jit(solution)/shard_map/all_gather | solution.py:33
  11.4 189.3 %collective-permute-start = (bf16[3]{0:T(256)(128)(2,1)S(1)}, bf16[3]{0:T(256)(128)(2,1)S(1)}, u32[]{:S(2)}, u32[]{:S(2)}) collective-permute-start(bf16[3]{0:T(256)(128)(2,1)S(1)} %slice.113), channel_id=1, source_target_pairs={{0,4},{4,8},{8,12},{12,16},{16,20},{20,24},{24,28},{1,5},{5,9},{9,... | collective-permute-start | bytes 26 | tf_op jit(solution)/shard_map/ppermute | solution.py:27
  61.4 139.9 %copy-start.97 = (s32[1,128]{1,0:T(1,128)S(1)}, s32[1,128]{1,0:T(1,128)}, u32[]{:S(2)}) copy-start(s32[1,128]{1,0:T(1,128)} %param.34) | copy-start | bytes 1540
  135.7 74.5 %copy-start.54 = (bf16[2048,48]{0,1:T(8,128)(2,1)}, bf16[2048,48]{0,1:T(8,128)(2,1)S(1)}, u32[]{:S(2)}) copy-start(bf16[2048,48]{0,1:T(8,128)(2,1)S(1)} %reshape.708) | copy-start | bytes 589828
  136.3 103.9 %copy-start.58 = (f32[128,48]{0,1:T(8,128)}, f32[128,48]{0,1:T(8,128)S(1)}, u32[]{:S(2)}) copy-start(f32[128,48]{0,1:T(8,128)S(1)} %get-tuple-element.964) | copy-start | bytes 73732
  136.7 105.7 %copy-start.45 = (f32[128,48]{0,1:T(8,128)}, f32[128,48]{0,1:T(8,128)S(1)}, u32[]{:S(2)}) copy-start(f32[128,48]{0,1:T(8,128)S(1)} %copy.271) | copy-start | bytes 73732
  200.5 11.0 copy-start.100
  200.7 12.0 copy-start.66
  200.7 12.0 copy-start.68
  200.7 12.0 copy-start.70
  200.7 12.0 copy-start.72
  202.8 9.9 copy-start.107
  210.2 2.1 collective-permute-start.1
  221.8 248.7 %all-gather.29.cloned.1.call-start = ((), (), s32[]{:S(2)}) async-start(), calls=%async_computation.18 | async-start | bytes 12976128 | tf_op jit(solution)/shard_map/all_gather | solution.py:238
  222.4 345.4 %all-gather.31.cloned.1.call-start = ((), (), s32[]{:S(2)}) async-start(), calls=%async_computation.19 | async-start | bytes 12976128 | tf_op jit(solution)/shard_map/all_gather | solution.py:244
  223.2 408.0 %all-gather.25.cloned.1.call-start = ((), (), s32[]{:S(2)}) async-start(), calls=%async_computation.16 | async-start | bytes 4325376 | tf_op jit(solution)/shard_map/all_gather | solution.py:237
  223.9 523.7 %all-gather.33.cloned.1.call-start = ((), (), s32[]{:S(2)}) async-start(), calls=%async_computation.20 | async-start | bytes 17301504 | tf_op jit(solution)/shard_map/all_gather | solution.py:370
  224.6 638.9 %all-gather.35.cloned.1.call-start = ((), (), s32[]{:S(2)}) async-start(), calls=%async_computation.21 | async-start | bytes 17301504 | tf_op jit(solution)/shard_map/all_gather | solution.py:371
  225.2 754.4 %all-gather.37.cloned.1.call-start = ((), (), s32[]{:S(2)}) async-start(), calls=%async_computation.22 | async-start | bytes 17301504 | tf_op jit(solution)/shard_map/all_gather | solution.py:372
  226.0 885.7 %all-gather.41.cloned.1.call-start = ((), (), s32[]{:S(2)}) async-start(), calls=%async_computation.34 | async-start | bytes 14155776 | tf_op jit(solution)/shard_map/all_gather | solution.py:58
  226.7 794.2 %copy-start.64 = (f32[2048]{0:T(1024)}, f32[2048]{0:T(1024)S(1)}, u32[]{:S(2)}) copy-start(f32[2048]{0:T(1024)S(1)} %convert_element_type.311) | copy-start | bytes 24580
  241.0 69.0 %copy-start.48 = (f32[128,64]{0,1:T(8,128)}, f32[128,64]{0,1:T(8,128)S(1)}, u32[]{:S(2)}) copy-start(f32[128,64]{0,1:T(8,128)S(1)} %get-tuple-element.956) | copy-start | bytes 98308
  241.1 69.0 %copy-start.50 = (f32[128,64]{0,1:T(8,128)}, f32[128,64]{0,1:T(8,128)S(1)}, u32[]{:S(2)}) copy-start(f32[128,64]{0,1:T(8,128)S(1)} %get-tuple-element.957) | copy-start | bytes 98308
  327.8 303.4 %copy-start.39 = (bf16[128,2,4,128]{0,3,2,1:T(8,128)(2,1)}, bf16[128,2,4,128]{0,3,2,1:T(8,128)(2,1)S(1)}, u32[]{:S(2)}) copy-start(bf16[128,2,4,128]{0,3,2,1:T(8,128)(2,1)S(1)} %copy.264) | copy-start | bytes 786436
  329.4 84.3 %copy-start.52 = (bf16[128,3072]{0,1:T(8,128)(2,1)}, bf16[128,3072]{0,1:T(8,128)(2,1)S(1)}, u32[]{:S(2)}) copy-start(bf16[128,3072]{0,1:T(8,128)(2,1)S(1)} %copy.266) | copy-start | bytes 2359300
  330.6 83.1 %copy-start.78 = (f32[128,128]{1,0:T(8,128)}, f32[128,128]{1,0:T(8,128)S(1)}, u32[]{:S(2)}) copy-start(f32[128,128]{1,0:T(8,128)S(1)} %fusion.138) | copy-start | bytes 196612
  478.9 553.6 %copy-start.6 = (f32[128,3072]{1,0:T(8,128)}, f32[128,3072]{1,0:T(8,128)S(1)}, u32[]{:S(2)}) copy-start(f32[128,3072]{1,0:T(8,128)S(1)} %get-tuple-element.917) | copy-start | bytes 4718596
  478.9 553.6 %copy-start.92 = (f32[128]{0:T(128)}, f32[128]{0:T(128)S(1)}, u32[]{:S(2)}) copy-start(f32[128]{0:T(128)S(1)} %fusion.158) | copy-start | bytes 1540
  634.5 386.4 %copy-start.4 = (f32[128,2048]{1,0:T(8,128)}, f32[128,2048]{1,0:T(8,128)S(1)}, u32[]{:S(2)}) copy-start(f32[128,2048]{1,0:T(8,128)S(1)} %get-tuple-element.967) | copy-start | bytes 3145732
  634.5 386.4 %copy-start.98 = (f32[128]{0:T(128)}, f32[128]{0:T(128)S(1)}, u32[]{:S(2)}) copy-start(f32[128]{0:T(128)S(1)} %fusion.159) | copy-start | bytes 1540
  634.7 228.9 %copy-start.16 = (bf16[128,2048]{1,0:T(8,128)(2,1)}, bf16[128,2048]{1,0:T(8,128)(2,1)S(1)}, u32[]{:S(2)}) copy-start(bf16[128,2048]{1,0:T(8,128)(2,1)S(1)} %multiply_convert_fusion.5) | copy-start | bytes 1572868
  1007.0 13.9 copy-start.33
  1020.9 11.5 copy-start.115
  1041.2 123.5 %reduce-scatter.40.cloned.1.call-start = ((), (), s32[]{:S(2)}) async-start(), calls=%async_computation.35 | async-start | bytes 1179648
  1089.5 257.1 %reduce-scatter.44.cloned.1.call-start = ((), (), s32[]{:S(2)}) async-start(), calls=%async_computation.37 | async-start | bytes 1892352
  1162.4 271.9 %reduce-scatter.42.cloned.1.call-start = ((), (), s32[]{:S(2)}) async-start(), calls=%async_computation.36 | async-start | bytes 1081344
  1164.6 406.9 %reduce-scatter.22.cloned.1.call-start = ((), (), s32[]{:S(2)}) async-start(), calls=%async_computation.24 | async-start | bytes 2162688 | tf_op jit(solution)/shard_map/reduce_scatter | solution.py:561
  1167.7 542.6 %reduce-scatter.24.cloned.1.call-start = ((), (), s32[]{:S(2)}) async-start(), calls=%async_computation.25 | async-start | bytes 2162688 | tf_op jit(solution)/shard_map/reduce_scatter | solution.py:562
  1169.7 727.0 %reduce-scatter.26.cloned.1.call-start = ((), (), s32[]{:S(2)}) async-start(), calls=%async_computation.26 | async-start | bytes 8650752 | tf_op jit(solution)/shard_map/reduce_scatter | solution.py:563
  1174.2 908.8 %reduce-scatter.20.cloned.1.call-start = ((), (), s32[]{:S(2)}) async-start(), calls=%async_computation.23 | async-start | bytes 8650752 | tf_op jit(solution)/shard_map/reduce_scatter | solution.py:560
  1180.4 1152.6 %reduce-scatter.32.cloned.1.call-start = ((), (), s32[]{:S(2)}) async-start(), calls=%async_computation.29 | async-start | bytes 25952256 | tf_op jit(solution)/shard_map/reduce_scatter | solution.py:570
  1192.0 1394.2 %reduce-scatter.28.cloned.1.call-start = ((), (), s32[]{:S(2)}) async-start(), calls=%async_computation.27 | async-start | bytes 25952256 | tf_op jit(solution)/shard_map/reduce_scatter | solution.py:564
  1203.6 2097.0 %reduce-scatter.34.cloned.1.call-start = ((), (), s32[]{:S(2)}) async-start(), calls=%async_computation.30 | async-start | bytes 34603008 | tf_op jit(solution)/shard_map/reduce_scatter | solution.py:403
  1218.2 2796.6 %reduce-scatter.36.cloned.1.call-start = ((), (), s32[]{:S(2)}) async-start(), calls=%async_computation.31 | async-start | bytes 34603008 | tf_op jit(solution)/shard_map/reduce_scatter | solution.py:404
  1232.6 3496.3 %reduce-scatter.38.cloned.1.call-start = ((), (), s32[]{:S(2)}) async-start(), calls=%async_computation.32 | async-start | bytes 34603008 | tf_op jit(solution)/shard_map/reduce_scatter | solution.py:405
  1247.3 4109.0 %reduce-scatter.30.cloned.1.call-start = ((), (), s32[]{:S(2)}) async-start(), calls=%async_computation.28 | async-start | bytes 30277632 | tf_op jit(solution)/shard_map/reduce_scatter | solution.py:565
  1250.5 3.1 collective-permute-start.2
  1276.1 10.1 copy-start.42
  1289.0 10.1 copy-start.55
  1289.0 10.1 copy-start.75
  1299.2 44.7 copy-start.123
  1299.2 44.7 copy-start.27
  1299.2 44.7 copy-start.35
  1299.2 44.7 copy-start.65
  1299.2 44.7 copy-start.99
  1299.2 44.7 copy-start.116
  (99 other events, 343.3 us)
Sparse Core Ops, SparseCore 0:
  10.9 112.1 all-gather.26
  126.1 52.6 all-gather.18
  181.8 52.6 all-gather.22
  237.4 61.8 all-gather.20
  301.0 70.6 all-gather.38
  374.5 96.0 all-gather.28
  473.5 94.2 all-gather.30
  570.8 60.3 all-gather.24
  634.1 113.4 all-gather.32
  750.4 113.0 all-gather.34
  866.5 113.0 all-gather.36
  1041.3 70.2 all-gather.40
  1114.8 36.0 reduce-scatter.39
  1162.5 136.8 reduce-scatter.43
  1301.7 132.5 reduce-scatter.41
  1436.9 134.5 reduce-scatter.21
  1574.3 135.9 reduce-scatter.23
  1713.0 183.6 reduce-scatter.25
  1899.5 183.4 reduce-scatter.19
  2089.9 243.1 reduce-scatter.31
  2341.2 245.0 reduce-scatter.27
  2589.1 711.4 reduce-scatter.33
  3303.5 711.2 reduce-scatter.35
  4017.6 711.2 reduce-scatter.37
  4731.8 624.5 reduce-scatter.29
where the time goes:
time: 5370 us; the launch traced here: 5360 us
  waiting for transfers between devices  4630 us (86%)
  matrix products  283 us (5%)
  blocking collectives  262 us (5%)
  other arithmetic  104 us (2%)
  local copies, waits for them, and re-layouts  63.9 us (1%)
    reduce_scatter x1, waiting for transfers between devices, on_device(): lax.psum_scatter(gate_grad_w, ('ctx', 'fsdp'), scatter_dimension=0, tiled...  714 us
    reduce_scatter x1, waiting for transfers between devices, on_device(): lax.psum_scatter(up_grad_w, ('ctx', 'fsdp'), scatter_dimension=0, tiled=T...  714 us
    reduce_scatter x1, waiting for transfers between devices, on_device(): lax.psum_scatter(down_grad_w, ('ctx', 'fsdp'), scatter_dimension=0, tiled...  714 us
    reduce_scatter x1, waiting for transfers between devices, on_device(): lax.psum_scatter(conv_in_grad_w, ('ctx', 'fsdp'), scatter_dimension=0, ti...  627 us
    reduce_scatter x1, waiting for transfers between devices, on_device(): lax.psum_scatter(zgate_grad_w, ('ctx', 'fsdp'), scatter_dimension=0, tile...  253 us
    reduce_scatter x1, waiting for transfers between devices, on_device(): lax.psum_scatter(mamba_grad_w, ('ctx', 'fsdp'), scatter_dimension=0, tile...  250 us
    reduce_scatter x1, waiting for transfers between devices, on_device(): lax.psum_scatter(query_grad_w, ('ctx', 'fsdp'), scatter_dimension=0, tile...  186 us
    reduce_scatter x1, waiting for transfers between devices, on_device(): lax.psum_scatter(attn_out_grad_w, ('ctx', 'fsdp'), scatter_dimension=0, t...  186 us
  transfers between devices with their start and end apart: 28, of which 22 were waited for; matrix products, arithmetic and copies ran while one was open for 7% of the time, Pallas kernels for 0%

commit v1 on v0

--- a/solution.py
+++ b/solution.py
@@ -6,6 +6,8 @@
 from jax import lax
 from jax.sharding import PartitionSpec as P
 
+CTX = "ctx"
+FSDP = "fsdp"
 QUERY_HEADS = 8
 KEY_VALUE_HEADS = 2
 HEAD_SIZE = 128
@@ -230,18 +232,18 @@
         mixer_gain_full,
         mamba_out_full,
     ) = (
-        lax.all_gather(norm_gain, ("ctx", "fsdp"), axis=0, tiled=True),
-        lax.all_gather(query_weight, ("ctx", "fsdp"), axis=0, tiled=True),
-        lax.all_gather(key_matrix, ("ctx", "fsdp"), axis=0, tiled=True),
-        lax.all_gather(value_matrix, ("ctx", "fsdp"), axis=0, tiled=True),
-        lax.all_gather(attn_out_weight, ("ctx", "fsdp"), axis=0, tiled=True),
-        lax.all_gather(mixer_gate_weight, ("ctx", "fsdp"), axis=0, tiled=True),
-        lax.all_gather(conv_in_weight, ("ctx", "fsdp"), axis=0, tiled=True),
-        lax.all_gather(step_weight, ("ctx", "fsdp"), axis=0, tiled=True),
-        lax.all_gather(conv_weight, ("ctx", "fsdp"), axis=1, tiled=True),
-        lax.all_gather(conv_bias, ("ctx", "fsdp"), axis=0, tiled=True),
-        lax.all_gather(mixer_gain, ("ctx", "fsdp"), axis=0, tiled=True),
-        lax.all_gather(mamba_out_weight, ("ctx", "fsdp"), axis=0, tiled=True),
+        lax.all_gather(norm_gain, (CTX, FSDP), axis=0, tiled=True),
+        lax.all_gather(query_weight, (CTX, FSDP), axis=0, tiled=True),
+        lax.all_gather(key_matrix, (CTX, FSDP), axis=0, tiled=True),
+        lax.all_gather(value_matrix, (CTX, FSDP), axis=0, tiled=True),
+        lax.all_gather(attn_out_weight, (CTX, FSDP), axis=0, tiled=True),
+        lax.all_gather(mixer_gate_weight, (CTX, FSDP), axis=0, tiled=True),
+        lax.all_gather(conv_in_weight, (CTX, FSDP), axis=0, tiled=True),
+        lax.all_gather(step_weight, (CTX, FSDP), axis=0, tiled=True),
+        lax.all_gather(conv_weight, (CTX, FSDP), axis=1, tiled=True),
+        lax.all_gather(conv_bias, (CTX, FSDP), axis=0, tiled=True),
+        lax.all_gather(mixer_gain, (CTX, FSDP), axis=0, tiled=True),
+        lax.all_gather(mamba_out_weight, (CTX, FSDP), axis=0, tiled=True),
     )
     tokens_per_worker = hidden_in.shape[1]
     head_cluster = QUERY_HEADS // KEY_VALUE_HEADS
@@ -249,7 +251,7 @@
     taps = CONV - 1
     resid = hidden_in[0].astype(single_float)
     documents = doc_ids[0]
-    places = (lax.axis_index("ctx") * tokens_per_worker + jnp.arange(tokens_per_worker)).astype(
+    places = (lax.axis_index(CTX) * tokens_per_worker + jnp.arange(tokens_per_worker)).astype(
         single_float
     )
     norm_one, norm_one_back = jax.vjp(rms_scale, resid, norm_full.astype(single_float))
@@ -302,9 +304,9 @@
         jnp.zeros((KEY_VALUE_HEADS, rows_of_query, HEAD_SIZE), single_float),
     )
     kv_whole = (
-        lax.all_gather(flattened_key, "ctx", axis=0, tiled=True),
-        lax.all_gather(value_lowered, "ctx", axis=0, tiled=True),
-        lax.all_gather(docs_low, "ctx", axis=0, tiled=True),
+        lax.all_gather(flattened_key, CTX, axis=0, tiled=True),
+        lax.all_gather(value_lowered, CTX, axis=0, tiled=True),
+        lax.all_gather(docs_low, CTX, axis=0, tiled=True),
     )
     peak, total, summed = fold_local(attend_piece, kv_whole, start_forward)
     attention_cluster = summed / total[:, :, None]
@@ -322,7 +324,7 @@
     )
     step_lin = jnp.dot(normalized_input, step_full, preferred_element_type=single_float)
     rim_rows, rim_docs = shifted(
-        (conv_lin[tokens_per_worker - taps :], docs_low[tokens_per_worker - taps :]), "ctx", 1
+        (conv_lin[tokens_per_worker - taps :], docs_low[tokens_per_worker - taps :]), CTX, 1
     )
     widened = jnp.concatenate([rim_rows, conv_lin], axis=0).astype(single_float)
     widened_docs = jnp.concatenate([rim_docs.astype(jnp.int32), documents])
@@ -346,7 +348,7 @@
         decay_rate,
     )
     chain_identity = (jnp.ones_like(carry_decay), jnp.zeros_like(state_loc))
-    _, state_in = prefix((carry_decay, state_loc), "ctx", chain_combine, chain_identity)
+    _, state_in = prefix((carry_decay, state_loc), CTX, chain_combine, chain_identity)
     mixed, mix_back = jax.vjp(
         partial(block_mix, documents=documents, prior_doc=prior_doc),
         mixer_in,
@@ -366,10 +368,10 @@
     ymix_low = ymix_vals.astype(brain_float_half)
     mamba_out = jnp.dot(ymix_low, mamba_out_full, preferred_element_type=single_float)
     ffn_gain_full, gate_full, up_full, down_full = (
-        lax.all_gather(ffn_gain, ("ctx", "fsdp"), axis=0, tiled=True),
-        lax.all_gather(gate_weight, ("ctx", "fsdp"), axis=0, tiled=True),
-        lax.all_gather(up_weight, ("ctx", "fsdp"), axis=0, tiled=True),
-        lax.all_gather(down_weight, ("ctx", "fsdp"), axis=0, tiled=True),
+        lax.all_gather(ffn_gain, (CTX, FSDP), axis=0, tiled=True),
+        lax.all_gather(gate_weight, (CTX, FSDP), axis=0, tiled=True),
+        lax.all_gather(up_weight, (CTX, FSDP), axis=0, tiled=True),
+        lax.all_gather(down_weight, (CTX, FSDP), axis=0, tiled=True),
     )
     mid = resid + attn_out + mamba_out
     norm_two, norm_two_back = jax.vjp(rms_scale, mid, ffn_gain_full.astype(single_float))
@@ -399,10 +401,10 @@
     grad_mid_norm, ffn_gain_grad = norm_two_back(grad_normed_two)
     grad_mid = grad_out.astype(single_float) + grad_mid_norm
     ffn_sums = (
-        lax.psum_scatter(ffn_gain_grad, ("ctx", "fsdp"), scatter_dimension=0, tiled=True),
-        lax.psum_scatter(gate_grad_w, ("ctx", "fsdp"), scatter_dimension=0, tiled=True),
-        lax.psum_scatter(up_grad_w, ("ctx", "fsdp"), scatter_dimension=0, tiled=True),
-        lax.psum_scatter(down_grad_w, ("ctx", "fsdp"), scatter_dimension=0, tiled=True),
+        lax.psum_scatter(ffn_gain_grad, (CTX, FSDP), scatter_dimension=0, tiled=True),
+        lax.psum_scatter(gate_grad_w, (CTX, FSDP), scatter_dimension=0, tiled=True),
+        lax.psum_scatter(up_grad_w, (CTX, FSDP), scatter_dimension=0, tiled=True),
+        lax.psum_scatter(down_grad_w, (CTX, FSDP), scatter_dimension=0, tiled=True),
     )
     branch_grad = grad_mid.astype(brain_float_half)
     attn_out_grad_w = jnp.einsum(
@@ -455,13 +457,13 @@
     start_back = (
         jnp.zeros((KEY_VALUE_HEADS, rows_of_query, HEAD_SIZE), single_float),
         jnp.zeros(
-            (tokens_per_worker * lax.axis_size("ctx"), 2 * KEY_VALUE_HEADS * HEAD_SIZE),
+            (tokens_per_worker * lax.axis_size(CTX), 2 * KEY_VALUE_HEADS * HEAD_SIZE),
             single_float,
         ),
     )
     query_acc, kv_grad = fold_local(attend_back, kv_whole, start_back)
     local_key_value = lax.psum_scatter(
-        kv_grad.astype(jnp.bfloat16), "ctx", scatter_dimension=0, tiled=True
+        kv_grad.astype(jnp.bfloat16), CTX, scatter_dimension=0, tiled=True
     ).astype(jnp.float32)
     query_turn_grad = (
         (query_acc * HEAD_SIZE ** (-0.5))
@@ -503,7 +505,7 @@
         skip_grad,
         grad_state_in,
     ) = mix_back(grad_mixed.reshape(tokens_per_worker, HS, HP))
-    _, state_later = carried_in((carry_decay, grad_state_in), "ctx", chain_combine, chain_identity)
+    _, state_later = carried_in((carry_decay, grad_state_in), CTX, chain_combine, chain_identity)
     decay_grad = jnp.sum(state_in * state_later, axis=(1, 2))
     grad_in_stats, grad_write_stats, grad_step_stats, grad_rate_stats = stats_back(
         (state_later, decay_grad)
@@ -517,7 +519,7 @@
         axis=1,
     )
     grad_widened, conv_weight_grad, conv_bias_grad = conv_back(grad_conv)
-    rim_grad = shifted(grad_widened[:taps].astype(jnp.bfloat16), "ctx", -1).astype(jnp.float32)
+    rim_grad = shifted(grad_widened[:taps].astype(jnp.bfloat16), CTX, -1).astype(jnp.float32)
     conv_lin_grad = (
         grad_widened[taps:].at[tokens_per_worker - taps :].add(rim_grad).astype(brain_float_half)
     )
@@ -556,22 +558,22 @@
     grad_resid_norm, norm_gain_grad = norm_one_back(grad_normed)
     input_grad = (grad_mid + grad_resid_norm).astype(brain_float_half)
     mixer_sums = (
-        lax.psum_scatter(norm_gain_grad, ("ctx", "fsdp"), scatter_dimension=0, tiled=True),
-        lax.psum_scatter(query_grad_w, ("ctx", "fsdp"), scatter_dimension=0, tiled=True),
-        lax.psum_scatter(key_grad_w, ("ctx", "fsdp"), scatter_dimension=0, tiled=True),
-        lax.psum_scatter(value_grad_w, ("ctx", "fsdp"), scatter_dimension=0, tiled=True),
-        lax.psum_scatter(attn_out_grad_w, ("ctx", "fsdp"), scatter_dimension=0, tiled=True),
-        lax.psum_scatter(zgate_grad_w, ("ctx", "fsdp"), scatter_dimension=0, tiled=True),
-        lax.psum_scatter(conv_in_grad_w, ("ctx", "fsdp"), scatter_dimension=0, tiled=True),
-        lax.psum_scatter(step_grad_w, ("ctx", "fsdp"), scatter_dimension=0, tiled=True),
-        lax.psum_scatter(conv_weight_grad, ("ctx", "fsdp"), scatter_dimension=1, tiled=True),
-        lax.psum_scatter(conv_bias_grad, ("ctx", "fsdp"), scatter_dimension=0, tiled=True),
-        lax.psum_scatter(mixer_gain_grad, ("ctx", "fsdp"), scatter_dimension=0, tiled=True),
-        lax.psum_scatter(mamba_grad_w, ("ctx", "fsdp"), scatter_dimension=0, tiled=True),
+        lax.psum_scatter(norm_gain_grad, (CTX, FSDP), scatter_dimension=0, tiled=True),
+        lax.psum_scatter(query_grad_w, (CTX, FSDP), scatter_dimension=0, tiled=True),
+        lax.psum_scatter(key_grad_w, (CTX, FSDP), scatter_dimension=0, tiled=True),
+        lax.psum_scatter(value_grad_w, (CTX, FSDP), scatter_dimension=0, tiled=True),
+        lax.psum_scatter(attn_out_grad_w, (CTX, FSDP), scatter_dimension=0, tiled=True),
+        lax.psum_scatter(zgate_grad_w, (CTX, FSDP), scatter_dimension=0, tiled=True),
+        lax.psum_scatter(conv_in_grad_w, (CTX, FSDP), scatter_dimension=0, tiled=True),
+        lax.psum_scatter(step_grad_w, (CTX, FSDP), scatter_dimension=0, tiled=True),
+        lax.psum_scatter(conv_weight_grad, (CTX, FSDP), scatter_dimension=1, tiled=True),
+        lax.psum_scatter(conv_bias_grad, (CTX, FSDP), scatter_dimension=0, tiled=True),
+        lax.psum_scatter(mixer_gain_grad, (CTX, FSDP), scatter_dimension=0, tiled=True),
+        lax.psum_scatter(mamba_grad_w, (CTX, FSDP), scatter_dimension=0, tiled=True),
     )
     summed_grads = tuple(mixer_sums) + tuple(ffn_sums)
     step_bias_sum, log_decay_sum, skip_sum = lax.psum(
-        (step_bias_grad, log_decay_grad, skip_grad), ("ctx", "fsdp")
+        (step_bias_grad, log_decay_grad, skip_grad), (CTX, FSDP)
     )
     return (
         block_out[None],
@@ -598,57 +600,569 @@
     )
 
 
+BF = jnp.bfloat16
+F32 = jnp.float32
+
+
+def dotf(left, right, dims):
+    return lax.dot_general(left, right, (dims, ((), ())), preferred_element_type=F32)
+
+
+def mm(left, right):
+    return dotf(left, right, ((left.ndim - 1,), (0,)))
+
+
+def mm_nt(left, right):
+    return dotf(left, right, ((1,), (1,)))
+
+
+def mm_tn(left, right):
+    return dotf(left, right, ((0,), (0,)))
+
+
+def gather_tokens(block):
+    return lax.all_gather(block, CTX, axis=0, tiled=True)
+
+
+def scatter_tokens(partial_sum):
+    return lax.psum_scatter(
+        partial_sum.astype(BF), CTX, scatter_dimension=0, tiled=True
+    ).astype(F32)
+
+
+def gather_rows(shard):
+    return lax.all_gather(shard, FSDP, axis=0, tiled=False)
+
+
+def scatter_rows(partial_sum):
+    return lax.psum_scatter(partial_sum.astype(BF), FSDP, scatter_dimension=0, tiled=False)
+
+
+def swap_columns(packed):
+    return lax.all_to_all(packed, CTX, split_axis=0, concat_axis=0, tiled=True)
+
+
+def same_document(documents):
+    places = jnp.arange(documents.shape[0])
+    return (documents[:, None] == documents[None, :]) & (places[:, None] >= places[None, :])
+
+
+def ssm_terms(step, rate, documents, chunks):
+    length, heads = step.shape
+    rows = length // chunks
+    step_c = step.reshape(chunks, rows, heads).transpose(0, 2, 1)
+    docs_c = documents.reshape(chunks, rows)
+    prior = jnp.concatenate([jnp.full((1,), -1, docs_c.dtype), docs_c[:-1, -1]])
+    last = docs_c[:, -1]
+    level = jnp.cumsum(step_c * rate[None, :, None], axis=2)
+    visible = jax.vmap(same_document)(docs_c)[:, None]
+    spread = level[:, :, :, None] - level[:, :, None, :]
+    pair = jnp.where(visible, jnp.exp(jnp.where(visible, spread, 0.0)), 0.0)
+    entry = jnp.where((docs_c == prior[:, None])[:, None], jnp.exp(level), 0.0)
+    tail = jnp.where((docs_c == last[:, None])[:, None], jnp.exp(level[:, :, -1:] - level), 0.0)
+    carry = jnp.exp(level[:, :, -1]) * (last == prior).astype(F32)[:, None]
+    return step_c, pair, entry, tail, carry
+
+
+def ssm_forward(xin, write, read, terms, skip):
+    step_c, pair, entry, tail, carry = terms
+    chunks, heads, rows = step_c.shape
+    x_c = xin.reshape(chunks, rows, heads, HP)
+    write_c = write.reshape(chunks, rows, STATE)
+    read_c = read.reshape(chunks, rows, STATE)
+    gram = jnp.einsum("ktn,kun->ktu", read_c, write_c, preferred_element_type=F32)
+    mixing = (pair * gram[:, None] * step_c[:, :, None, :]).astype(BF)
+    inner = jnp.einsum("khtu,kuhp->kthp", mixing, x_c, preferred_element_type=F32)
+    weight = (tail * step_c).transpose(0, 2, 1)
+    weighted = (x_c.astype(F32) * weight[..., None]).astype(BF)
+    local = jnp.einsum("kthp,ktn->khpn", weighted, write_c, preferred_element_type=F32)
+    state = jnp.zeros_like(local[0])
+    entering = []
+    for k in range(chunks):
+        entering.append(state)
+        state = carry[k][:, None, None] * state + local[k]
+    entering = jnp.stack(entering)
+    reached = jnp.einsum(
+        "ktn,khpn->kthp", read_c, entering.astype(BF), preferred_element_type=F32
+    )
+    y = (
+        inner
+        + reached * entry.transpose(0, 2, 1)[..., None]
+        + skip[None, None, :, None] * x_c.astype(F32)
+    )
+    return y.reshape(chunks * rows, heads * HP), (gram, mixing, entering, reached)
+
+
+def ssm_backward(grad, xin, write, read, terms, skip, rate, saved):
+    step_c, pair, entry, tail, carry = terms
+    gram, mixing, entering, reached = saved
+    chunks, heads, rows = step_c.shape
+    x_c = xin.reshape(chunks, rows, heads, HP)
+    x_f = x_c.astype(F32)
+    write_c = write.reshape(chunks, rows, STATE)
+    read_c = read.reshape(chunks, rows, STATE)
+    g = grad.reshape(chunks, rows, heads, HP)
+    g_low = g.astype(BF)
+    skip_grad = jnp.sum(g * x_f, axis=(0, 1, 3))
+    gx = skip[None, None, :, None] * g
+    gx = gx + jnp.einsum("khtu,kthp->kuhp", mixing, g_low, preferred_element_type=F32)
+    g_mixing = jnp.einsum("kthp,kuhp->khtu", g_low, x_c, preferred_element_type=F32)
+    masked = g_mixing * pair
+    g_gram = jnp.sum(masked * step_c[:, :, None, :], axis=1).astype(BF)
+    both = masked * gram[:, None]
+    column = jnp.sum(both, axis=2)
+    row = jnp.sum(both * step_c[:, :, None, :], axis=3)
+    g_level = row - step_c * column
+    g_step = column
+    entry_t = entry.transpose(0, 2, 1)[..., None]
+    g_entry = jnp.sum(g * reached, axis=3).transpose(0, 2, 1)
+    g_level = g_level + g_entry * entry
+    g_reached = (g * entry_t).astype(BF)
+    g_read = jnp.einsum("ktu,kun->ktn", g_gram, write_c, preferred_element_type=F32)
+    g_write = jnp.einsum("ktu,ktn->kun", g_gram, read_c, preferred_element_type=F32)
+    g_read = g_read + jnp.einsum(
+        "kthp,khpn->ktn", g_reached, entering.astype(BF), preferred_element_type=F32
+    )
+    g_enter = jnp.einsum("kthp,ktn->khpn", g_reached, read_c, preferred_element_type=F32)
+    state = jnp.zeros_like(g_enter[0])
+    leaving = [None] * chunks
+    for k in reversed(range(chunks)):
+        leaving[k] = state
+        state = carry[k][:, None, None] * state + g_enter[k]
+    leaving = jnp.stack(leaving)
+    g_carry = jnp.sum(entering * leaving, axis=(2, 3))
+    leaving_low = leaving.astype(BF)
+    weight = tail * step_c
+    weight_t = weight.transpose(0, 2, 1)[..., None]
+    seen = jnp.einsum("ktn,khpn->kthp", write_c, leaving_low, preferred_element_type=F32)
+    gx = gx + weight_t * seen
+    g_weight = jnp.sum(x_f * seen, axis=3).transpose(0, 2, 1)
+    weighted = (x_f * weight_t).astype(BF)
+    g_write = g_write + jnp.einsum(
+        "kthp,khpn->ktn", weighted, leaving_low, preferred_element_type=F32
+    )
+    moved = g_weight * weight
+    g_step = g_step + g_weight * tail
+    g_level = g_level - moved
+    end = jnp.sum(moved, axis=2) + g_carry * carry
+    g_level = g_level.at[:, :, -1].add(end)
+    g_la = jnp.flip(jnp.cumsum(jnp.flip(g_level, 2), axis=2), 2)
+    g_step = g_step + g_la * rate[None, :, None]
+    rate_grad = jnp.sum(g_la * step_c, axis=(0, 2))
+    length = chunks * rows
+    return (
+        gx.reshape(length, heads * HP),
+        g_write.reshape(length, STATE),
+        g_read.reshape(length, STATE),
+        g_step.transpose(0, 2, 1).reshape(length, heads),
+        rate_grad,
+        skip_grad,
+    )
+
+
+def head_parallel(
+    hidden_in,
+    out_grad,
+    doc_ids,
+    norm_gain,
+    query_weight,
+    key_matrix,
+    value_matrix,
+    attn_out_weight,
+    mixer_gate_weight,
+    conv_in_weight,
+    step_weight,
+    conv_weight,
+    conv_bias,
+    step_bias,
+    log_decay,
+    skip_gain,
+    mixer_gain,
+    mamba_out_weight,
+    ffn_gain,
+    gate_weight,
+    up_weight,
+    down_weight,
+):
+    ctx = lax.axis_size(CTX)
+    seqs = lax.axis_size(FSDP)
+    me = lax.axis_index(CTX)
+    mine = lax.axis_index(FSDP)
+    tokens, width = hidden_in.shape[1:]
+    length = ctx * tokens
+    krows = query_weight.shape[0]
+    dssm = HS * HP
+    heads = HS // ctx
+    inner = heads * HP
+    bc = 2 * STATE // ctx
+    ff = gate_weight.shape[1] // ctx
+    head = HEAD_SIZE * QUERY_HEADS // ctx
+    taps = CONV - 1
+    step_pad = 128 - bc % 128
+
+    small = jnp.concatenate(
+        [
+            norm_gain,
+            ffn_gain,
+            mixer_gain,
+            conv_bias,
+            conv_weight.reshape(-1),
+            doc_ids[0].astype(BF),
+        ]
+    )
+    small = lax.all_gather(small, (CTX, FSDP), axis=0, tiled=False)
+    cuts = []
+    at = 0
+    for n in (norm_gain.size, ffn_gain.size, mixer_gain.size, conv_bias.size, conv_weight.size, tokens):
+        cuts.append(small[:, at : at + n])
+        at += n
+    gain_one = cuts[0].reshape(-1).astype(F32)
+    gain_two = cuts[1].reshape(-1).astype(F32)
+    gain_mix = lax.dynamic_slice_in_dim(cuts[2].reshape(-1), me * inner, inner).astype(F32)
+    bias_all = cuts[3].reshape(-1)
+    taps_all = cuts[4].reshape(ctx * seqs, CONV, -1).transpose(1, 0, 2).reshape(CONV, -1)
+    documents = lax.dynamic_index_in_dim(
+        cuts[5].reshape(ctx, seqs, tokens), mine, 1, False
+    ).reshape(length).astype(jnp.int32)
+
+    def own_channels(full):
+        return jnp.concatenate(
+            [
+                lax.dynamic_slice_in_dim(full, me * inner, inner, full.ndim - 1),
+                lax.dynamic_slice_in_dim(full, dssm + me * bc, bc, full.ndim - 1),
+            ],
+            axis=-1,
+        )
+
+    conv_taps = own_channels(taps_all).astype(F32)
+    conv_shift = own_channels(bias_all).astype(F32)
+    bias_own = lax.dynamic_slice_in_dim(step_bias, me * heads, heads)
+    decay_own = lax.dynamic_slice_in_dim(log_decay, me * heads, heads)
+    skip_own = lax.dynamic_slice_in_dim(skip_gain, me * heads, heads)
+
+    def by_column(weight, n):
+        return weight.reshape(krows, ctx, n).transpose(1, 0, 2)
+
+    kv_repeat = ctx // KEY_VALUE_HEADS
+    conv_pack = jnp.concatenate(
+        [
+            by_column(conv_in_weight[:, :dssm], inner),
+            by_column(conv_in_weight[:, dssm:], bc),
+            jnp.pad(by_column(step_weight, heads), ((0, 0), (0, 0), (0, step_pad - heads))),
+        ],
+        axis=2,
+    )
+    rest_pack = jnp.concatenate(
+        [
+            by_column(query_weight, head),
+            jnp.repeat(
+                key_matrix.reshape(krows, KEY_VALUE_HEADS, HEAD_SIZE).transpose(1, 0, 2),
+                kv_repeat,
+                axis=0,
+            ),
+            jnp.repeat(
+                value_matrix.reshape(krows, KEY_VALUE_HEADS, HEAD_SIZE).transpose(1, 0, 2),
+                kv_repeat,
+                axis=0,
+            ),
+            by_column(mixer_gate_weight, inner),
+        ],
+        axis=2,
+    )
+    ffn_pack = jnp.concatenate([by_column(gate_weight, ff), by_column(up_weight, ff)], axis=2)
+    conv_cols = conv_pack.shape[2]
+    rest_cols = rest_pack.shape[2]
+    mixer_pack = swap_columns(jnp.concatenate([conv_pack, rest_pack], axis=2))
+    conv_in_own = gather_rows(mixer_pack[:, :, :conv_cols]).reshape(width, conv_cols)
+    rest_own = gather_rows(mixer_pack[:, :, conv_cols:]).reshape(width, rest_cols)
+    attn_out_own = gather_rows(attn_out_weight).reshape(head, width)
+    mamba_out_own = gather_rows(mamba_out_weight).reshape(inner, width)
+    ffn_own = gather_rows(swap_columns(ffn_pack)).reshape(width, 2 * ff)
+    down_own = gather_rows(down_weight).reshape(ff, width)
+
+    def to_shards(x):
+        return x.reshape(-1, ctx, seqs, krows).transpose(0, 2, 1, 3).reshape(-1, width)
+
+    def from_shards(x):
+        return x.reshape(-1, seqs, ctx, krows).transpose(0, 2, 1, 3).reshape(-1, width)
+
+    resid = hidden_in[0].astype(F32)
+    scale_one = lax.rsqrt(jnp.mean(resid * resid, axis=-1, keepdims=True) + EPSILON)
+    normed = gather_tokens(to_shards((resid * scale_one * gain_one).astype(BF)))
+    conv_all = mm(normed, conv_in_own)
+    rest_all = mm(normed, rest_own)
+    conv_lin = conv_all[:, : inner + bc].astype(BF).astype(F32)
+    step_lin = conv_all[:, inner + bc : inner + bc + heads]
+    q_lin = rest_all[:, :head]
+    k_lin = rest_all[:, head : head + HEAD_SIZE]
+    value = rest_all[:, head + HEAD_SIZE : head + 2 * HEAD_SIZE].astype(BF)
+    zgate = rest_all[:, head + 2 * HEAD_SIZE :]
+
+    widened = jnp.concatenate([jnp.zeros((taps, inner + bc), F32), conv_lin], axis=0)
+    widened_docs = jnp.concatenate([jnp.full((taps,), -1, jnp.int32), documents])
+    conv_act, conv_back = jax.vjp(
+        partial(conv_part, widened_docs=widened_docs, documents=documents),
+        widened,
+        conv_taps,
+        conv_shift,
+    )
+    conv_act = conv_act.astype(BF)
+    shared = lax.all_gather(conv_act[:, inner:], CTX, axis=0, tiled=False)
+    shared = shared.transpose(1, 0, 2).reshape(length, 2 * STATE)
+    write, read = shared[:, :STATE], shared[:, STATE:]
+    xin = conv_act[:, :inner]
+
+    places = jnp.arange(length).astype(F32)
+    query_turned, unturn = jax.vjp(
+        partial(rotate, places=places), q_lin.reshape(length, head // HEAD_SIZE, HEAD_SIZE)
+    )
+    key_turned, unturn_key = jax.vjp(
+        partial(rotate, places=places), k_lin.reshape(length, 1, HEAD_SIZE)
+    )
+    query = query_turned.astype(BF)
+    key = key_turned.astype(BF)[:, 0]
+    visible = same_document(documents)
+    scores = jnp.einsum("thd,ud->htu", query, key, preferred_element_type=F32) * HEAD_SIZE**-0.5
+    scores = jnp.where(visible[None], scores, NEGATIVE_FLOOR)
+    weights = jnp.where(
+        visible[None], jnp.exp(scores - jnp.max(scores, axis=-1, keepdims=True)), 0.0
+    )
+    probs = weights / jnp.sum(weights, axis=-1, keepdims=True)
+    probs_low = probs.astype(BF)
+    attn_mix = jnp.einsum("htu,ud->thd", probs_low, value, preferred_element_type=F32)
+    attn_low = attn_mix.reshape(length, head).astype(BF)
+
+    step_size, step_back = jax.vjp(
+        lambda lin, bias: jax.nn.softplus(lin + bias[None, :]), step_lin, bias_own
+    )
+    rate = -jnp.exp(decay_own)
+    terms = ssm_terms(step_size, rate, documents, ctx)
+    y, saved = ssm_forward(xin, write, read, terms, skip_own)
+    gated, gated_back = jax.vjp(lambda a, z: a * jax.nn.silu(z), y, zgate)
+    mean_square = lax.psum(jnp.sum(gated * gated, axis=-1), CTX) / dssm
+    scale_mix = lax.rsqrt(mean_square + EPSILON)[:, None]
+    ymix = (gated * scale_mix * gain_mix).astype(BF)
+
+    branch = scatter_tokens(mm(attn_low, attn_out_own) + mm(ymix, mamba_out_own))
+    mid = resid + branch
+    scale_two = lax.rsqrt(jnp.mean(mid * mid, axis=-1, keepdims=True) + EPSILON)
+    normed_two = gather_tokens(to_shards((mid * scale_two * gain_two).astype(BF)))
+    grad_all = gather_tokens(out_grad[0])
+
+    gate_up = mm(normed_two, ffn_own)
+    gate_lin, up_lin = gate_up[:, :ff], gate_up[:, ff:]
+    sigmoid_gate = jax.nn.sigmoid(gate_lin)
+    silu_gate = gate_lin * sigmoid_gate
+    hidden = (silu_gate * up_lin).astype(BF)
+    grad_hidden = mm_nt(grad_all, down_own)
+    grad_gate = (
+        grad_hidden * up_lin * (sigmoid_gate + silu_gate * (1.0 - sigmoid_gate))
+    ).astype(BF)
+    grad_up = (grad_hidden * silu_gate).astype(BF)
+    grad_gu = jnp.concatenate([grad_gate, grad_up], axis=1)
+    grad_n2 = from_shards(scatter_tokens(mm_nt(grad_gu, ffn_own)))
+    block_out = (mid + scatter_tokens(mm(hidden, down_own))).astype(BF)
+    down_grad = scatter_rows(mm_tn(hidden, grad_all).reshape(seqs, ff // seqs, width)).astype(F32)
+    ffn_grad = scatter_rows(mm_tn(normed_two, grad_gu).reshape(seqs, ctx, krows, 2 * ff))
+    ffn_grad = swap_columns(ffn_grad).astype(F32)
+
+    turned = grad_n2 * gain_two
+    hat_two = mid * scale_two
+    ffn_gain_grad = jnp.sum(grad_n2 * hat_two, axis=0)
+    grad_mid = out_grad[0].astype(F32) + scale_two * (
+        turned - hat_two * jnp.mean(turned * hat_two, axis=-1, keepdims=True)
+    )
+    branch_grad = gather_tokens(grad_mid.astype(BF))
+
+    attn_out_grad = scatter_rows(mm_tn(attn_low, branch_grad).reshape(seqs, -1, width)).astype(F32)
+    mamba_out_grad = scatter_rows(mm_tn(ymix, branch_grad).reshape(seqs, -1, width)).astype(F32)
+    grad_attn = mm_nt(branch_grad, attn_out_own).astype(BF).reshape(length, -1, HEAD_SIZE)
+    grad_ymix = mm_nt(branch_grad, mamba_out_own)
+
+    grad_prob = jnp.einsum("thd,ud->htu", grad_attn, value, preferred_element_type=F32)
+    delta = jnp.sum(probs * grad_prob, axis=-1, keepdims=True)
+    grad_score = (probs * (grad_prob - delta)).astype(BF)
+    grad_query = (
+        jnp.einsum("htu,ud->thd", grad_score, key, preferred_element_type=F32) * HEAD_SIZE**-0.5
+    )
+    grad_key = (
+        jnp.einsum("htu,thd->ud", grad_score, query, preferred_element_type=F32) * HEAD_SIZE**-0.5
+    )
+    grad_value = jnp.einsum("htu,thd->ud", probs_low, grad_attn, preferred_element_type=F32)
+    grad_q_lin = unturn(grad_query)[0].reshape(length, head).astype(BF)
+    grad_k_lin = unturn_key(grad_key[:, None])[0].reshape(length, HEAD_SIZE).astype(BF)
+
+    hat = gated * scale_mix
+    turned_mix = grad_ymix * gain_mix
+    mixer_gain_grad = jnp.sum(grad_ymix * hat, axis=0)
+    along = lax.psum(jnp.sum(turned_mix * hat, axis=-1), CTX)[:, None] / dssm
+    grad_gated = scale_mix * (turned_mix - hat * along)
+    grad_y, grad_zgate = gated_back(grad_gated)
+
+    grad_xin, grad_write, grad_read, grad_step, grad_rate, skip_grad = ssm_backward(
+        grad_y, xin, write, read, terms, skip_own, rate, saved
+    )
+    grad_shared = jnp.concatenate([grad_write, grad_read], axis=1).astype(BF)
+    grad_shared = lax.psum_scatter(
+        grad_shared.reshape(length, ctx, bc).transpose(1, 0, 2), CTX, scatter_dimension=0
+    ).astype(F32)
+    grad_widened, taps_grad, shift_grad = conv_back(
+        jnp.concatenate([grad_xin, grad_shared], axis=1)
+    )
+    grad_step_lin, step_bias_grad = step_back(grad_step)
+    log_decay_grad = grad_rate * rate
+    grad_conv = jnp.concatenate(
+        [
+            grad_widened[taps:].astype(BF),
+            jnp.pad(grad_step_lin.astype(BF), ((0, 0), (0, step_pad - heads))),
+        ],
+        axis=1,
+    )
+    grad_rest = jnp.concatenate(
+        [grad_q_lin, grad_k_lin, grad_value.astype(BF), grad_zgate.astype(BF)], axis=1
+    )
+
+    grad_normed = from_shards(
+        scatter_tokens(mm_nt(grad_conv, conv_in_own) + mm_nt(grad_rest, rest_own))
+    )
+    conv_grad = scatter_rows(mm_tn(normed, grad_conv).reshape(seqs, ctx, krows, conv_cols))
+    rest_grad = scatter_rows(mm_tn(normed, grad_rest).reshape(seqs, ctx, krows, rest_cols))
+    mixer_grad = swap_columns(jnp.concatenate([conv_grad, rest_grad], axis=2)).astype(F32)
+    turned_one = grad_normed * gain_one
+    hat_one = resid * scale_one
+    norm_gain_grad = jnp.sum(grad_normed * hat_one, axis=0)
+    input_grad = (
+        grad_mid
+        + scale_one
+        * (turned_one - hat_one * jnp.mean(turned_one * hat_one, axis=-1, keepdims=True))
+    ).astype(BF)
+
+    def spread_out(own, at, total):
+        return lax.dynamic_update_slice_in_dim(
+            jnp.zeros(own.shape[:-1] + (total,), F32), own, at, own.ndim - 1
+        )
+
+    def spread_channels(own):
+        full = spread_out(own[..., :inner], me * inner, dssm + 2 * STATE)
+        return lax.dynamic_update_slice_in_dim(full, own[..., inner:], dssm + me * bc, own.ndim - 1)
+
+    parts = (
+        norm_gain_grad,
+        ffn_gain_grad,
+        spread_out(mixer_gain_grad, me * inner, dssm),
+        spread_channels(shift_grad),
+        spread_channels(taps_grad).reshape(-1),
+        spread_out(step_bias_grad, me * heads, HS),
+        spread_out(log_decay_grad, me * heads, HS),
+        spread_out(skip_grad, me * heads, HS),
+    )
+    sums = lax.psum(jnp.concatenate(parts), (CTX, FSDP))
+    pieces = []
+    at = 0
+    for part in parts:
+        pieces.append(sums[at : at + part.size])
+        at += part.size
+    place = me * seqs + mine
+
+    def own_piece(full):
+        n = full.shape[-1] // (ctx * seqs)
+        return lax.dynamic_slice_in_dim(full, place * n, n, full.ndim - 1)
+
+    def by_row(packed, start, n):
+        return packed[:, :, start : start + n].transpose(1, 0, 2).reshape(krows, -1)
+
+    base = conv_cols
+    key_grad = mixer_grad[:, :, base + head : base + head + HEAD_SIZE]
+    value_grad = mixer_grad[:, :, base + head + HEAD_SIZE : base + head + 2 * HEAD_SIZE]
+
+    def over_queries(packed):
+        return (
+            packed.reshape(KEY_VALUE_HEADS, kv_repeat, krows, HEAD_SIZE)
+            .sum(axis=1)
+            .transpose(1, 0, 2)
+            .reshape(krows, -1)
+        )
+
+    return (
+        block_out[None],
+        input_grad[None],
+        own_piece(pieces[0]),
+        by_row(mixer_grad, base, head),
+        over_queries(key_grad),
+        over_queries(value_grad),
+        attn_out_grad,
+        by_row(mixer_grad, base + head + 2 * HEAD_SIZE, inner),
+        jnp.concatenate(
+            [by_row(mixer_grad, 0, inner), by_row(mixer_grad, inner, bc)], axis=1
+        ),
+        by_row(mixer_grad, inner + bc, heads),
+        own_piece(pieces[4].reshape(CONV, -1)),
+        own_piece(pieces[3]),
+        pieces[5],
+        pieces[6],
+        pieces[7],
+        own_piece(pieces[2]),
+        mamba_out_grad,
+        own_piece(pieces[1]),
+        by_row(ffn_grad, 0, ff),
+        by_row(ffn_grad, ff, ff),
+        down_grad,
+    )
+
+
 def solution(mesh):
     placed = (
-        P("fsdp", "ctx", None),
-        P("fsdp", "ctx", None),
-        P("fsdp", "ctx"),
-        P(("ctx", "fsdp")),
-        P(("ctx", "fsdp"), None),
-        P(("ctx", "fsdp"), None),
-        P(("ctx", "fsdp"), None),
-        P(("ctx", "fsdp"), None),
-        P(("ctx", "fsdp"), None),
-        P(("ctx", "fsdp"), None),
-        P(("ctx", "fsdp"), None),
-        P(None, ("ctx", "fsdp")),
-        P(("ctx", "fsdp")),
+        P(FSDP, CTX, None),
+        P(FSDP, CTX, None),
+        P(FSDP, CTX),
+        P((CTX, FSDP)),
+        P((CTX, FSDP), None),
+        P((CTX, FSDP), None),
+        P((CTX, FSDP), None),
+        P((CTX, FSDP), None),
+        P((CTX, FSDP), None),
+        P((CTX, FSDP), None),
+        P((CTX, FSDP), None),
+        P(None, (CTX, FSDP)),
+        P((CTX, FSDP)),
         P(),
         P(),
         P(),
-        P(("ctx", "fsdp")),
-        P(("ctx", "fsdp"), None),
-        P(("ctx", "fsdp")),
-        P(("ctx", "fsdp"), None),
-        P(("ctx", "fsdp"), None),
-        P(("ctx", "fsdp"), None),
-    )
+        P((CTX, FSDP)),
+        P((CTX, FSDP), None),
+        P((CTX, FSDP)),
+        P((CTX, FSDP), None),
+        P((CTX, FSDP), None),
+        P((CTX, FSDP), None),
+    )
+    ctx = mesh.shape[CTX]
+    whole_heads = QUERY_HEADS % ctx == 0 and HS % ctx == 0 and ctx % KEY_VALUE_HEADS == 0
     return jax.shard_map(
-        on_device,
+        head_parallel if whole_heads else on_device,
         mesh=mesh,
         in_specs=placed,
         out_specs=(
-            P("fsdp", "ctx", None),
-            P("fsdp", "ctx", None),
-            P(("ctx", "fsdp")),
-            P(("ctx", "fsdp"), None),
-            P(("ctx", "fsdp"), None),
-            P(("ctx", "fsdp"), None),
-            P(("ctx", "fsdp"), None),
-            P(("ctx", "fsdp"), None),
-            P(("ctx", "fsdp"), None),
-            P(("ctx", "fsdp"), None),
-            P(None, ("ctx", "fsdp")),
-            P(("ctx", "fsdp")),
+            P(FSDP, CTX, None),
+            P(FSDP, CTX, None),
+            P((CTX, FSDP)),
+            P((CTX, FSDP), None),
+            P((CTX, FSDP), None),
+            P((CTX, FSDP), None),
+            P((CTX, FSDP), None),
+            P((CTX, FSDP), None),
+            P((CTX, FSDP), None),
+            P((CTX, FSDP), None),
+            P(None, (CTX, FSDP)),
+            P((CTX, FSDP)),
             P(),
             P(),
             P(),
-            P(("ctx", "fsdp")),
-            P(("ctx", "fsdp"), None),
-            P(("ctx", "fsdp")),
-            P(("ctx", "fsdp"), None),
-            P(("ctx", "fsdp"), None),
-            P(("ctx", "fsdp"), None),
+            P((CTX, FSDP)),
+            P((CTX, FSDP), None),
+            P((CTX, FSDP)),
+            P((CTX, FSDP), None),
+            P((CTX, FSDP), None),
+            P((CTX, FSDP), None),
         ),
         check_vma=False,
     )

time: 5370 us -> 1290 us (0.24)
  waiting for transfers between devices: 4630 us -> 809 us
  matrix products: 283 us -> 136 us
  blocking collectives: 262 us -> 135 us
    reduce_scatter x10 -> x11, waiting for transfers between devices: 3920 us -> 379 us  [the longest x6 218 us: scatter_rows(): lax.psum_scatter(partial_sum.astype(BF), FSDP, scatter_dimension=0, tiled...]
    all_gather x12 -> x10, waiting for transfers between devices: 609 us -> 304 us  [the longest x4 150 us: gather_tokens(): return lax.all_gather(block, CTX, axis=0, tiled=True)]
    all_gather x6 -> x1, blocking collectives: 178 us -> 23.2 us  [gather_rows(): return lax.all_gather(shard, FSDP, axis=0, tiled=False)]
    dot_general x58 -> x36, matrix products: 282 us -> 136 us  [the longest x18 108 us: dotf(): lax.dot_general(left, right, (dims, ((), ())), preferred_element_type=F32)]
    psum x0 -> x1, waiting for transfers between devices: none -> 124 us  [head_parallel(): sums = lax.psum(jnp.concatenate(parts), (CTX, FSDP))]
    unnamed x28 -> x22, waiting for transfers between devices: 92.9 us -> 2.06 us
  transfers between devices with their start and end apart: 28 -> 24, of which waited for: 22 -> 20; matrix products, arithmetic and copies ran while one was open for 7% -> 15% of each run, Pallas kernels for 0% -> 0%
where the time goes in v1:
time: 1290 us; the launch traced here: 1280 us
  waiting for transfers between devices  809 us (63%)
  matrix products  136 us (11%)
  blocking collectives  135 us (10%)
  local copies, waits for them, and re-layouts  89.6 us (7%)
  other arithmetic  72.7 us (6%)
  starting transfers between devices  18.8 us (1%)
  between operations  17 us (1%)
    reduce_scatter x6, waiting for transfers between devices, scatter_rows(): lax.psum_scatter(partial_sum.astype(BF), FSDP, scatter_dimension=0, tiled...  218 us
    reduce_scatter x4, waiting for transfers between devices, scatter_tokens(): lax.psum_scatter(partial_sum.astype(BF), CTX, scatter_dimension=0, tiled=...  161 us
    all_gather x4, waiting for transfers between devices, gather_tokens(): return lax.all_gather(block, CTX, axis=0, tiled=True)  150 us
    all_gather x5, waiting for transfers between devices, gather_rows(): return lax.all_gather(shard, FSDP, axis=0, tiled=False)  146 us
    psum x1, waiting for transfers between devices, head_parallel(): sums = lax.psum(jnp.concatenate(parts), (CTX, FSDP))  124 us
    dot_general x18, matrix products, dotf(): lax.dot_general(left, right, (dims, ((), ())), preferred_element_type=F32)  108 us
    unnamed x1, blocking collectives  42.4 us
    all_to_all x2, blocking collectives, swap_columns(): return lax.all_to_all(packed, CTX, split_axis=0, concat_axis=0, tiled=True)  42.1 us
  transfers between devices with their start and end apart: 24, of which 20 were waited for; matrix products, arithmetic and copies ran while one was open for 15% of the time, Pallas kernels for 0%

profile of v1, /device:TPU:0, one launch (start us, length us, event | category | flops | bytes accessed | tf_op | source)
XLA Modules:
  0.0 1278.0 jit_solution(44175159064080902)
XLA Ops:
  15.3 23.3 %all_to_all.20 = bf16[8,64,1280]{2,1,0:T(8,128)(2,1)S(1)} all-to-all(bf16[8,64,1280]{2,1,0:T(8,128)(2,1)S(1)} %copy.358), channel_id=1, replica_groups=mesh['ctx'=8,'fsdp'=4] {'ctx'}, dimensions={0} | all-to-all | bytes 2621440 | tf_op jit(solution)/shard_map/all_to_all | solution.py:642
  40.0 42.4 %all-reduce.16 = bf16[29184]{0:T(1024)(128)(2,1)S(1)} all-reduce(bf16[29184]{0:T(1024)(128)(2,1)S(1)} %dynamic-update-slice.3), channel_id=2, replica_groups=mesh['ctx'=8,'fsdp'=4] {'ctx','fsdp'}, use_global_device_ids=true, to_apply=%add.16 | all-reduce | flops 29184 | bytes 116736
  87.0 37.6 %all-gather.20.cloned.1.call-done = bf16[1024,2048]{0,1:T(8,128)(2,1)} async-done(((bf16[128,2048]{0,1:T(8,128)(2,1)}), bf16[1024,2048]{0,1:T(8,128)(2,1)}) %all-gather.20.cloned.1.call-update) | async-done | bytes 4194320 | tf_op jit(solution)/shard_map/all_gather | solution.py:624
  124.6 5.2 fusion.166
  131.7 3.0 multiply_convert_fusion.4
  140.0 23.2 %all-gather.2 = bf16[128,2048]{1,0:T(8,128)(2,1)} all-gather(bf16[32,2048]{1,0:T(8,128)(2,1)S(1)} %copy-done.51), channel_id=4, replica_groups=mesh['ctx'=8,'fsdp'=4] {'fsdp'}, dimensions={0}, use_global_device_ids=true | all-gather | bytes 655360 | tf_op jit(solution)/shard_map/all_gather | solution.py:634
  170.7 27.9 %all-gather.26.cloned.1.call-done = bf16[32,64,768]{2,1,0:T(8,128)(2,1)} async-done(((bf16[8,64,768]{2,1,0:T(8,128)(2,1)}), bf16[32,64,768]{2,1,0:T(8,128)(2,1)}) %all-gather.26.cloned.1.call-update) | async-done | bytes 3145744 | tf_op jit(solution)/shard_map/all_gather | solution.py:634
  198.6 6.2 fusion.165
  211.1 4.6 fusion.113
  215.7 7.4 all-gather.30.cloned.1.call-done
  240.8 13.9 %psum.21 = f32[1024]{0:T(1024)S(1)} all-reduce(f32[1024]{0:T(1024)S(1)} %get-tuple-element.142), channel_id=1, replica_groups=mesh['ctx'=8,'fsdp'=4] {'ctx'}, use_global_device_ids=true, to_apply=%region_5.6 | all-reduce | flops 1024 | bytes 8192 | tf_op jit(solution)/shard_map/psum | solution.py:942
  254.6 7.1 all-gather.32.cloned.1.call-done
  261.7 8.8 add_convert_fusion.1
  273.8 18.9 %all_to_all.21 = bf16[8,64,1024]{2,1,0:T(8,128)(2,1)} all-to-all(bf16[8,64,1024]{2,1,0:T(8,128)(2,1)S(1)} %copy.375), channel_id=1, replica_groups=mesh['ctx'=8,'fsdp'=4] {'ctx'}, dimensions={0} | all-to-all | bytes 2097152 | tf_op jit(solution)/shard_map/all_to_all | solution.py:642
  292.7 8.8 all-gather.22.cloned.1.call-start
  301.6 19.3 %reduce-scatter.12.cloned.1.call-done = bf16[128,2048]{1,0:T(8,128)(2,1)} async-done(((bf16[1024,2048]{1,0:T(8,128)(2,1)}), bf16[128,2048]{1,0:T(8,128)(2,1)}) %reduce-scatter.12.cloned.1.call-update) | async-done | bytes 524304 | tf_op jit(solution)/shard_map/reduce_scatter | solution.py:628
  329.9 73.5 %all-gather.34.cloned.1.call-done = bf16[32,64,1024]{2,1,0:T(8,128)(2,1)} async-done(((bf16[8,64,1024]{2,1,0:T(8,128)(2,1)}), bf16[32,64,1024]{2,1,0:T(8,128)(2,1)}) %all-gather.34.cloned.1.call-update) | async-done | bytes 4194320 | tf_op jit(solution)/shard_map/all_gather | solution.py:634
  403.3 38.6 %all-gather.22.cloned.1.call-done = bf16[1024,2048]{0,1:T(8,128)(2,1)} async-done(((bf16[128,2048]{0,1:T(8,128)(2,1)}), bf16[1024,2048]{0,1:T(8,128)(2,1)}) %all-gather.22.cloned.1.call-update) | async-done | bytes 4194320 | tf_op jit(solution)/shard_map/all_gather | solution.py:624
  441.9 10.0 fusion.168
  452.0 37.6 %all-gather.36.cloned.1.call-done = bf16[512,2048]{1,0:T(8,128)(2,1)} async-done(((bf16[128,2048]{1,0:T(8,128)(2,1)}), bf16[512,2048]{1,0:T(8,128)(2,1)}) %all-gather.36.cloned.1.call-update) | async-done | bytes 2097168 | tf_op jit(solution)/shard_map/all_gather | solution.py:634
  489.5 37.4 %all-gather.38.cloned.1.call-done = bf16[1,1024,2048]{2,1,0:T(8,128)(2,1)} async-done(((bf16[1,128,2048]{2,1,0:T(8,128)(2,1)}), bf16[1,1024,2048]{2,1,0:T(8,128)(2,1)}) %all-gather.38.cloned.1.call-update) | async-done | bytes 4194320 | tf_op jit(solution)/shard_map/all_gather | solution.py:624
  526.9 8.1 multiply_convert_fusion.2
  536.4 6.2 convolution_convert_fusion.2
  542.6 51.5 %reduce-scatter.16.cloned.1.call-done = bf16[128,2048]{1,0:T(8,128)(2,1)} async-done(((bf16[1024,2048]{1,0:T(8,128)(2,1)}), bf16[128,2048]{1,0:T(8,128)(2,1)}) %reduce-scatter.16.cloned.1.call-update) | async-done | bytes 524304 | tf_op jit(solution)/shard_map/reduce_scatter | solution.py:628
  596.3 2.3 copy.377
  598.6 2.5 copy.378
  601.1 2.6 multiply_reduce_fusion.13
  603.7 2.6 fusion.156
  606.6 36.6 %all-gather.24.cloned.1.call-done = bf16[1024,2048]{1,0:T(8,128)(2,1)} async-done(((bf16[128,2048]{1,0:T(8,128)(2,1)}), bf16[1024,2048]{1,0:T(8,128)(2,1)}) %all-gather.24.cloned.1.call-update) | async-done | bytes 4194320 | tf_op jit(solution)/shard_map/all_gather | solution.py:624
  643.2 6.8 multiply_reduce_fusion.9
  650.0 13.1 %psum.22 = f32[1024]{0:T(1024)S(1)} all-reduce(f32[1024]{0:T(1024)S(1)} %get-tuple-element.124), channel_id=1, replica_groups=mesh['ctx'=8,'fsdp'=4] {'ctx'}, use_global_device_ids=true, to_apply=%region_12.13 | all-reduce | flops 1024 | bytes 8192 | tf_op jit(solution)/shard_map/psum | solution.py:998
  663.1 5.8 multiply_reduce_fusion.8
  670.3 3.7 multiply_reduce_fusion.3
  675.1 2.3 fusion.115
  695.9 2.3 maximum_bitcast_fusion
  698.6 9.4 convolution_convert_fusion.1
  708.1 6.3 fusion.12
  716.9 3.1 fusion.32
  728.3 3.8 fusion.15
  732.4 4.4 convolution_convert_fusion.6
  737.9 4.7 multiply_reduce_fusion.6
  745.5 3.8 convolution_convert_fusion.4
  749.6 4.1 fusion.2
  753.8 2.4 fusion.20
  759.4 2.4 fusion.45
  762.5 4.8 convolution_convert_fusion.3
  768.7 5.2 convolution_convert_fusion.5
  774.3 5.7 fusion.98
  779.9 4.5 add_convert_fusion
  786.3 4.4 convolution_convert_fusion
  790.7 22.6 %reduce-scatter.30.cloned.1.call-done = bf16[1,8,64,1024]{3,2,1,0:T(8,128)(2,1)} async-done(((bf16[4,8,64,1024]{3,2,1,0:T(8,128)(2,1)}), bf16[1,8,64,1024]{3,2,1,0:T(8,128)(2,1)}) %reduce-scatter.30.cloned.1.call-update) | async-done | bytes 1048592 | tf_op jit(solution)/shard_map/reduce_scatter | solution.py:638
  813.3 3.7 all-to-all-start.3
  817.0 42.9 %reduce-scatter.32.cloned.1.call-done = bf16[1,128,2048]{2,1,0:T(8,128)(2,1)} async-done(((bf16[4,128,2048]{2,1,0:T(8,128)(2,1)}), bf16[1,128,2048]{2,1,0:T(8,128)(2,1)}) %reduce-scatter.32.cloned.1.call-update) | async-done | bytes 524304 | tf_op jit(solution)/shard_map/reduce_scatter | solution.py:638
  865.9 17.8 %reduce-scatter.26.cloned.1.call-done = bf16[1,32,2048]{2,1,0:T(8,128)(2,1)} async-done(((bf16[4,32,2048]{2,1,0:T(8,128)(2,1)}), bf16[1,32,2048]{2,1,0:T(8,128)(2,1)}) %reduce-scatter.26.cloned.1.call-update) | async-done | bytes 131088 | tf_op jit(solution)/shard_map/reduce_scatter | solution.py:638
  885.3 42.6 %reduce-scatter.22.cloned.1.call-done = bf16[1,8,64,512]{3,2,1,0:T(8,128)(2,1)} async-done(((bf16[4,8,64,512]{3,2,1,0:T(8,128)(2,1)}), bf16[1,8,64,512]{3,2,1,0:T(8,128)(2,1)}) %reduce-scatter.22.cloned.1.call-update) | async-done | bytes 524304 | tf_op jit(solution)/shard_map/reduce_scatter | solution.py:638
  927.9 61.9 %reduce-scatter.24.cloned.1.call-done = bf16[1,8,64,768]{3,2,1,0:T(8,128)(2,1)} async-done(((bf16[4,8,64,768]{3,2,1,0:T(8,128)(2,1)}), bf16[1,8,64,768]{3,2,1,0:T(8,128)(2,1)}) %reduce-scatter.24.cloned.1.call-update) | async-done | bytes 786448 | tf_op jit(solution)/shard_map/reduce_scatter | solution.py:638
  989.8 2.5 pad_maximum_fusion.5
  992.3 4.3 all-to-all-start.2
  997.5 30.0 %reduce-scatter.28.cloned.1.call-done = bf16[1,96,2048]{2,1,0:T(8,128)(2,1)} async-done(((bf16[4,96,2048]{2,1,0:T(8,128)(2,1)}), bf16[1,96,2048]{2,1,0:T(8,128)(2,1)}) %reduce-scatter.28.cloned.1.call-update) | async-done | bytes 393232 | tf_op jit(solution)/shard_map/reduce_scatter | solution.py:638
  1036.8 44.7 %reduce-scatter.20.cloned.1.call-done = bf16[128,2048]{1,0:T(8,128)(2,1)} async-done(((bf16[1024,2048]{1,0:T(8,128)(2,1)}), bf16[128,2048]{1,0:T(8,128)(2,1)}) %reduce-scatter.20.cloned.1.call-update) | async-done | bytes 524304 | tf_op jit(solution)/shard_map/reduce_scatter | solution.py:628
  1084.9 2.7 copy.399
  1090.3 45.9 %reduce-scatter.14.cloned.1.call-done = bf16[128,2048]{1,0:T(8,128)(2,1)} async-done(((bf16[1024,2048]{1,0:T(8,128)(2,1)}), bf16[128,2048]{1,0:T(8,128)(2,1)}) %reduce-scatter.14.cloned.1.call-update) | async-done | bytes 524304 | tf_op jit(solution)/shard_map/reduce_scatter | solution.py:628
  1136.2 3.3 fusion.71
  1139.5 123.8 %all-reduce.19.cloned.1.call-done = f32[25232]{0:T(1024)} async-done(((f32[25232]{0:T(1024)}), f32[25232]{0:T(1024)}) %all-reduce.19.cloned.1.call-update) | async-done | bytes 100944 | tf_op jit(solution)/shard_map/psum | solution.py:1059
  (558 shorter events, 142.4 us)
Async XLA Ops:
  7.2 79.8 %all-gather.28.cloned.1.call-start = ((), (), s32[]{:S(2)}) async-start(), calls=%async_computation.31 | async-start | bytes 2621440 | tf_op jit(solution)/shard_map/all_gather | solution.py:634
  15.2 24.3 %copy-start.123 = (bf16[4,112]{1,0:T(4,128)(2,1)S(1)}, bf16[4,112]{1,0:T(4,128)(2,1)}, u32[]{:S(2)}) copy-start(bf16[4,112]{1,0:T(4,128)(2,1)} %param.35) | copy-start | bytes 2692
  15.3 24.4 %copy-start.136 = (s32[1,128]{1,0:T(1,128)S(1)}, s32[1,128]{1,0:T(1,128)}, u32[]{:S(2)}) copy-start(s32[1,128]{1,0:T(1,128)} %param.26) | copy-start | bytes 1540
  15.3 24.4 %copy-start.127 = (bf16[64]{0:T(256)(128)(2,1)S(1)}, bf16[64]{0:T(256)(128)(2,1)}, u32[]{:S(2)}) copy-start(bf16[64]{0:T(256)(128)(2,1)} %param.27) | copy-start | bytes 388
  15.3 24.4 %copy-start.128 = (bf16[64]{0:T(256)(128)(2,1)S(1)}, bf16[64]{0:T(256)(128)(2,1)}, u32[]{:S(2)}) copy-start(bf16[64]{0:T(256)(128)(2,1)} %param.42) | copy-start | bytes 388
  15.3 24.3 %copy-start.129 = (bf16[96]{0:T(256)(128)(2,1)S(1)}, bf16[96]{0:T(256)(128)(2,1)}, u32[]{:S(2)}) copy-start(bf16[96]{0:T(256)(128)(2,1)} %param.40) | copy-start | bytes 580
  15.3 24.3 %copy-start.130 = (bf16[112]{0:T(256)(128)(2,1)S(1)}, bf16[112]{0:T(256)(128)(2,1)}, u32[]{:S(2)}) copy-start(bf16[112]{0:T(256)(128)(2,1)} %param.36) | copy-start | bytes 676
  15.3 67.2 %copy-start.1 = (bf16[1,128,2048]{2,1,0:T(8,128)(2,1)S(1)}, bf16[1,128,2048]{2,1,0:T(8,128)(2,1)}, u32[]{:S(2)}) copy-start(bf16[1,128,2048]{2,1,0:T(8,128)(2,1)} %param.24) | copy-start | bytes 1572868
  39.5 85.1 %all-gather.20.cloned.1.call-start = ((), (), s32[]{:S(2)}) async-start(), calls=%async_computation.15 | async-start | bytes 4718592 | tf_op jit(solution)/shard_map/all_gather | solution.py:624
  84.9 113.7 %all-gather.26.cloned.1.call-start = ((), (), s32[]{:S(2)}) async-start(), calls=%async_computation.30 | async-start | bytes 3932160 | tf_op jit(solution)/shard_map/all_gather | solution.py:634
  85.9 137.2 %all-gather.30.cloned.1.call-start = ((), (), s32[]{:S(2)}) async-start(), calls=%async_computation.32 | async-start | bytes 1179648 | tf_op jit(solution)/shard_map/all_gather | solution.py:910
  86.9 44.2 %copy-start.75 = (pred[1024]{0:T(1024)(128)(4,1)}, pred[1024]{0:T(1024)(128)(4,1)S(1)}, u32[]{:S(2)}) copy-start(pred[1024]{0:T(1024)(128)(4,1)S(1)} %get-tuple-element.211) | copy-start | bytes 3076
  86.9 44.2 %copy-start.77 = (pred[1024]{0:T(1024)(128)(4,1)}, pred[1024]{0:T(1024)(128)(4,1)S(1)}, u32[]{:S(2)}) copy-start(pred[1024]{0:T(1024)(128)(4,1)S(1)} %get-tuple-element.212) | copy-start | bytes 3076
  86.9 44.2 %copy-start.79 = (pred[1024]{0:T(1024)(128)(4,1)}, pred[1024]{0:T(1024)(128)(4,1)S(1)}, u32[]{:S(2)}) copy-start(pred[1024]{0:T(1024)(128)(4,1)S(1)} %get-tuple-element.213) | copy-start | bytes 3076
  86.9 44.2 %copy-start.65 = (f32[1,448]{1,0:T(1,128)}, f32[1,448]{1,0:T(1,128)S(1)}, u32[]{:S(2)}) copy-start(f32[1,448]{1,0:T(1,128)S(1)} %get-tuple-element.192) | copy-start | bytes 5380
  86.9 44.2 %copy-start.67 = (f32[1,448]{1,0:T(1,128)}, f32[1,448]{1,0:T(1,128)S(1)}, u32[]{:S(2)}) copy-start(f32[1,448]{1,0:T(1,128)S(1)} %get-tuple-element.193) | copy-start | bytes 5380
  87.0 44.2 %copy-start.69 = (f32[1,448]{1,0:T(1,128)}, f32[1,448]{1,0:T(1,128)S(1)}, u32[]{:S(2)}) copy-start(f32[1,448]{1,0:T(1,128)S(1)} %get-tuple-element.194) | copy-start | bytes 5380
  131.7 6.3 copy-start.138
  131.7 7.0 copy-start.125
  131.7 8.2 copy-start.51
  136.4 125.4 %all-gather.32.cloned.1.call-start = ((), (), s32[]{:S(2)}) async-start(), calls=%async_computation.33 | async-start | bytes 1966080 | tf_op jit(solution)/shard_map/all_gather | solution.py:634
  137.0 183.9 %reduce-scatter.12.cloned.1.call-start = ((), (), s32[]{:S(2)}) async-start(), calls=%async_computation.16 | async-start | bytes 4718592 | tf_op jit(solution)/shard_map/reduce_scatter | solution.py:628
  138.1 29.0 %copy-start.117 = (f32[6]{0:T(128)}, f32[6]{0:T(128)S(1)}, u32[]{:S(2)}) copy-start(f32[6]{0:T(128)S(1)} %dynamic_slice.48) | copy-start | bytes 76
  138.8 30.2 %copy-start.119 = (f32[6]{0:T(128)}, f32[6]{0:T(128)S(1)}, u32[]{:S(2)}) copy-start(f32[6]{0:T(128)S(1)} %exponential_negate_fusion) | copy-start | bytes 76
  139.1 29.9 %copy-start.89 = (pred[8,1,128]{2,0,1:T(8,128)(4,1)}, pred[8,1,128]{2,0,1:T(8,128)(4,1)S(1)}, u32[]{:S(2)}) copy-start(pred[8,1,128]{2,0,1:T(8,128)(4,1)S(1)} %copy.499) | copy-start | bytes 3076
  139.1 65.7 %copy-start.81 = (pred[8,1,128]{2,0,1:T(8,128)(4,1)}, pred[8,1,128]{2,0,1:T(8,128)(4,1)S(1)}, u32[]{:S(2)}) copy-start(pred[8,1,128]{2,0,1:T(8,128)(4,1)S(1)} %copy.500) | copy-start | bytes 3076
  198.6 6.4 copy-start.115
  270.6 132.7 %all-gather.34.cloned.1.call-start = ((), (), s32[]{:S(2)}) async-start(), calls=%async_computation.34 | async-start | bytes 5242880 | tf_op jit(solution)/shard_map/all_gather | solution.py:634
  273.2 28.3 %copy-start.56 = (f32[32,64]{1,0:T(8,128)S(1)}, f32[32,64]{1,0:T(8,128)}, u32[]{:S(2)}) copy-start(f32[32,64]{1,0:T(8,128)} %get-tuple-element.187) | copy-start | bytes 24580
  292.7 149.2 %all-gather.22.cloned.1.call-start = ((), (), s32[]{:S(2)}) async-start(), calls=%async_computation.17 | async-start | bytes 4718592 | tf_op jit(solution)/shard_map/all_gather | solution.py:624
  322.3 281.4 %copy-start.100 = (f32[128]{0:T(128)}, f32[128]{0:T(128)S(1)}, u32[]{:S(2)}) copy-start(f32[128]{0:T(128)S(1)} %add_rsqrt_fusion.1) | copy-start | bytes 1540
  328.5 161.1 %all-gather.36.cloned.1.call-start = ((), (), s32[]{:S(2)}) async-start(), calls=%async_computation.35 | async-start | bytes 2621440 | tf_op jit(solution)/shard_map/all_gather | solution.py:634
  329.2 197.7 %all-gather.38.cloned.1.call-start = ((), (), s32[]{:S(2)}) async-start(), calls=%async_computation.36 | async-start | bytes 4718592 | tf_op jit(solution)/shard_map/all_gather | solution.py:624
  329.8 264.3 %reduce-scatter.16.cloned.1.call-start = ((), (), s32[]{:S(2)}) async-start(), calls=%async_computation.19 | async-start | bytes 4718592 | tf_op jit(solution)/shard_map/reduce_scatter | solution.py:628
  526.9 9.4 copy-start.133
  542.6 100.7 %all-gather.24.cloned.1.call-start = ((), (), s32[]{:S(2)}) async-start(), calls=%async_computation.20 | async-start | bytes 4718592 | tf_op jit(solution)/shard_map/all_gather | solution.py:624
  603.7 46.3 %copy-start.113 = (f32[128]{0:T(128)}, f32[128]{0:T(128)S(1)}, u32[]{:S(2)}) copy-start(f32[128]{0:T(128)S(1)} %broadcast_multiply_fusion.4) | copy-start | bytes 1540
  606.4 130.5 %reduce-scatter.18.cloned.1.call-start = ((), (), s32[]{:S(2)}) async-start(), calls=%async_computation.21 | async-start | bytes 1179648 | tf_op jit(solution)/shard_map/reduce_scatter | solution.py:1006
  698.2 115.2 %reduce-scatter.30.cloned.1.call-start = ((), (), s32[]{:S(2)}) async-start(), calls=%async_computation.28 | async-start | bytes 5242880 | tf_op jit(solution)/shard_map/reduce_scatter | solution.py:638
  708.0 152.0 %reduce-scatter.32.cloned.1.call-start = ((), (), s32[]{:S(2)}) async-start(), calls=%async_computation.29 | async-start | bytes 2621440 | tf_op jit(solution)/shard_map/reduce_scatter | solution.py:638
  714.4 169.3 %reduce-scatter.26.cloned.1.call-start = ((), (), s32[]{:S(2)}) async-start(), calls=%async_computation.26 | async-start | bytes 655360 | tf_op jit(solution)/shard_map/reduce_scatter | solution.py:638
  728.3 16.4 %copy-start.83 = (bf16[1024,6]{0,1:T(8,128)(2,1)}, bf16[1024,6]{0,1:T(8,128)(2,1)S(1)}, u32[]{:S(2)}) copy-start(bf16[1024,6]{0,1:T(8,128)(2,1)S(1)} %get-tuple-element.136) | copy-start | bytes 36868
  732.2 195.7 %reduce-scatter.22.cloned.1.call-start = ((), (), s32[]{:S(2)}) async-start(), calls=%async_computation.24 | async-start | bytes 2621440 | tf_op jit(solution)/shard_map/reduce_scatter | solution.py:638
  749.3 240.5 %reduce-scatter.24.cloned.1.call-start = ((), (), s32[]{:S(2)}) async-start(), calls=%async_computation.25 | async-start | bytes 3932160 | tf_op jit(solution)/shard_map/reduce_scatter | solution.py:638
  767.3 6.9 copy-start.49
  767.4 260.2 %reduce-scatter.28.cloned.1.call-start = ((), (), s32[]{:S(2)}) async-start(), calls=%async_computation.27 | async-start | bytes 1966080 | tf_op jit(solution)/shard_map/reduce_scatter | solution.py:638
  773.9 307.6 %reduce-scatter.20.cloned.1.call-start = ((), (), s32[]{:S(2)}) async-start(), calls=%async_computation.22 | async-start | bytes 4718592 | tf_op jit(solution)/shard_map/reduce_scatter | solution.py:628
  784.5 351.7 %reduce-scatter.14.cloned.1.call-start = ((), (), s32[]{:S(2)}) async-start(), calls=%async_computation.18 | async-start | bytes 4718592 | tf_op jit(solution)/shard_map/reduce_scatter | solution.py:628
  790.7 26.3 %copy-start.47 = (f32[32,64]{1,0:T(8,128)S(1)}, f32[32,64]{1,0:T(8,128)}, u32[]{:S(2)}) copy-start(f32[32,64]{1,0:T(8,128)} %copy-done.46) | copy-start | bytes 24580
  813.3 48.8 %all-to-all-start.3 = ((bf16[8,64,1024]{2,1,0:T(8,128)(2,1)}), bf16[8,64,1024]{2,1,0:T(8,128)(2,1)S(1)}, u32[]{:S(2)}, u32[]{:S(2)}) async-start(bf16[8,64,1024]{2,1,0:T(8,128)(2,1)} %bitcast.490), calls=%async_computation.13 | async-start | bytes 2097152 | tf_op jit(solution)/shard_map/all_to_all | solution.py:642
  862.6 22.6 %copy-start.71 = (f32[448]{0:T(512)S(1)}, f32[448]{0:T(512)}, u32[]{:S(2)}) copy-start(f32[448]{0:T(512)} %get-tuple-element.117) | copy-start | bytes 5380
  862.7 22.6 %copy-start.72 = (f32[448]{0:T(512)S(1)}, f32[448]{0:T(512)}, u32[]{:S(2)}) copy-start(f32[448]{0:T(512)} %get-tuple-element.118) | copy-start | bytes 5380
  862.7 22.6 %copy-start.73 = (f32[448]{0:T(512)S(1)}, f32[448]{0:T(512)}, u32[]{:S(2)}) copy-start(f32[448]{0:T(512)} %get-tuple-element.119) | copy-start | bytes 5380
  862.7 22.6 %copy-start.74 = (f32[448]{0:T(512)S(1)}, f32[448]{0:T(512)}, u32[]{:S(2)}) copy-start(f32[448]{0:T(512)} %get-tuple-element.131) | copy-start | bytes 5380
  989.8 7.1 copy-start.102
  992.3 37.2 %all-to-all-start.2 = ((bf16[8,64,1280]{2,1,0:T(8,128)(2,1)}), bf16[8,64,1280]{2,1,0:T(8,128)(2,1)}, u32[]{:S(2)}, u32[]{:S(2)}) async-start(bf16[8,64,1280]{2,1,0:T(8,128)(2,1)} %pad_maximum_fusion.5), calls=%async_computation.9 | async-start | bytes 2621440 | tf_op jit(solution)/shard_map/all_to_all | solution.py:642
  996.6 266.7 %all-reduce.19.cloned.1.call-start = ((), (), s32[]{:S(2)}) async-start(), calls=%async_computation.23 | async-start | bytes 204800 | tf_op jit(solution)/shard_map/psum | solution.py:1059
  1036.8 50.8 %copy-start.23 = (f32[1,128,2048]{1,2,0:T(8,128)S(1)}, f32[1,128,2048]{1,2,0:T(8,128)}, u32[]{:S(2)}) copy-start(f32[1,128,2048]{1,2,0:T(8,128)} %copy-done.22) | copy-start | bytes 3145732
  1036.8 50.8 %copy-start.112 = (f32[128]{0:T(128)S(1)}, f32[128]{0:T(128)}, u32[]{:S(2)}) copy-start(f32[128]{0:T(128)} %copy-done.111) | copy-start | bytes 1540
  1084.9 51.4 %copy-start.2 = (bf16[1,128,2048]{2,1,0:T(8,128)(2,1)S(1)}, bf16[1,128,2048]{2,1,0:T(8,128)(2,1)}, u32[]{:S(2)}) copy-start(bf16[1,128,2048]{2,1,0:T(8,128)(2,1)} %param.24) | copy-start | bytes 1572868
  1084.9 51.4 %copy-start.6 = (f32[128,2048]{1,0:T(8,128)S(1)}, f32[128,2048]{1,0:T(8,128)}, u32[]{:S(2)}) copy-start(f32[128,2048]{1,0:T(8,128)} %copy.378) | copy-start | bytes 3145732
  1084.9 51.4 %copy-start.18 = (bf16[128,2048]{1,0:T(8,128)(2,1)S(1)}, bf16[128,2048]{1,0:T(8,128)(2,1)}, u32[]{:S(2)}) copy-start(bf16[128,2048]{1,0:T(8,128)(2,1)} %reduce-scatter.12.cloned.1.call-done) | copy-start | bytes 1572868
  1084.9 51.4 %copy-start.101 = (f32[128]{0:T(128)S(1)}, f32[128]{0:T(128)}, u32[]{:S(2)}) copy-start(f32[128]{0:T(128)} %copy-done.100) | copy-start | bytes 1540
  1084.9 51.4 %copy-start.114 = (f32[128]{0:T(128)S(1)}, f32[128]{0:T(128)}, u32[]{:S(2)}) copy-start(f32[128]{0:T(128)} %copy-done.113) | copy-start | bytes 1540
  (107 other events, 288.3 us)
Sparse Core Ops, SparseCore 0:
  39.6 46.2 all-gather.27
  88.4 36.1 all-gather.19
  126.8 71.7 all-gather.25
  200.9 22.1 all-gather.29
  224.6 37.1 all-gather.31
  270.7 50.1 reduce-scatter.11
  322.5 80.7 all-gather.33
  405.9 35.9 all-gather.21
  443.6 45.9 all-gather.35
  491.4 35.4 all-gather.37
  542.7 51.3 reduce-scatter.15
  606.5 36.6 all-gather.23
  698.3 36.0 reduce-scatter.17
  736.5 76.7 reduce-scatter.29
  815.5 44.3 reduce-scatter.31
  862.7 20.9 reduce-scatter.25
  885.8 42.1 reduce-scatter.21
  930.2 59.5 reduce-scatter.23
  992.2 35.2 reduce-scatter.27
  1031.1 50.3 reduce-scatter.19
  1084.9 51.3 reduce-scatter.13
  1142.7 120.5 all-reduce.18

commit v2 on v1

--- a/solution.py
+++ b/solution.py
@@ -1,9 +1,12 @@
 from functools import partial
+import itertools
 import math
 
 import jax
 import jax.numpy as jnp
 from jax import lax
+from jax.experimental import pallas as pl
+from jax.experimental.pallas import tpu as pltpu
 from jax.sharding import PartitionSpec as P
 
 CTX = "ctx"
@@ -620,14 +623,333 @@
     return dotf(left, right, ((0,), (0,)))
 
 
-def gather_tokens(block):
-    return lax.all_gather(block, CTX, axis=0, tiled=True)
-
-
-def scatter_tokens(partial_sum):
-    return lax.psum_scatter(
-        partial_sum.astype(BF), CTX, scatter_dimension=0, tiled=True
-    ).astype(F32)
+MESH = pl.DeviceIdType.MESH
+PLANE = 8
+
+
+def plane():
+    me = lax.axis_index(CTX)
+    sibling = me + 1 - 2 * (me % 2)
+    by_x = me + 2 - 4 * ((me // 2) % 2)
+    by_y = me + 4 - 8 * (me // 4)
+    return me, sibling, by_x, by_y
+
+
+def greet(peers):
+    barrier = pltpu.get_barrier_semaphore()
+    for axis, other in peers:
+        pl.semaphore_signal(barrier, inc=1, device_id={axis: other}, device_id_type=MESH)
+    pl.semaphore_wait(barrier, len(peers))
+
+
+def remote(src, dst, send_sem, recv_sem, axis, to):
+    return pltpu.make_async_remote_copy(
+        src_ref=src,
+        dst_ref=dst,
+        send_sem=send_sem,
+        recv_sem=recv_sem,
+        device_id={axis: to},
+        device_id_type=MESH,
+    )
+
+
+def gather_kernel(pieces, x_ref, o_ref, own_sem, send_sem, recv_sem):
+    rows = x_ref.shape[0]
+    n = rows // pieces
+    half = pieces // 2
+    me, sibling, by_x, by_y = plane()
+    across = by_x + by_y - me
+    greet([(CTX, sibling), (CTX, by_x), (CTX, by_y)])
+    keep = pltpu.make_async_copy(x_ref, o_ref.at[pl.ds(me * rows, rows)], own_sem)
+    keep.start()
+    started = []
+
+    def at(block, piece):
+        return o_ref.at[pl.ds(block * rows + piece * n, n)]
+
+    def go(src, block, piece, kind, to, slot):
+        copy = remote(
+            src, at(block, piece), send_sem.at[slot, piece], recv_sem.at[kind, piece], CTX, to
+        )
+        copy.start()
+        started.append(copy)
+
+    def arrived(block, piece, kind):
+        here = at(block, piece)
+        remote(here, here, send_sem.at[0, piece], recv_sem.at[kind, piece], CTX, sibling).wait_recv()
+
+    for i in range(pieces):
+        a, b = i, pieces - 1 - i
+        go(x_ref.at[pl.ds(a * n, n)], me, a, 1, by_x, 1)
+        go(x_ref.at[pl.ds(b * n, n)], me, b, 2, by_y, 2)
+    for i in range(pieces):
+        go(x_ref.at[pl.ds(i * n, n)], me, i, 0, sibling, 0)
+    for i in range(pieces):
+        a, b = i, pieces - 1 - i
+        arrived(by_x, a, 1)
+        if i < half:
+            go(at(by_x, a), by_x, a, 5, by_y, 5)
+        go(at(by_x, a), by_x, a, 3, sibling, 3)
+        arrived(by_y, b, 2)
+        if i < half:
+            go(at(by_y, b), by_y, b, 5, by_x, 5)
+        go(at(by_y, b), by_y, b, 4, sibling, 4)
+    for i in range(half):
+        for p in (i, pieces - 1 - i):
+            arrived(across, p, 5)
+            go(at(across, p), across, p, 6, sibling, 6)
+    shift = sibling - me
+    for p in range(pieces):
+        arrived(sibling, p, 0)
+        arrived(by_x + shift, p, 3)
+        arrived(by_y + shift, p, 4)
+        arrived(across + shift, p, 6)
+    for copy in started:
+        copy.wait_send()
+    keep.wait()
+
+
+def gather_tokens(block, ids, pieces=4):
+    rows, cols = block.shape
+    return pl.pallas_call(
+        partial(gather_kernel, pieces),
+        out_shape=jax.ShapeDtypeStruct((PLANE * rows, cols), block.dtype),
+        in_specs=[pl.BlockSpec(memory_space=pl.ANY)],
+        out_specs=pl.BlockSpec(memory_space=pl.ANY),
+        scratch_shapes=[
+            pltpu.SemaphoreType.DMA,
+            pltpu.SemaphoreType.DMA((7, pieces)),
+            pltpu.SemaphoreType.DMA((7, pieces)),
+        ],
+        cost_estimate=lasting(22 if cols > 1024 else 8),
+        compiler_params=pltpu.CompilerParams(collective_id=next(ids), has_side_effects=True),
+    )(block)
+
+
+def scatter_kernel(p_ref, o_ref, own, got, out, rx, ry, dx, dy, own_sem, send_sem, recv_sem):
+    rows = o_ref.shape[0]
+    h = rows // 2
+    me, sibling, by_x, by_y = plane()
+    across = by_x + by_y - me
+    shift = sibling - me
+    greet([(CTX, sibling), (CTX, by_x), (CTX, by_y)])
+    top, low = pl.ds(0, h), pl.ds(h, h)
+    loads, sends = [], []
+    for k, block in enumerate((across, by_x, by_y, me)):
+        for j in range(2):
+            copy = remote(
+                p_ref.at[pl.ds((block + shift) * rows + j * h, h)],
+                got.at[k, pl.ds(j * h, h)],
+                send_sem.at[k * 2 + j],
+                recv_sem.at[k * 2 + j],
+                CTX,
+                sibling,
+            )
+            copy.start()
+            sends.append(copy)
+            load = pltpu.make_async_copy(
+                p_ref.at[pl.ds(block * rows + j * h, h)],
+                own.at[k, pl.ds(j * h, h)],
+                own_sem.at[k * 2 + j],
+            )
+            load.start()
+            loads.append(load)
+
+    def pair(k, j):
+        sends[k * 2 + j].wait_recv()
+        loads[k * 2 + j].wait()
+        part = pl.ds(j * h, h)
+        return own[k, part].astype(F32) + got[k, part].astype(F32)
+
+    def go(src, dst, slot, to):
+        copy = remote(src, dst, send_sem.at[slot], recv_sem.at[slot], CTX, to)
+        copy.start()
+        sends.append(copy)
+        return copy
+
+    out[0, top] = pair(0, 0).astype(out.dtype)
+    across_x = go(out.at[0, top], dx, 8, by_x)
+    out[0, low] = pair(0, 1).astype(out.dtype)
+    across_y = go(out.at[0, low], dy, 9, by_y)
+    out[1, top] = pair(1, 0).astype(out.dtype)
+    x_top = go(out.at[1, top], rx.at[top], 10, by_x)
+    out[2, low] = pair(2, 1).astype(out.dtype)
+    y_low = go(out.at[2, low], ry.at[low], 11, by_y)
+    across_y.wait_recv()
+    out[1, low] = (pair(1, 1) + dy[...].astype(F32)).astype(out.dtype)
+    x_low = go(out.at[1, low], rx.at[low], 12, by_x)
+    across_x.wait_recv()
+    out[2, top] = (pair(2, 0) + dx[...].astype(F32)).astype(out.dtype)
+    y_top = go(out.at[2, top], ry.at[top], 13, by_y)
+    first, second = pair(3, 0), pair(3, 1)
+    x_top.wait_recv()
+    y_top.wait_recv()
+    o_ref[top] = first + rx[top].astype(F32) + ry[top].astype(F32)
+    x_low.wait_recv()
+    y_low.wait_recv()
+    o_ref[low] = second + rx[low].astype(F32) + ry[low].astype(F32)
+    for copy in sends:
+        copy.wait_send()
+
+
+def scatter_tokens(partial_sum, ids):
+    rows, cols = partial_sum.shape[0] // PLANE, partial_sum.shape[1]
+
+    def room(*shape):
+        return pltpu.VMEM(shape, BF)
+
+    return pl.pallas_call(
+        scatter_kernel,
+        out_shape=jax.ShapeDtypeStruct((rows, cols), F32),
+        in_specs=[pl.BlockSpec(memory_space=pl.ANY)],
+        out_specs=pl.BlockSpec(memory_space=pltpu.VMEM),
+        scratch_shapes=[
+            room(4, rows, cols),
+            room(4, rows, cols),
+            room(3, rows, cols),
+            room(rows, cols),
+            room(rows, cols),
+            room(rows // 2, cols),
+            room(rows // 2, cols),
+            pltpu.SemaphoreType.DMA((8,)),
+            pltpu.SemaphoreType.DMA((14,)),
+            pltpu.SemaphoreType.DMA((14,)),
+        ],
+        cost_estimate=lasting(22 if cols > 1024 else 8),
+        compiler_params=pltpu.CompilerParams(
+            collective_id=next(ids), has_side_effects=True, vmem_limit_bytes=40 * 2**20
+        ),
+    )(partial_sum.astype(BF))
+
+
+def row_sum_kernel(x_ref, o_ref, got, send_sem, recv_sem):
+    me = lax.axis_index(CTX)
+    greet([(CTX, (me + j) % PLANE) for j in range(1, PLANE)])
+    copies = []
+    for j in range(1, PLANE):
+        copy = remote(
+            x_ref, got.at[j - 1], send_sem.at[j - 1], recv_sem.at[j - 1], CTX, (me + j) % PLANE
+        )
+        copy.start()
+        copies.append(copy)
+    total = x_ref[...]
+    for j, copy in enumerate(copies):
+        copy.wait_recv()
+        total = total + got[j]
+    o_ref[...] = total
+    for copy in copies:
+        copy.wait_send()
+
+
+def row_sum(rows, ids):
+    tile = rows.reshape(8, -1)
+    total = pl.pallas_call(
+        row_sum_kernel,
+        out_shape=jax.ShapeDtypeStruct(tile.shape, F32),
+        in_specs=[pl.BlockSpec(memory_space=pltpu.VMEM)],
+        out_specs=pl.BlockSpec(memory_space=pltpu.VMEM),
+        scratch_shapes=[
+            pltpu.VMEM((PLANE - 1,) + tile.shape, F32),
+            pltpu.SemaphoreType.DMA((PLANE - 1,)),
+            pltpu.SemaphoreType.DMA((PLANE - 1,)),
+        ],
+        cost_estimate=lasting(5),
+        compiler_params=pltpu.CompilerParams(collective_id=next(ids), has_side_effects=True),
+    )(tile)
+    return total.reshape(rows.shape)
+
+
+def small_gather_kernel(seqs, x_ref, o_ref, own_sem, send_sem, recv_sem):
+    me, mine = lax.axis_index(CTX), lax.axis_index(FSDP)
+    others = [(FSDP, (mine + j) % seqs) for j in range(1, seqs)]
+    greet(others + [(CTX, (me + j) % PLANE) for j in range(1, PLANE)])
+    keep = pltpu.make_async_copy(x_ref, o_ref.at[me, mine], own_sem)
+    keep.start()
+    copies = []
+    for j, (_, other) in enumerate(others):
+        copy = remote(x_ref, o_ref.at[me, mine], send_sem.at[j], recv_sem.at[j], FSDP, other)
+        copy.start()
+        copies.append(copy)
+    keep.wait()
+    for copy in copies:
+        copy.wait_recv()
+    for j in range(1, PLANE):
+        k = seqs + j
+        copy = remote(
+            o_ref.at[me], o_ref.at[me], send_sem.at[k], recv_sem.at[k], CTX, (me + j) % PLANE
+        )
+        copy.start()
+        copies.append(copy)
+    for copy in copies[seqs - 1 :]:
+        copy.wait_recv()
+    for copy in copies:
+        copy.wait_send()
+
+
+def small_gather(tile, seqs, ids):
+    return pl.pallas_call(
+        partial(small_gather_kernel, seqs),
+        out_shape=jax.ShapeDtypeStruct((PLANE, seqs) + tile.shape, tile.dtype),
+        in_specs=[pl.BlockSpec(memory_space=pltpu.VMEM)],
+        out_specs=pl.BlockSpec(memory_space=pltpu.VMEM),
+        scratch_shapes=[
+            pltpu.SemaphoreType.DMA,
+            pltpu.SemaphoreType.DMA((PLANE + seqs,)),
+            pltpu.SemaphoreType.DMA((PLANE + seqs,)),
+        ],
+        cost_estimate=lasting(8),
+        compiler_params=pltpu.CompilerParams(collective_id=next(ids), has_side_effects=True),
+    )(tile)
+
+
+def small_scatter_kernel(seqs, x_ref, o_ref, got, total, late, send_sem, recv_sem):
+    me, mine = lax.axis_index(CTX), lax.axis_index(FSDP)
+    others = [(FSDP, (mine + j) % seqs) for j in range(1, seqs)]
+    greet(others + [(CTX, (me + j) % PLANE) for j in range(1, PLANE)])
+    copies = []
+    for j in range(1, PLANE):
+        to = (me + j) % PLANE
+        copy = remote(x_ref.at[to], got.at[j - 1], send_sem.at[j], recv_sem.at[j], CTX, to)
+        copy.start()
+        copies.append(copy)
+    acc = x_ref[me]
+    for j, copy in enumerate(copies):
+        copy.wait_recv()
+        acc = acc + got[j]
+    total[...] = acc
+    first = len(copies)
+    for j, (_, other) in enumerate(others):
+        k = PLANE + j
+        copy = remote(total.at[other], late.at[j], send_sem.at[k], recv_sem.at[k], FSDP, other)
+        copy.start()
+        copies.append(copy)
+    out = total[mine]
+    for j, copy in enumerate(copies[first:]):
+        copy.wait_recv()
+        out = out + late[j]
+    o_ref[...] = out
+    for copy in copies:
+        copy.wait_send()
+
+
+def small_scatter(tiles, ids):
+    seqs = tiles.shape[1]
+    tile = tiles.shape[2:]
+    return pl.pallas_call(
+        partial(small_scatter_kernel, seqs),
+        out_shape=jax.ShapeDtypeStruct(tile, F32),
+        in_specs=[pl.BlockSpec(memory_space=pltpu.VMEM)],
+        out_specs=pl.BlockSpec(memory_space=pltpu.VMEM),
+        scratch_shapes=[
+            pltpu.VMEM((PLANE - 1,) + tiles.shape[1:], F32),
+            pltpu.VMEM(tiles.shape[1:], F32),
+            pltpu.VMEM((seqs - 1,) + tile, F32),
+            pltpu.SemaphoreType.DMA((PLANE + seqs,)),
+            pltpu.SemaphoreType.DMA((PLANE + seqs,)),
+        ],
+        cost_estimate=lasting(8),
+        compiler_params=pltpu.CompilerParams(collective_id=next(ids), has_side_effects=True),
+    )(tiles)
 
 
 def gather_rows(shard):
@@ -636,6 +958,14 @@
 
 def scatter_rows(partial_sum):
     return lax.psum_scatter(partial_sum.astype(BF), FSDP, scatter_dimension=0, tiled=False)
+
+
+def after(value, *earlier):
+    return lax.optimization_barrier((value, *earlier))[0]
+
+
+def lasting(us):
+    return pl.CostEstimate(flops=int(us * 1e9), bytes_accessed=int(us * 3e6), transcendentals=0)
 
 
 def swap_columns(packed):
@@ -800,6 +1130,8 @@
     taps = CONV - 1
     step_pad = 128 - bc % 128
 
+    ids = itertools.count(1)
+
     small = jnp.concatenate(
         [
             norm_gain,
@@ -810,7 +1142,10 @@
             doc_ids[0].astype(BF),
         ]
     )
-    small = lax.all_gather(small, (CTX, FSDP), axis=0, tiled=False)
+    small_size = small.size
+    tile_rows = -(-small_size // 2048) * 16
+    small = jnp.pad(small, (0, tile_rows * 128 - small_size)).reshape(tile_rows, 128)
+    small = small_gather(small, seqs, ids).reshape(ctx * seqs, -1)
     cuts = []
     at = 0
     for n in (norm_gain.size, ffn_gain.size, mixer_gain.size, conv_bias.size, conv_weight.size, tokens):
@@ -873,12 +1208,18 @@
     conv_cols = conv_pack.shape[2]
     rest_cols = rest_pack.shape[2]
     mixer_pack = swap_columns(jnp.concatenate([conv_pack, rest_pack], axis=2))
-    conv_in_own = gather_rows(mixer_pack[:, :, :conv_cols]).reshape(width, conv_cols)
-    rest_own = gather_rows(mixer_pack[:, :, conv_cols:]).reshape(width, rest_cols)
-    attn_out_own = gather_rows(attn_out_weight).reshape(head, width)
-    mamba_out_own = gather_rows(mamba_out_weight).reshape(inner, width)
-    ffn_own = gather_rows(swap_columns(ffn_pack)).reshape(width, 2 * ff)
-    down_own = gather_rows(down_weight).reshape(ff, width)
+    ffn_pack = swap_columns(after(ffn_pack, mixer_pack))
+    conv_in_own = gather_rows(mixer_pack[:, :, :conv_cols])
+    rest_own = gather_rows(after(mixer_pack[:, :, conv_cols:], conv_in_own))
+    out_own = gather_rows(after(jnp.concatenate([attn_out_weight, mamba_out_weight]), rest_own))
+    ffn_own = gather_rows(after(ffn_pack, out_own))
+    down_own = gather_rows(after(down_weight, ffn_own)).reshape(ff, width)
+    conv_in_own = conv_in_own.reshape(width, conv_cols)
+    rest_own = rest_own.reshape(width, rest_cols)
+    out_rows = attn_out_weight.shape[0]
+    attn_out_own = out_own[:, :out_rows].reshape(head, width)
+    mamba_out_own = out_own[:, out_rows:].reshape(inner, width)
+    ffn_own = ffn_own.reshape(width, 2 * ff)
 
     def to_shards(x):
         return x.reshape(-1, ctx, seqs, krows).transpose(0, 2, 1, 3).reshape(-1, width)
@@ -888,7 +1229,7 @@
 
     resid = hidden_in[0].astype(F32)
     scale_one = lax.rsqrt(jnp.mean(resid * resid, axis=-1, keepdims=True) + EPSILON)
-    normed = gather_tokens(to_shards((resid * scale_one * gain_one).astype(BF)))
+    normed = gather_tokens(to_shards((resid * scale_one * gain_one).astype(BF)), ids)
     conv_all = mm(normed, conv_in_own)
     rest_all = mm(normed, rest_own)
     conv_lin = conv_all[:, : inner + bc].astype(BF).astype(F32)
@@ -907,8 +1248,7 @@
         conv_shift,
     )
     conv_act = conv_act.astype(BF)
-    shared = lax.all_gather(conv_act[:, inner:], CTX, axis=0, tiled=False)
-    shared = shared.transpose(1, 0, 2).reshape(length, 2 * STATE)
+    shared = gather_tokens(conv_act[:, inner:].T, ids, 2).T
     write, read = shared[:, :STATE], shared[:, STATE:]
     xin = conv_act[:, :inner]
 
@@ -939,15 +1279,15 @@
     terms = ssm_terms(step_size, rate, documents, ctx)
     y, saved = ssm_forward(xin, write, read, terms, skip_own)
     gated, gated_back = jax.vjp(lambda a, z: a * jax.nn.silu(z), y, zgate)
-    mean_square = lax.psum(jnp.sum(gated * gated, axis=-1), CTX) / dssm
+    mean_square = row_sum(jnp.sum(gated * gated, axis=-1), ids) / dssm
     scale_mix = lax.rsqrt(mean_square + EPSILON)[:, None]
     ymix = (gated * scale_mix * gain_mix).astype(BF)
 
-    branch = scatter_tokens(mm(attn_low, attn_out_own) + mm(ymix, mamba_out_own))
+    branch = scatter_tokens(mm(attn_low, attn_out_own) + mm(ymix, mamba_out_own), ids)
     mid = resid + branch
     scale_two = lax.rsqrt(jnp.mean(mid * mid, axis=-1, keepdims=True) + EPSILON)
-    normed_two = gather_tokens(to_shards((mid * scale_two * gain_two).astype(BF)))
-    grad_all = gather_tokens(out_grad[0])
+    normed_two = gather_tokens(to_shards((mid * scale_two * gain_two).astype(BF)), ids)
+    grad_all = gather_tokens(out_grad[0], ids)
 
     gate_up = mm(normed_two, ffn_own)
     gate_lin, up_lin = gate_up[:, :ff], gate_up[:, ff:]
@@ -960,11 +1300,11 @@
     ).astype(BF)
     grad_up = (grad_hidden * silu_gate).astype(BF)
     grad_gu = jnp.concatenate([grad_gate, grad_up], axis=1)
-    grad_n2 = from_shards(scatter_tokens(mm_nt(grad_gu, ffn_own)))
-    block_out = (mid + scatter_tokens(mm(hidden, down_own))).astype(BF)
-    down_grad = scatter_rows(mm_tn(hidden, grad_all).reshape(seqs, ff // seqs, width)).astype(F32)
-    ffn_grad = scatter_rows(mm_tn(normed_two, grad_gu).reshape(seqs, ctx, krows, 2 * ff))
-    ffn_grad = swap_columns(ffn_grad).astype(F32)
+    grad_n2 = from_shards(scatter_tokens(mm_nt(grad_gu, ffn_own), ids))
+    block_out = (mid + scatter_tokens(mm(hidden, down_own), ids)).astype(BF)
+    down_grad = scatter_rows(mm_tn(hidden, grad_all).reshape(seqs, ff // seqs, width))
+    ffn_grad = mm_tn(normed_two, grad_gu).reshape(seqs, ctx, krows, 2 * ff).astype(BF)
+    ffn_grad = scatter_rows(after(ffn_grad, down_grad))
 
     turned = grad_n2 * gain_two
     hat_two = mid * scale_two
@@ -972,10 +1312,17 @@
     grad_mid = out_grad[0].astype(F32) + scale_two * (
         turned - hat_two * jnp.mean(turned * hat_two, axis=-1, keepdims=True)
     )
-    branch_grad = gather_tokens(grad_mid.astype(BF))
-
-    attn_out_grad = scatter_rows(mm_tn(attn_low, branch_grad).reshape(seqs, -1, width)).astype(F32)
-    mamba_out_grad = scatter_rows(mm_tn(ymix, branch_grad).reshape(seqs, -1, width)).astype(F32)
+    branch_grad = gather_tokens(grad_mid.astype(BF), ids)
+
+    out_grad_own = jnp.concatenate(
+        [
+            mm_tn(attn_low, branch_grad).reshape(seqs, -1, width),
+            mm_tn(ymix, branch_grad).reshape(seqs, -1, width),
+        ],
+        axis=1,
+    ).astype(BF)
+    out_grad_own = scatter_rows(after(out_grad_own, ffn_grad)).astype(F32)
+    attn_out_grad, mamba_out_grad = out_grad_own[:out_rows], out_grad_own[out_rows:]
     grad_attn = mm_nt(branch_grad, attn_out_own).astype(BF).reshape(length, -1, HEAD_SIZE)
     grad_ymix = mm_nt(branch_grad, mamba_out_own)
 
@@ -995,7 +1342,7 @@
     hat = gated * scale_mix
     turned_mix = grad_ymix * gain_mix
     mixer_gain_grad = jnp.sum(grad_ymix * hat, axis=0)
-    along = lax.psum(jnp.sum(turned_mix * hat, axis=-1), CTX)[:, None] / dssm
+    along = row_sum(jnp.sum(turned_mix * hat, axis=-1), ids)[:, None] / dssm
     grad_gated = scale_mix * (turned_mix - hat * along)
     grad_y, grad_zgate = gated_back(grad_gated)
 
@@ -1003,9 +1350,7 @@
         grad_y, xin, write, read, terms, skip_own, rate, saved
     )
     grad_shared = jnp.concatenate([grad_write, grad_read], axis=1).astype(BF)
-    grad_shared = lax.psum_scatter(
-        grad_shared.reshape(length, ctx, bc).transpose(1, 0, 2), CTX, scatter_dimension=0
-    ).astype(F32)
+    grad_shared = scatter_tokens(grad_shared.T, ids).T
     grad_widened, taps_grad, shift_grad = conv_back(
         jnp.concatenate([grad_xin, grad_shared], axis=1)
     )
@@ -1023,10 +1368,13 @@
     )
 
     grad_normed = from_shards(
-        scatter_tokens(mm_nt(grad_conv, conv_in_own) + mm_nt(grad_rest, rest_own))
-    )
-    conv_grad = scatter_rows(mm_tn(normed, grad_conv).reshape(seqs, ctx, krows, conv_cols))
-    rest_grad = scatter_rows(mm_tn(normed, grad_rest).reshape(seqs, ctx, krows, rest_cols))
+        scatter_tokens(mm_nt(grad_conv, conv_in_own) + mm_nt(grad_rest, rest_own), ids)
+    )
+    rest_grad = mm_tn(normed, grad_rest).reshape(seqs, ctx, krows, rest_cols).astype(BF)
+    rest_grad = scatter_rows(after(rest_grad, out_grad_own))
+    conv_grad = mm_tn(normed, grad_conv).reshape(seqs, ctx, krows, conv_cols).astype(BF)
+    conv_grad = scatter_rows(after(conv_grad, rest_grad))
+    ffn_grad = swap_columns(ffn_grad).astype(F32)
     mixer_grad = swap_columns(jnp.concatenate([conv_grad, rest_grad], axis=2)).astype(F32)
     turned_one = grad_normed * gain_one
     hat_one = resid * scale_one
@@ -1056,17 +1404,23 @@
         spread_out(log_decay_grad, me * heads, HS),
         spread_out(skip_grad, me * heads, HS),
     )
-    sums = lax.psum(jnp.concatenate(parts), (CTX, FSDP))
+    place = (ctx, seqs)
+    tiles = [part.reshape(place + (-1,)) for part in parts[:4]]
+    tiles.append(parts[4].reshape((CONV,) + place + (-1,)).transpose(1, 2, 0, 3).reshape(place + (-1,)))
+    tiles.append(
+        jnp.broadcast_to(jnp.concatenate(parts[5:]), place + (3 * HS,))
+    )
+    sizes = [tile.shape[-1] for tile in tiles]
+    tile_rows = -(-sum(sizes) // 1024) * 8
+    tiles = jnp.concatenate(tiles, axis=-1)
+    tiles = jnp.pad(tiles, ((0, 0), (0, 0), (0, tile_rows * 128 - sum(sizes))))
+    sums = small_scatter(tiles.reshape(place + (tile_rows, 128)), ids).reshape(-1)
     pieces = []
     at = 0
-    for part in parts:
-        pieces.append(sums[at : at + part.size])
-        at += part.size
-    place = me * seqs + mine
-
-    def own_piece(full):
-        n = full.shape[-1] // (ctx * seqs)
-        return lax.dynamic_slice_in_dim(full, place * n, n, full.ndim - 1)
+    for size in sizes:
+        pieces.append(sums[at : at + size])
+        at += size
+    per_head = pieces[5].reshape(3, HS)
 
     def by_row(packed, start, n):
         return packed[:, :, start : start + n].transpose(1, 0, 2).reshape(krows, -1)
@@ -1086,7 +1440,7 @@
     return (
         block_out[None],
         input_grad[None],
-        own_piece(pieces[0]),
+        pieces[0],
         by_row(mixer_grad, base, head),
         over_queries(key_grad),
         over_queries(value_grad),
@@ -1096,17 +1450,17 @@
             [by_row(mixer_grad, 0, inner), by_row(mixer_grad, inner, bc)], axis=1
         ),
         by_row(mixer_grad, inner + bc, heads),
-        own_piece(pieces[4].reshape(CONV, -1)),
-        own_piece(pieces[3]),
-        pieces[5],
-        pieces[6],
-        pieces[7],
-        own_piece(pieces[2]),
+        pieces[4].reshape(CONV, -1),
+        pieces[3],
+        per_head[0],
+        per_head[1],
+        per_head[2],
+        pieces[2],
         mamba_out_grad,
-        own_piece(pieces[1]),
+        pieces[1],
         by_row(ffn_grad, 0, ff),
         by_row(ffn_grad, ff, ff),
-        down_grad,
+        down_grad.astype(F32),
     )
 
 
@@ -1136,7 +1490,7 @@
         P((CTX, FSDP), None),
     )
     ctx = mesh.shape[CTX]
-    whole_heads = QUERY_HEADS % ctx == 0 and HS % ctx == 0 and ctx % KEY_VALUE_HEADS == 0
+    whole_heads = ctx == PLANE and QUERY_HEADS % ctx == 0 and HS % ctx == 0
     return jax.shard_map(
         head_parallel if whole_heads else on_device,
         mesh=mesh,

time: 1290 us -> 696 us (0.54)
  waiting for transfers between devices: 809 us -> 115 us
  Pallas kernels: 0 us -> 238 us
  blocking collectives: 135 us -> 41.6 us
  matrix products: 136 us -> 121 us
    pallas_call x0 -> x14, Pallas kernels: none -> 238 us  [the longest x5 106 us: scatter_tokens(): pl.pallas_call(scatter_kernel, out_shape=jax.ShapeDtypeStruct((rows, cols...]
    reduce_scatter x5 -> x0, waiting for transfers between devices: 161 us -> none  [the longest x4 161 us: scatter_tokens(): lax.psum_scatter(partial_sum.astype(BF), CTX, scatter_dimension=0, tiled=...]
    all_gather x5 -> x0, waiting for transfers between devices: 158 us -> none  [the longest x4 150 us: gather_tokens(): return lax.all_gather(block, CTX, axis=0, tiled=True)]
    reduce_scatter x6 -> x5, waiting for transfers between devices: 218 us -> 88.9 us  [scatter_rows(): lax.psum_scatter(partial_sum.astype(BF), FSDP, scatter_dimension=0, tiled...]
    psum x1 -> x0, waiting for transfers between devices: 124 us -> none  [head_parallel(): sums = lax.psum(jnp.concatenate(parts), (CTX, FSDP))]
    all_gather x5, waiting for transfers between devices: 146 us -> 25.5 us  [gather_rows(): return lax.all_gather(shard, FSDP, axis=0, tiled=False)]
    unnamed x1 -> x0, blocking collectives: 42.4 us -> none
    psum x2 -> x0, blocking collectives: 26.9 us -> none  [the longest x1 13.9 us: head_parallel(): mean_square = lax.psum(jnp.sum(gated * gated, axis=-1), CTX) / dssm]
  transfers between devices with their start and end apart: 24 -> 12, of which waited for: 20 -> 4; matrix products, arithmetic and copies ran while one was open for 15% -> 28% of each run, Pallas kernels for 0% -> 27%
where the time goes in v2:
time: 696 us; the launch traced here: 687 us
  Pallas kernels  238 us (34%)
  matrix products  121 us (17%)
  waiting for transfers between devices  115 us (17%)
  local copies, waits for them, and re-layouts  82.9 us (12%)
  other arithmetic  60.7 us (9%)
  blocking collectives  41.6 us (6%)
  between operations  17.5 us (3%)
  starting transfers between devices  9.2 us (1%)
    pallas_call x5, Pallas kernels, scatter_tokens(): pl.pallas_call(scatter_kernel, out_shape=jax.ShapeDtypeStruct((rows, cols...  106 us
    pallas_call x5, Pallas kernels, gather_tokens(): pl.pallas_call(partial(gather_kernel, pieces), out_shape=jax.ShapeDtypeSt...  98.3 us
    reduce_scatter x5, waiting for transfers between devices, scatter_rows(): lax.psum_scatter(partial_sum.astype(BF), FSDP, scatter_dimension=0, tiled...  88.9 us
    dot_general x18, matrix products, dotf(): lax.dot_general(left, right, (dims, ((), ())), preferred_element_type=F32)  88 us
    all_to_all x2, blocking collectives, swap_columns(): return lax.all_to_all(packed, CTX, split_axis=0, concat_axis=0, tiled=True)  41.6 us
    all_gather x5, waiting for transfers between devices, gather_rows(): return lax.all_gather(shard, FSDP, axis=0, tiled=False)  25.5 us
    unnamed x350, local copies, waits for them, and re-layouts  25.1 us
  transfers between devices with their start and end apart: 12, of which 4 were waited for; matrix products, arithmetic and copies ran while one was open for 28% of the time, Pallas kernels for 27%

profile of v2, /device:TPU:0, one launch (start us, length us, event | category | flops | bytes accessed | tf_op | source)
XLA Modules:
  0.0 686.6 jit_solution(889918407486147623)
XLA Ops:
  12.2 2.1 concatenate.92
  14.5 23.1 %all_to_all.20 = bf16[8,64,1280]{2,1,0:T(8,128)(2,1)S(1)} all-to-all(bf16[8,64,1280]{2,1,0:T(8,128)(2,1)S(1)} %copy.487), channel_id=1, replica_groups=mesh['ctx'=8,'fsdp'=4] {'ctx'}, dimensions={0} | all-to-all | bytes 2621440 | tf_op jit(solution)/shard_map/all_to_all | solution.py:972
  40.8 18.5 %all_to_all.21 = bf16[8,64,1024]{2,1,0:T(8,128)(2,1)} all-to-all(bf16[8,64,1024]{2,1,0:T(8,128)(2,1)S(1)} %copy.506), channel_id=1, replica_groups=mesh['ctx'=8,'fsdp'=4] {'ctx'}, dimensions={0} | all-to-all | bytes 2097152 | tf_op jit(solution)/shard_map/all_to_all | solution.py:972
  61.3 11.5 %shard_map.373 = bf16[8,4,16,128]{3,2,1,0:T(8,128)(2,1)} custom-call(bf16[16,128]{1,0:T(8,128)(2,1)} %pad_bitcast_fusion.1.x_ref), custom_call_target="tpu_custom_call" | custom-call | flops 8000000000 | bytes 24000000 | tf_op jit(solution)/shard_map/pallas_call | solution.py:890
  79.8 2.0 copy.485.x_ref
  81.8 22.2 %shard_map.374 = bf16[1024,2048]{1,0:T(8,128)(2,1)} custom-call(bf16[128,2048]{1,0:T(8,128)(2,1)} %copy.485.x_ref), custom_call_target="tpu_custom_call" | custom-call | flops 22000001024 | bytes 66000000 | tf_op jit(solution)/shard_map/pallas_call | solution.py:714
  104.0 22.3 %shard_map.380 = bf16[1024,2048]{1,0:T(8,128)(2,1)} custom-call(bf16[128,2048]{1,0:T(8,128)(2,1)} %bitcast.479), custom_call_target="tpu_custom_call" | custom-call | flops 22000001024 | bytes 66000000 | tf_op jit(solution)/shard_map/pallas_call | solution.py:714
  128.7 2.8 slice.438
  131.5 5.3 fusion.158
  142.1 3.2 multiply_convert_fusion.4
  148.1 10.2 %shard_map.375 = bf16[512,1024]{1,0:T(8,128)(2,1)} custom-call(bf16[64,1024]{1,0:T(8,128)(2,1)} %slice_bitcast_fusion.14.x_ref), custom_call_target="tpu_custom_call" | custom-call | flops 8000000000 | bytes 24000000 | tf_op jit(solution)/shard_map/pallas_call | solution.py:714
  158.4 2.1 slice_bitcast_fusion.6
  161.3 2.1 copy.492
  163.4 2.1 copy.554
  167.5 2.1 copy.491
  169.6 2.1 copy.555
  181.2 6.8 fusion.157
  190.4 6.1 shard_map.376
  202.0 2.4 fusion.35
  205.9 2.7 add_convert_fusion.1.p_ref
  208.6 29.3 %shard_map.377 = f32[128,2048]{1,0:T(8,128)S(1)} custom-call(bf16[1024,2048]{1,0:T(8,128)(2,1)S(1)} %add_convert_fusion.1.p_ref), custom_call_target="tpu_custom_call" | custom-call | flops 22000001024 | bytes 66000000 | tf_op jit(solution)/shard_map/pallas_call | solution.py:801
  239.7 21.7 %shard_map.378 = bf16[1024,2048]{1,0:T(8,128)(2,1)} custom-call(bf16[128,2048]{1,0:T(8,128)(2,1)} %copy.505.x_ref), custom_call_target="tpu_custom_call" | custom-call | flops 22000001024 | bytes 66000000 | tf_op jit(solution)/shard_map/pallas_call | solution.py:714
  261.4 10.0 %fusion.160 = f32[1024,1024]{0,1:T(8,128)} fusion(bf16[1024,2048]{1,0:T(8,128)(2,1)} %shard_map.378, bf16[2048,1024]{1,0:T(8,128)(2,1)} %bitcast.564), kind=kOutput, calls=%fused_computation.357 | convolution fusion | flops 4294967296 | bytes 12582912 | tf_op jit(solution)/shard_map/dot_general | solution.py:611
  271.4 25.5 %all-gather.19.cloned.1.call-done = bf16[512,2048]{1,0:T(8,128)(2,1)} async-done(((bf16[128,2048]{1,0:T(8,128)(2,1)}), bf16[512,2048]{1,0:T(8,128)(2,1)}) %all-gather.19.cloned.1.call-update) | async-done | bytes 2097168 | tf_op jit(solution)/shard_map/all_gather | solution.py:956
  296.9 8.1 %multiply_convert_fusion.2 = (bf16[1024,512]{0,1:T(8,128)(2,1)S(1)}, bf16[1024,512]{0,1:T(8,128)(2,1)S(1)}, bf16[1024,512]{0,1:T(8,128)(2,1)}) fusion(f32[1024,1024]{0,1:T(8,128)} %fusion.160, bf16[1024,2048]{1,0:T(8,128)(2,1)} %shard_map.380, bf16[512,2048]{1,0:T(8,128)(2,1)} %all-gather.19.cloned.1.call-done), kind=kOutput, calls=%fused_computation.45 | convolution fusion | flops 2154823680 | bytes 13631488 | tf_op jit(solution)/shard_map/dot_general | solution.py:611
  306.0 4.8 convolution_convert_fusion.2.p_ref
  310.8 22.6 %shard_map.381 = f32[128,2048]{1,0:T(8,128)S(1)} custom-call(bf16[1024,2048]{1,0:T(8,128)(2,1)S(1)} %convolution_convert_fusion.2.p_ref), custom_call_target="tpu_custom_call" | custom-call | flops 22000001024 | bytes 66000000 | tf_op jit(solution)/shard_map/pallas_call | solution.py:801
  338.6 21.9 %shard_map.382 = bf16[1024,2048]{1,0:T(8,128)(2,1)} custom-call(bf16[128,2048]{1,0:T(8,128)(2,1)} %fusion.149.x_ref), custom_call_target="tpu_custom_call" | custom-call | flops 22000001024 | bytes 66000000 | tf_op jit(solution)/shard_map/pallas_call | solution.py:714
  360.5 3.6 convolution_convert_fusion.7
  364.4 5.4 multiply_reduce_fusion.9
  369.8 3.0 fusion.38
  372.8 3.3 fusion.2
  376.2 2.4 fusion.13
  381.6 6.1 shard_map.383
  388.4 4.7 multiply_reduce_fusion.8
  393.1 2.3 fusion.100
  395.6 5.0 convolution_convert_fusion.3
  401.8 9.2 %convolution_convert_fusion.1 = bf16[2048,1024]{1,0:T(8,128)(2,1)} fusion(bf16[1024,2048]{1,0:T(8,128)(2,1)} %shard_map.378, bf16[1024,512]{0,1:T(8,128)(2,1)} %copy-done.159, bf16[1024,512]{0,1:T(8,128)(2,1)S(1)} %copy-done.158), kind=kOutput, calls=%fused_computation.14 | convolution fusion | flops 4301258752 | bytes 10485760 | tf_op jit(solution)/shard_map/dot_general | solution.py:611
  414.4 2.1 convolution_bitcast_fusion
  416.7 3.9 multiply_reduce_fusion.3
  423.7 2.1 fusion.108
  428.6 3.0 fusion.25
  437.5 2.1 copy.571
  445.8 9.7 %shard_map.384 = f32[64,1024]{1,0:T(8,128)S(1)} custom-call(bf16[512,1024]{1,0:T(8,128)(2,1)S(1)} %maximum_bitcast_fusion.p_ref), custom_call_target="tpu_custom_call" | custom-call | flops 8000000000 | bytes 24000000 | tf_op jit(solution)/shard_map/pallas_call | solution.py:801
  455.6 3.9 multiply_reduce_fusion.6
  462.7 3.8 convolution_convert_fusion.5
  466.9 6.1 fusion.91
  473.0 2.4 add_convert_fusion.p_ref
  475.5 21.6 %shard_map.385 = f32[128,2048]{1,0:T(8,128)S(1)} custom-call(bf16[1024,2048]{1,0:T(8,128)(2,1)S(1)} %add_convert_fusion.p_ref), custom_call_target="tpu_custom_call" | custom-call | flops 22000001024 | bytes 66000000 | tf_op jit(solution)/shard_map/pallas_call | solution.py:801
  499.1 6.3 convolution_convert_fusion.4
  508.5 3.1 fusion.8
  516.9 2.4 convolution_convert_fusion.p_ref
  519.3 22.3 %shard_map.379 = f32[128,2048]{1,0:T(8,128)S(1)} custom-call(bf16[1024,2048]{1,0:T(8,128)(2,1)S(1)} %convolution_convert_fusion.p_ref), custom_call_target="tpu_custom_call" | custom-call | flops 22000001024 | bytes 66000000 | tf_op jit(solution)/shard_map/pallas_call | solution.py:801
  541.7 10.5 %shard_map.386 = f32[8,128]{1,0:T(8,128)} custom-call(f32[8,4,8,128]{3,2,1,0:T(8,128)} %copy.575.x_ref), custom_call_target="tpu_custom_call" | custom-call | flops 8000000000 | bytes 24000000 | tf_op jit(solution)/shard_map/pallas_call | solution.py:938
  552.2 4.3 all-to-all-start.3
  556.6 2.5 copy.533
  560.2 2.5 copy.534
  563.4 3.0 fusion.64
  566.4 18.9 %reduce-scatter.8.cloned.1.call-done = bf16[1,8,64,512]{3,2,1,0:T(8,128)(2,1)} async-done(((bf16[4,8,64,512]{3,2,1,0:T(8,128)(2,1)}), bf16[1,8,64,512]{3,2,1,0:T(8,128)(2,1)}) %reduce-scatter.8.cloned.1.call-update) | async-done | bytes 524304 | tf_op jit(solution)/shard_map/reduce_scatter | solution.py:960
  585.3 2.4 pad_maximum_fusion.6
  587.8 4.3 all-to-all-start.2
  593.2 37.8 %reduce-scatter.10.cloned.1.call-done = bf16[1,128,2048]{2,1,0:T(8,128)(2,1)} async-done(((bf16[4,128,2048]{2,1,0:T(8,128)(2,1)}), bf16[1,128,2048]{2,1,0:T(8,128)(2,1)}) %reduce-scatter.10.cloned.1.call-update) | async-done | bytes 524304 | tf_op jit(solution)/shard_map/reduce_scatter | solution.py:960
  631.0 2.1 bitcast_convert_fusion
  644.3 32.2 %reduce-scatter.14.cloned.1.call-done = bf16[1,128,2048]{2,1,0:T(8,128)(2,1)} async-done(((bf16[4,128,2048]{2,1,0:T(8,128)(2,1)}), bf16[1,128,2048]{2,1,0:T(8,128)(2,1)}) %reduce-scatter.14.cloned.1.call-update) | async-done | bytes 524304 | tf_op jit(solution)/shard_map/reduce_scatter | solution.py:960
  (579 shorter events, 113.4 us)
Async XLA Ops:
  7.2 52.1 %all-gather.15.cloned.1.call-start = ((), (), s32[]{:S(2)}) async-start(), calls=%async_computation.16 | async-start | bytes 2621440 | tf_op jit(solution)/shard_map/all_gather | solution.py:956
  9.2 122.2 %all-gather.11.cloned.1.call-start = ((), (), s32[]{:S(2)}) async-start(), calls=%async_computation.14 | async-start | bytes 2621440 | tf_op jit(solution)/shard_map/all_gather | solution.py:956
  38.5 142.6 %all-gather.13.cloned.1.call-start = ((), (), s32[]{:S(2)}) async-start(), calls=%async_computation.15 | async-start | bytes 3932160 | tf_op jit(solution)/shard_map/all_gather | solution.py:956
  39.6 221.8 %all-gather.17.cloned.1.call-start = ((), (), s32[]{:S(2)}) async-start(), calls=%async_computation.17 | async-start | bytes 5242880 | tf_op jit(solution)/shard_map/all_gather | solution.py:956
  40.1 20.4 %copy-start.149 = (s32[1,128]{1,0:T(1,128)S(1)}, s32[1,128]{1,0:T(1,128)}, u32[]{:S(2)}) copy-start(s32[1,128]{1,0:T(1,128)} %param.26) | copy-start | bytes 1540
  40.1 20.4 %copy-start.139 = (bf16[4,112]{1,0:T(4,128)(2,1)S(1)}, bf16[4,112]{1,0:T(4,128)(2,1)}, u32[]{:S(2)}) copy-start(bf16[4,112]{1,0:T(4,128)(2,1)} %param.35) | copy-start | bytes 2692
  40.2 20.5 %copy-start.142 = (bf16[64]{0:T(256)(128)(2,1)S(1)}, bf16[64]{0:T(256)(128)(2,1)}, u32[]{:S(2)}) copy-start(bf16[64]{0:T(256)(128)(2,1)} %param.27) | copy-start | bytes 388
  40.2 20.5 %copy-start.143 = (bf16[64]{0:T(256)(128)(2,1)S(1)}, bf16[64]{0:T(256)(128)(2,1)}, u32[]{:S(2)}) copy-start(bf16[64]{0:T(256)(128)(2,1)} %param.42) | copy-start | bytes 388
  40.2 20.4 %copy-start.144 = (bf16[96]{0:T(256)(128)(2,1)S(1)}, bf16[96]{0:T(256)(128)(2,1)}, u32[]{:S(2)}) copy-start(bf16[96]{0:T(256)(128)(2,1)} %param.40) | copy-start | bytes 580
  40.2 20.4 %copy-start.145 = (bf16[112]{0:T(256)(128)(2,1)S(1)}, bf16[112]{0:T(256)(128)(2,1)}, u32[]{:S(2)}) copy-start(bf16[112]{0:T(256)(128)(2,1)} %param.36) | copy-start | bytes 676
  59.3 237.6 %all-gather.19.cloned.1.call-start = ((), (), s32[]{:S(2)}) async-start(), calls=%async_computation.18 | async-start | bytes 2621440 | tf_op jit(solution)/shard_map/all_gather | solution.py:956
  59.9 406.6 %reduce-scatter.6.cloned.1.call-start = ((), (), s32[]{:S(2)}) async-start(), calls=%async_computation.9 | async-start | bytes 3932160 | tf_op jit(solution)/shard_map/reduce_scatter | solution.py:960
  60.5 136.7 %copy-start.85 = (f32[1024]{0:T(1024)}, f32[1024]{0:T(1024)S(1)}, u32[]{:S(2)}) copy-start(f32[1024]{0:T(1024)S(1)} %iota_convert_fusion) | copy-start | bytes 12292
  61.3 13.8 %copy-start.24 = (bf16[1,128,2048]{2,1,0:T(8,128)(2,1)S(1)}, bf16[1,128,2048]{2,1,0:T(8,128)(2,1)}, u32[]{:S(2)}) copy-start(bf16[1,128,2048]{2,1,0:T(8,128)(2,1)} %param.24) | copy-start | bytes 1572868
  76.6 60.2 %copy-start.133 = (f32[6]{0:T(128)}, f32[6]{0:T(128)S(1)}, u32[]{:S(2)}) copy-start(f32[6]{0:T(128)S(1)} %dynamic_slice.33) | copy-start | bytes 76
  76.7 100.8 %copy-start.152 = (f32[6]{0:T(128)}, f32[6]{0:T(128)S(1)}, u32[]{:S(2)}) copy-start(f32[6]{0:T(128)S(1)} %dynamic_slice.35) | copy-start | bytes 76
  76.7 61.5 %copy-start.137 = (f32[6]{0:T(128)}, f32[6]{0:T(128)S(1)}, u32[]{:S(2)}) copy-start(f32[6]{0:T(128)S(1)} %exponential_negate_fusion) | copy-start | bytes 76
  76.8 27.3 %copy-start.131 = (f32[128]{0:T(128)}, f32[128]{0:T(128)S(1)}, u32[]{:S(2)}) copy-start(f32[128]{0:T(128)S(1)} %add_rsqrt_fusion.1) | copy-start | bytes 1540
  76.9 65.1 %copy-start.103 = (pred[1024]{0:T(1024)(128)(4,1)}, pred[1024]{0:T(1024)(128)(4,1)S(1)}, u32[]{:S(2)}) copy-start(pred[1024]{0:T(1024)(128)(4,1)S(1)} %get-tuple-element.229) | copy-start | bytes 3076
  76.9 65.1 %copy-start.105 = (pred[1024]{0:T(1024)(128)(4,1)}, pred[1024]{0:T(1024)(128)(4,1)S(1)}, u32[]{:S(2)}) copy-start(pred[1024]{0:T(1024)(128)(4,1)S(1)} %get-tuple-element.230) | copy-start | bytes 3076
  76.9 65.1 %copy-start.107 = (pred[1024]{0:T(1024)(128)(4,1)}, pred[1024]{0:T(1024)(128)(4,1)S(1)}, u32[]{:S(2)}) copy-start(pred[1024]{0:T(1024)(128)(4,1)S(1)} %get-tuple-element.231) | copy-start | bytes 3076
  77.0 260.4 %copy-start.77 = (f32[2048]{0:T(1024)}, f32[2048]{0:T(1024)S(1)}, u32[]{:S(2)}) copy-start(f32[2048]{0:T(1024)S(1)} %reshape.833) | copy-start | bytes 24580
  77.0 65.0 %copy-start.95 = (f32[1,448]{1,0:T(1,128)}, f32[1,448]{1,0:T(1,128)S(1)}, u32[]{:S(2)}) copy-start(f32[1,448]{1,0:T(1,128)S(1)} %get-tuple-element.204) | copy-start | bytes 5380
  77.0 65.0 %copy-start.97 = (f32[1,448]{1,0:T(1,128)}, f32[1,448]{1,0:T(1,128)S(1)}, u32[]{:S(2)}) copy-start(f32[1,448]{1,0:T(1,128)S(1)} %get-tuple-element.205) | copy-start | bytes 5380
  77.1 65.0 %copy-start.99 = (f32[1,448]{1,0:T(1,128)}, f32[1,448]{1,0:T(1,128)S(1)}, u32[]{:S(2)}) copy-start(f32[1,448]{1,0:T(1,128)S(1)} %get-tuple-element.206) | copy-start | bytes 5380
  77.1 65.0 %copy-start.101 = (f32[1,448]{1,0:T(1,128)}, f32[1,448]{1,0:T(1,128)S(1)}, u32[]{:S(2)}) copy-start(f32[1,448]{1,0:T(1,128)S(1)} %get-tuple-element.207) | copy-start | bytes 5380
  77.3 100.2 %copy-start.79 = (pred[8,128,128]{2,1,0:T(8,128)(4,1)}, pred[8,128,128]{2,1,0:T(8,128)(4,1)S(1)}, u32[]{:S(2)}) copy-start(pred[8,128,128]{2,1,0:T(8,128)(4,1)S(1)} %compare_and_fusion) | copy-start | bytes 393220
  126.6 20.2 %copy-start.109 = (pred[8,128]{1,0:T(8,128)(4,1)}, pred[8,128]{1,0:T(8,128)(4,1)S(1)}, u32[]{:S(2)}) copy-start(pred[8,128]{1,0:T(8,128)(4,1)S(1)} %get-tuple-element.240) | copy-start | bytes 3076
  126.6 20.4 %copy-start.111 = (pred[8,128]{1,0:T(8,128)(4,1)}, pred[8,128]{1,0:T(8,128)(4,1)S(1)}, u32[]{:S(2)}) copy-start(pred[8,128]{1,0:T(8,128)(4,1)S(1)} %get-tuple-element.239) | copy-start | bytes 3076
  126.8 19.3 %copy-start.128 = (f32[8]{0:T(128)}, f32[8]{0:T(128)S(1)}, u32[]{:S(2)}) copy-start(f32[8]{0:T(128)S(1)} %convert_reduce_fusion) | copy-start | bytes 100
  138.3 8.7 %copy-start.65 = (f32[8,6,128]{2,0,1:T(8,128)}, f32[8,6,128]{2,0,1:T(8,128)S(1)}, u32[]{:S(2)}) copy-start(f32[8,6,128]{2,0,1:T(8,128)S(1)} %get-tuple-element.169) | copy-start | bytes 73732
  140.4 37.1 %copy-start.88 = (f32[8,6,128]{2,1,0:T(8,128)}, f32[8,6,128]{2,1,0:T(8,128)S(1)}, u32[]{:S(2)}) copy-start(f32[8,6,128]{2,1,0:T(8,128)S(1)} %copy.489) | copy-start | bytes 73732
  146.8 28.6 %copy-start.126 = (f32[6]{0:T(128)}, f32[6]{0:T(128)S(1)}, u32[]{:S(2)}) copy-start(f32[6]{0:T(128)S(1)} %get-tuple-element.223) | copy-start | bytes 76
  146.8 28.8 %copy-start.115 = (f32[6]{0:T(128)}, f32[6]{0:T(128)S(1)}, u32[]{:S(2)}) copy-start(f32[6]{0:T(128)S(1)} %get-tuple-element.221) | copy-start | bytes 76
  146.8 28.8 %copy-start.119 = (f32[6]{0:T(128)}, f32[6]{0:T(128)S(1)}, u32[]{:S(2)}) copy-start(f32[6]{0:T(128)S(1)} %get-tuple-element.222) | copy-start | bytes 76
  146.8 29.1 %copy-start.113 = (f32[6]{0:T(128)}, f32[6]{0:T(128)S(1)}, u32[]{:S(2)}) copy-start(f32[6]{0:T(128)S(1)} %get-tuple-element.219) | copy-start | bytes 76
  146.8 29.1 %copy-start.117 = (f32[6]{0:T(128)}, f32[6]{0:T(128)S(1)}, u32[]{:S(2)}) copy-start(f32[6]{0:T(128)S(1)} %get-tuple-element.220) | copy-start | bytes 76
  146.8 29.3 %copy-start.124 = (f32[6]{0:T(128)}, f32[6]{0:T(128)S(1)}, u32[]{:S(2)}) copy-start(f32[6]{0:T(128)S(1)} %get-tuple-element.218) | copy-start | bytes 76
  147.0 26.3 %copy-start.67 = (f32[8,128,6]{1,2,0:T(8,128)}, f32[8,128,6]{1,2,0:T(8,128)S(1)}, u32[]{:S(2)}) copy-start(f32[8,128,6]{1,2,0:T(8,128)S(1)} %copy.498) | copy-start | bytes 73732
  147.0 30.5 %copy-start.69 = (f32[8,128,6]{1,2,0:T(8,128)}, f32[8,128,6]{1,2,0:T(8,128)S(1)}, u32[]{:S(2)}) copy-start(f32[8,128,6]{1,2,0:T(8,128)S(1)} %copy.501) | copy-start | bytes 73732
  147.1 30.4 %copy-start.91 = (f32[8,6,128]{2,1,0:T(8,128)}, f32[8,6,128]{2,1,0:T(8,128)S(1)}, u32[]{:S(2)}) copy-start(f32[8,6,128]{2,1,0:T(8,128)S(1)} %copy.493) | copy-start | bytes 73732
  181.1 8.0 %copy-start.17 = (f32[8,128,6,64]{1,0,3,2:T(8,128)}, f32[8,128,6,64]{1,0,3,2:T(8,128)S(1)}, u32[]{:S(2)}) copy-start(f32[8,128,6,64]{1,0,3,2:T(8,128)S(1)} %copy.502) | copy-start | bytes 4718596
  190.4 15.3 %copy-start.14 = (f32[1024,384]{0,1:T(8,128)}, f32[1024,384]{0,1:T(8,128)S(1)}, u32[]{:S(2)}) copy-start(f32[1024,384]{0,1:T(8,128)S(1)} %get-tuple-element.161) | copy-start | bytes 4718596
  208.6 29.3 %copy-start.25 = (bf16[1,128,2048]{2,1,0:T(8,128)(2,1)S(1)}, bf16[1,128,2048]{2,1,0:T(8,128)(2,1)}, u32[]{:S(2)}) copy-start(bf16[1,128,2048]{2,1,0:T(8,128)(2,1)} %param.24) | copy-start | bytes 1572868
  238.2 99.3 %copy-start.4 = (f32[128,2048]{1,0:T(8,128)}, f32[128,2048]{1,0:T(8,128)S(1)}, u32[]{:S(2)}) copy-start(f32[128,2048]{1,0:T(8,128)S(1)} %get-tuple-element.159) | copy-start | bytes 3145732
  238.2 99.2 %copy-start.121 = (f32[128]{0:T(128)}, f32[128]{0:T(128)S(1)}, u32[]{:S(2)}) copy-start(f32[128]{0:T(128)S(1)} %add_rsqrt_fusion) | copy-start | bytes 1540
  296.9 9.1 %copy-start.146 = (bf16[32,64,1024]{2,1,0:T(8,128)(2,1)S(1)}, bf16[32,64,1024]{2,1,0:T(8,128)(2,1)}, u32[]{:S(2)}) copy-start(bf16[32,64,1024]{2,1,0:T(8,128)(2,1)} %all-gather.17.cloned.1.call-done) | copy-start | bytes 12582916
  337.4 23.1 %copy-start.135 = (f32[128]{0:T(128)}, f32[128]{0:T(128)S(1)}, u32[]{:S(2)}) copy-start(f32[128]{0:T(128)S(1)} %broadcast_multiply_fusion.3) | copy-start | bytes 1540
  338.6 21.9 %copy-start.38 = (bf16[4,32,2048]{2,1,0:T(8,128)(2,1)S(1)}, bf16[4,32,2048]{2,1,0:T(8,128)(2,1)}, u32[]{:S(2)}) copy-start(bf16[4,32,2048]{2,1,0:T(8,128)(2,1)} %slice.414) | copy-start | bytes 1572868
  393.1 7.5 %copy-start.49 = (bf16[1024,384]{0,1:T(8,128)(2,1)}, bf16[1024,384]{0,1:T(8,128)(2,1)S(1)}, u32[]{:S(2)}) copy-start(bf16[1024,384]{0,1:T(8,128)(2,1)S(1)} %get-tuple-element.172) | copy-start | bytes 2359300
  400.6 141.0 %reduce-scatter.12.cloned.1.call-start = ((), (), s32[]{:S(2)}) async-start(), calls=%async_computation.12 | async-start | bytes 5242880 | tf_op jit(solution)/shard_map/reduce_scatter | solution.py:960
  401.8 9.2 %copy-start.31 = (f32[1024,384]{0,1:T(8,128)S(1)}, f32[1024,384]{0,1:T(8,128)}, u32[]{:S(2)}) copy-start(f32[1024,384]{0,1:T(8,128)} %get-tuple-element.152) | copy-start | bytes 4718596
  412.5 172.8 %reduce-scatter.8.cloned.1.call-start = ((), (), s32[]{:S(2)}) async-start(), calls=%async_computation.10 | async-start | bytes 2621440 | tf_op jit(solution)/shard_map/reduce_scatter | solution.py:960
  445.8 9.7 %copy-start.13 = (f32[1024,448]{0,1:T(8,128)S(1)}, f32[1024,448]{0,1:T(8,128)}, u32[]{:S(2)}) copy-start(f32[1024,448]{0,1:T(8,128)} %copy-done.12) | copy-start | bytes 5505028
  445.8 9.7 %copy-start.27 = (f32[1024,448]{0,1:T(8,128)S(1)}, f32[1024,448]{0,1:T(8,128)}, u32[]{:S(2)}) copy-start(f32[1024,448]{0,1:T(8,128)} %get-tuple-element.171) | copy-start | bytes 5505028
  445.8 9.7 %copy-start.104 = (pred[1024]{0:T(1024)(128)(4,1)S(1)}, pred[1024]{0:T(1024)(128)(4,1)}, u32[]{:S(2)}) copy-start(pred[1024]{0:T(1024)(128)(4,1)} %copy-done.103) | copy-start | bytes 3076
  445.8 9.7 %copy-start.106 = (pred[1024]{0:T(1024)(128)(4,1)S(1)}, pred[1024]{0:T(1024)(128)(4,1)}, u32[]{:S(2)}) copy-start(pred[1024]{0:T(1024)(128)(4,1)} %copy-done.105) | copy-start | bytes 3076
  445.8 9.7 %copy-start.108 = (pred[1024]{0:T(1024)(128)(4,1)S(1)}, pred[1024]{0:T(1024)(128)(4,1)}, u32[]{:S(2)}) copy-start(pred[1024]{0:T(1024)(128)(4,1)} %copy-done.107) | copy-start | bytes 3076
  466.5 164.5 %reduce-scatter.10.cloned.1.call-start = ((), (), s32[]{:S(2)}) async-start(), calls=%async_computation.11 | async-start | bytes 2621440 | tf_op jit(solution)/shard_map/reduce_scatter | solution.py:960
  475.5 22.3 %copy-start.132 = (f32[128]{0:T(128)S(1)}, f32[128]{0:T(128)}, u32[]{:S(2)}) copy-start(f32[128]{0:T(128)} %copy-done.131) | copy-start | bytes 1540
  497.4 7.9 %copy-start.23 = (f32[128,2048]{0,1:T(8,128)}, f32[128,2048]{0,1:T(8,128)S(1)}, u32[]{:S(2)}) copy-start(f32[128,2048]{0,1:T(8,128)S(1)} %copy.532) | copy-start | bytes 3145732
  505.4 171.1 %reduce-scatter.14.cloned.1.call-start = ((), (), s32[]{:S(2)}) async-start(), calls=%async_computation.13 | async-start | bytes 2621440 | tf_op jit(solution)/shard_map/reduce_scatter | solution.py:960
  552.2 35.6 %all-to-all-start.3 = ((bf16[8,64,1024]{2,1,0:T(8,128)(2,1)}), bf16[8,64,1024]{2,1,0:T(8,128)(2,1)}, u32[]{:S(2)}, u32[]{:S(2)}) async-start(bf16[8,64,1024]{2,1,0:T(8,128)(2,1)} %bitcast.492), calls=%async_computation.8 | async-start | bytes 2097152 | tf_op jit(solution)/shard_map/all_to_all | solution.py:972
  587.8 49.2 %all-to-all-start.2 = ((bf16[8,64,1280]{2,1,0:T(8,128)(2,1)}), bf16[8,64,1280]{2,1,0:T(8,128)(2,1)}, u32[]{:S(2)}, u32[]{:S(2)}) async-start(bf16[8,64,1280]{2,1,0:T(8,128)(2,1)} %pad_maximum_fusion.6), calls=%async_computation.4 | async-start | bytes 2621440 | tf_op jit(solution)/shard_map/all_to_all | solution.py:972
  (112 other events, 382.2 us)
Sparse Core Ops, SparseCore 0:
  10.2 48.6 all-gather.14
  61.0 44.6 all-gather.10
  107.9 62.2 all-gather.12
  171.5 79.4 all-gather.16
  252.4 44.4 all-gather.18
  400.7 58.5 reduce-scatter.5
  461.7 76.7 reduce-scatter.11
  540.9 44.4 reduce-scatter.7
  587.6 43.3 reduce-scatter.9
  633.2 43.1 reduce-scatter.13

commit v3 on v2

--- a/solution.py
+++ b/solution.py
@@ -635,6 +635,13 @@
     return me, sibling, by_x, by_y
 
 
+def unused(kernel, used, extra):
+    def call(*refs):
+        return kernel(*refs[:used], *refs[used + extra :])
+
+    return call
+
+
 def greet(peers):
     barrier = pltpu.get_barrier_semaphore()
     for axis, other in peers:
@@ -653,13 +660,25 @@
     )
 
 
-def gather_kernel(pieces, x_ref, o_ref, own_sem, send_sem, recv_sem):
+def together(*tasks):
+    tasks = list(tasks)
+    while tasks:
+        for task in list(tasks):
+            if next(task, None) is None:
+                tasks.remove(task)
+
+
+def other_places(axis, count):
+    place = lax.axis_index(axis)
+    return [(axis, (place + j) % count) for j in range(1, count)]
+
+
+def gather_steps(pieces, x_ref, o_ref, own_sem, send_sem, recv_sem):
     rows = x_ref.shape[0]
     n = rows // pieces
     half = pieces // 2
     me, sibling, by_x, by_y = plane()
     across = by_x + by_y - me
-    greet([(CTX, sibling), (CTX, by_x), (CTX, by_y)])
     keep = pltpu.make_async_copy(x_ref, o_ref.at[pl.ds(me * rows, rows)], own_sem)
     keep.start()
     started = []
@@ -684,6 +703,7 @@
         go(x_ref.at[pl.ds(b * n, n)], me, b, 2, by_y, 2)
     for i in range(pieces):
         go(x_ref.at[pl.ds(i * n, n)], me, i, 0, sibling, 0)
+    yield True
     for i in range(pieces):
         a, b = i, pieces - 1 - i
         arrived(by_x, a, 1)
@@ -694,10 +714,12 @@
         if i < half:
             go(at(by_y, b), by_y, b, 5, by_x, 5)
         go(at(by_y, b), by_y, b, 4, sibling, 4)
+        yield True
     for i in range(half):
         for p in (i, pieces - 1 - i):
             arrived(across, p, 5)
             go(at(across, p), across, p, 6, sibling, 6)
+        yield True
     shift = sibling - me
     for p in range(pieces):
         arrived(sibling, p, 0)
@@ -709,12 +731,94 @@
     keep.wait()
 
 
-def gather_tokens(block, ids, pieces=4):
+def chain_steps(pieces, count, x_ref, o_ref, own_sem, send_sem, recv_sem):
+    mine = lax.axis_index(FSDP)
+    n = x_ref.shape[0] // pieces
+    up, down = mine + 1, mine - 1
+    has_up, has_down = mine < count - 1, mine > 0
+    keep = pltpu.make_async_copy(x_ref, o_ref.at[mine], own_sem)
+    keep.start()
+
+    def copy(src, block, piece, way, hop, to):
+        return remote(
+            src,
+            o_ref.at[block, pl.ds(piece * n, n)],
+            send_sem.at[way, hop, piece],
+            recv_sem.at[way, hop, piece],
+            FSDP,
+            to,
+        )
+
+    def own(piece):
+        return x_ref.at[pl.ds(piece * n, n)]
+
+    for p in range(pieces):
+
+        @pl.when(has_up)
+        def _(p=p):
+            copy(own(p), mine, p, 0, 0, up).start()
+
+        @pl.when(has_down)
+        def _(p=p):
+            copy(own(p), mine, p, 1, 0, down).start()
+
+    yield True
+    for d in range(1, count):
+        for p in range(pieces):
+
+            @pl.when(mine >= d)
+            def _(d=d, p=p):
+                here = o_ref.at[mine - d, pl.ds(p * n, n)]
+                copy(here, mine - d, p, 0, d - 1, down).wait_recv()
+
+                @pl.when(has_up)
+                def _():
+                    copy(here, mine - d, p, 0, d, up).start()
+
+            @pl.when(mine + d < count)
+            def _(d=d, p=p):
+                here = o_ref.at[mine + d, pl.ds(p * n, n)]
+                copy(here, mine + d, p, 1, d - 1, up).wait_recv()
+
+                @pl.when(has_down)
+                def _():
+                    copy(here, mine + d, p, 1, d, down).start()
+
+            yield True
+    for d in range(count - 1):
+        for p in range(pieces):
+
+            @pl.when((mine >= d) & has_up)
+            def _(d=d, p=p):
+                copy(own(p), mine - d, p, 0, d, up).wait_send()
+
+            @pl.when((mine + d < count) & has_down)
+            def _(d=d, p=p):
+                copy(own(p), mine + d, p, 1, d, down).wait_send()
+
+    keep.wait()
+
+
+def chain_scratch(pieces, count):
+    return [
+        pltpu.SemaphoreType.DMA,
+        pltpu.SemaphoreType.DMA((2, count - 1, pieces)),
+        pltpu.SemaphoreType.DMA((2, count - 1, pieces)),
+    ]
+
+
+def gather_kernel(pieces, *refs):
+    me, sibling, by_x, by_y = plane()
+    greet([(CTX, sibling), (CTX, by_x), (CTX, by_y)])
+    together(gather_steps(pieces, *refs))
+
+
+def gather_tokens(block, ids, pieces=4, waits=()):
     rows, cols = block.shape
     return pl.pallas_call(
-        partial(gather_kernel, pieces),
+        unused(partial(gather_kernel, pieces), 1, len(waits)),
         out_shape=jax.ShapeDtypeStruct((PLANE * rows, cols), block.dtype),
-        in_specs=[pl.BlockSpec(memory_space=pl.ANY)],
+        in_specs=[pl.BlockSpec(memory_space=pl.ANY)] * (1 + len(waits)),
         out_specs=pl.BlockSpec(memory_space=pl.ANY),
         scratch_shapes=[
             pltpu.SemaphoreType.DMA,
@@ -723,19 +827,22 @@
         ],
         cost_estimate=lasting(22 if cols > 1024 else 8),
         compiler_params=pltpu.CompilerParams(collective_id=next(ids), has_side_effects=True),
-    )(block)
-
-
-def scatter_kernel(p_ref, o_ref, own, got, out, rx, ry, dx, dy, own_sem, send_sem, recv_sem):
+    )(block, *waits)
+
+
+def scatter_steps(
+    seqs, p_ref, o_ref, own, got, out, rx, ry, dx, dy, own_sem, send_sem, recv_sem, make=None
+):
     rows = o_ref.shape[0]
     h = rows // 2
     me, sibling, by_x, by_y = plane()
     across = by_x + by_y - me
     shift = sibling - me
-    greet([(CTX, sibling), (CTX, by_x), (CTX, by_y)])
     top, low = pl.ds(0, h), pl.ds(h, h)
     loads, sends = [], []
     for k, block in enumerate((across, by_x, by_y, me)):
+        if make is not None:
+            make(block // 2)
         for j in range(2):
             copy = remote(
                 p_ref.at[pl.ds((block + shift) * rows + j * h, h)],
@@ -761,12 +868,25 @@
         part = pl.ds(j * h, h)
         return own[k, part].astype(F32) + got[k, part].astype(F32)
 
+    def put(part, total):
+        if not seqs:
+            o_ref[part] = total
+            return
+        chunk = total.shape[1] // (PLANE * seqs)
+        per = 128 // chunk
+        for k in range(total.shape[1] // 128):
+            blocks = [(n % seqs) * PLANE + n // seqs for n in range(k * per, (k + 1) * per)]
+            o_ref[part, k * 128 : (k + 1) * 128] = jnp.concatenate(
+                [total[:, b * chunk : (b + 1) * chunk] for b in blocks], axis=1
+            )
+
     def go(src, dst, slot, to):
         copy = remote(src, dst, send_sem.at[slot], recv_sem.at[slot], CTX, to)
         copy.start()
         sends.append(copy)
         return copy
 
+    yield True
     out[0, top] = pair(0, 0).astype(out.dtype)
     across_x = go(out.at[0, top], dx, 8, by_x)
     out[0, low] = pair(0, 1).astype(out.dtype)
@@ -775,51 +895,63 @@
     x_top = go(out.at[1, top], rx.at[top], 10, by_x)
     out[2, low] = pair(2, 1).astype(out.dtype)
     y_low = go(out.at[2, low], ry.at[low], 11, by_y)
+    yield True
     across_y.wait_recv()
     out[1, low] = (pair(1, 1) + dy[...].astype(F32)).astype(out.dtype)
     x_low = go(out.at[1, low], rx.at[low], 12, by_x)
     across_x.wait_recv()
     out[2, top] = (pair(2, 0) + dx[...].astype(F32)).astype(out.dtype)
     y_top = go(out.at[2, top], ry.at[top], 13, by_y)
+    yield True
     first, second = pair(3, 0), pair(3, 1)
     x_top.wait_recv()
     y_top.wait_recv()
-    o_ref[top] = first + rx[top].astype(F32) + ry[top].astype(F32)
+    put(top, first + rx[top].astype(F32) + ry[top].astype(F32))
     x_low.wait_recv()
     y_low.wait_recv()
-    o_ref[low] = second + rx[low].astype(F32) + ry[low].astype(F32)
+    put(low, second + rx[low].astype(F32) + ry[low].astype(F32))
     for copy in sends:
         copy.wait_send()
 
 
-def scatter_tokens(partial_sum, ids):
-    rows, cols = partial_sum.shape[0] // PLANE, partial_sum.shape[1]
-
+def scatter_kernel(seqs, *refs):
+    me, sibling, by_x, by_y = plane()
+    greet([(CTX, sibling), (CTX, by_x), (CTX, by_y)])
+    together(scatter_steps(seqs, *refs))
+
+
+def scatter_scratch(rows, cols):
     def room(*shape):
         return pltpu.VMEM(shape, BF)
 
+    return [
+        room(4, rows, cols),
+        room(4, rows, cols),
+        room(3, rows, cols),
+        room(rows, cols),
+        room(rows, cols),
+        room(rows // 2, cols),
+        room(rows // 2, cols),
+        pltpu.SemaphoreType.DMA((8,)),
+        pltpu.SemaphoreType.DMA((14,)),
+        pltpu.SemaphoreType.DMA((14,)),
+    ]
+
+
+def scatter_tokens(partial_sum, ids, waits=(), seqs=0):
+    rows, cols = partial_sum.shape[0] // PLANE, partial_sum.shape[1]
+
     return pl.pallas_call(
-        scatter_kernel,
+        unused(partial(scatter_kernel, seqs), 1, len(waits)),
         out_shape=jax.ShapeDtypeStruct((rows, cols), F32),
-        in_specs=[pl.BlockSpec(memory_space=pl.ANY)],
+        in_specs=[pl.BlockSpec(memory_space=pl.ANY)] * (1 + len(waits)),
         out_specs=pl.BlockSpec(memory_space=pltpu.VMEM),
-        scratch_shapes=[
-            room(4, rows, cols),
-            room(4, rows, cols),
-            room(3, rows, cols),
-            room(rows, cols),
-            room(rows, cols),
-            room(rows // 2, cols),
-            room(rows // 2, cols),
-            pltpu.SemaphoreType.DMA((8,)),
-            pltpu.SemaphoreType.DMA((14,)),
-            pltpu.SemaphoreType.DMA((14,)),
-        ],
+        scratch_shapes=scatter_scratch(rows, cols),
         cost_estimate=lasting(22 if cols > 1024 else 8),
         compiler_params=pltpu.CompilerParams(
             collective_id=next(ids), has_side_effects=True, vmem_limit_bytes=40 * 2**20
         ),
-    )(partial_sum.astype(BF))
+    )(partial_sum.astype(BF), *waits)
 
 
 def row_sum_kernel(x_ref, o_ref, got, send_sem, recv_sem):
@@ -841,12 +973,13 @@
         copy.wait_send()
 
 
-def row_sum(rows, ids):
+def row_sum(rows, ids, waits=()):
     tile = rows.reshape(8, -1)
     total = pl.pallas_call(
-        row_sum_kernel,
+        unused(row_sum_kernel, 1, len(waits)),
         out_shape=jax.ShapeDtypeStruct(tile.shape, F32),
-        in_specs=[pl.BlockSpec(memory_space=pltpu.VMEM)],
+        in_specs=[pl.BlockSpec(memory_space=pltpu.VMEM)]
+        + [pl.BlockSpec(memory_space=pl.ANY)] * len(waits),
         out_specs=pl.BlockSpec(memory_space=pltpu.VMEM),
         scratch_shapes=[
             pltpu.VMEM((PLANE - 1,) + tile.shape, F32),
@@ -855,74 +988,185 @@
         ],
         cost_estimate=lasting(5),
         compiler_params=pltpu.CompilerParams(collective_id=next(ids), has_side_effects=True),
-    )(tile)
+    )(tile, *waits)
     return total.reshape(rows.shape)
 
 
-def small_gather_kernel(seqs, x_ref, o_ref, own_sem, send_sem, recv_sem):
+def small_gather_steps(seqs, x_ref, o_ref, own_sem, send_sem, recv_sem):
     me, mine = lax.axis_index(CTX), lax.axis_index(FSDP)
-    others = [(FSDP, (mine + j) % seqs) for j in range(1, seqs)]
-    greet(others + [(CTX, (me + j) % PLANE) for j in range(1, PLANE)])
     keep = pltpu.make_async_copy(x_ref, o_ref.at[me, mine], own_sem)
     keep.start()
     copies = []
-    for j, (_, other) in enumerate(others):
-        copy = remote(x_ref, o_ref.at[me, mine], send_sem.at[j], recv_sem.at[j], FSDP, other)
+    for j, (axis, other) in enumerate(other_places(FSDP, seqs)):
+        copy = remote(x_ref, o_ref.at[me, mine], send_sem.at[j], recv_sem.at[j], axis, other)
         copy.start()
         copies.append(copy)
+    yield True
     keep.wait()
     for copy in copies:
         copy.wait_recv()
-    for j in range(1, PLANE):
+    for j, (axis, other) in enumerate(other_places(CTX, PLANE)):
         k = seqs + j
-        copy = remote(
-            o_ref.at[me], o_ref.at[me], send_sem.at[k], recv_sem.at[k], CTX, (me + j) % PLANE
-        )
+        copy = remote(o_ref.at[me], o_ref.at[me], send_sem.at[k], recv_sem.at[k], axis, other)
         copy.start()
         copies.append(copy)
+    for _ in range(8):
+        yield True
     for copy in copies[seqs - 1 :]:
         copy.wait_recv()
     for copy in copies:
         copy.wait_send()
 
 
-def small_gather(tile, seqs, ids):
+def columns(ref, place, count):
+    return ref.at[:, pl.ds(pl.multiple_of(place * count, 128), count)]
+
+
+def swap_steps(delay, patience, routes, own_sem, send_sem, recv_sem):
+    me = lax.axis_index(CTX)
+    for _ in range(delay):
+        yield True
+    keeps, copies = [], []
+    for k, (part, land) in enumerate(routes):
+        keep = pltpu.make_async_copy(part(me), land(me), own_sem.at[k])
+        keep.start()
+        keeps.append(keep)
+    for j in (4, 2, 6, 3, 5, 7, 1):
+        to = (me + j) % PLANE
+        for k, (part, land) in enumerate(routes):
+            copy = remote(part(to), land(me), send_sem.at[j, k], recv_sem.at[j, k], CTX, to)
+            copy.start()
+            copies.append(copy)
+    for _ in range(patience):
+        yield True
+    for copy in copies:
+        copy.wait_recv()
+    for copy in copies:
+        copy.wait_send()
+    for keep in keeps:
+        keep.wait()
+
+
+def swap_scratch(routes):
+    return [
+        pltpu.SemaphoreType.DMA((routes,)),
+        pltpu.SemaphoreType.DMA((PLANE, routes)),
+        pltpu.SemaphoreType.DMA((PLANE, routes)),
+    ]
+
+
+def one_after(*tasks):
+    for task in tasks:
+        yield from task
+
+
+def opening_kernel(seqs, pieces, *refs):
+    tile, shard, hat, rows, query, zgate, channels, mixed, gate, up = refs[:10]
+    o_tile, o_shard, o_hat, o_rows, conv, rest, ffn, o_conv = refs[10:18]
+    sems = refs[18:]
+    sems = [sems[k : k + 3] for k in range(0, len(sems), 3)]
+    head = query.shape[1] // PLANE
+    inner = zgate.shape[1] // PLANE
+    half = gate.shape[1] // PLANE
+    greet(other_places(FSDP, seqs) + other_places(CTX, PLANE))
+    to_conv = [
+        (lambda to: columns(channels, to, inner), lambda at: conv.at[at, :, :inner]),
+        (lambda to: mixed.at[to], lambda at: conv.at[at, :, inner:]),
+    ]
+    to_rest = [
+        (lambda to: columns(query, to, head), lambda at: rest.at[at, :, :head]),
+        (lambda to: columns(zgate, to, inner), lambda at: rest.at[at, :, head:]),
+    ]
+    to_ffn = [
+        (lambda to: columns(gate, to, half), lambda at: ffn.at[at, :, :half]),
+        (lambda to: columns(up, to, half), lambda at: ffn.at[at, :, half:]),
+    ]
+    together(
+        one_after(
+            swap_steps(0, 1, to_conv, *sems[0]), chain_steps(4, seqs, conv, o_conv, *sems[1])
+        ),
+        chain_steps(4, seqs, shard, o_shard, *sems[2]),
+        small_gather_steps(seqs, tile, o_tile, *sems[3]),
+        gather_steps(pieces, hat, o_hat, *sems[4]),
+        swap_steps(1, 8, to_rest, *sems[5]),
+        swap_steps(3, 8, to_ffn, *sems[6]),
+        one_after(delay_steps(5), gather_steps(pieces, rows, o_rows, *sems[7])),
+    )
+
+
+def delay_steps(turns):
+    for _ in range(turns):
+        yield True
+
+
+def opening(tile, shard, hat, rows, query, zgate, channels, mixed, gate, up, seqs, ids, pieces=2):
+    anywhere = pl.BlockSpec(memory_space=pl.ANY)
+    krows = query.shape[0]
+    inner = zgate.shape[1] // PLANE
+    conv_cols = inner + mixed.shape[2]
+    rest_cols = query.shape[1] // PLANE + inner
+    ffn_cols = (gate.shape[1] + up.shape[1]) // PLANE
+
+    def shape(*dims):
+        return jax.ShapeDtypeStruct(dims, BF)
+
+    def three(*dims):
+        return [
+            pltpu.SemaphoreType.DMA,
+            pltpu.SemaphoreType.DMA(dims),
+            pltpu.SemaphoreType.DMA(dims),
+        ]
+
     return pl.pallas_call(
-        partial(small_gather_kernel, seqs),
-        out_shape=jax.ShapeDtypeStruct((PLANE, seqs) + tile.shape, tile.dtype),
-        in_specs=[pl.BlockSpec(memory_space=pltpu.VMEM)],
-        out_specs=pl.BlockSpec(memory_space=pltpu.VMEM),
-        scratch_shapes=[
-            pltpu.SemaphoreType.DMA,
-            pltpu.SemaphoreType.DMA((PLANE + seqs,)),
-            pltpu.SemaphoreType.DMA((PLANE + seqs,)),
-        ],
-        cost_estimate=lasting(8),
+        partial(opening_kernel, seqs, pieces),
+        out_shape=(
+            shape(PLANE, seqs, *tile.shape),
+            shape(seqs, *shard.shape),
+            shape(PLANE * hat.shape[0], hat.shape[1]),
+            shape(PLANE * rows.shape[0], rows.shape[1]),
+            shape(PLANE, krows, conv_cols),
+            shape(PLANE, krows, rest_cols),
+            shape(PLANE, krows, ffn_cols),
+            shape(seqs, PLANE, krows, conv_cols),
+        ),
+        in_specs=[anywhere] * 10,
+        out_specs=(anywhere,) * 8,
+        scratch_shapes=swap_scratch(2)
+        + chain_scratch(4, seqs)
+        + chain_scratch(4, seqs)
+        + three(PLANE + seqs)
+        + three(7, pieces)
+        + swap_scratch(2)
+        + swap_scratch(2)
+        + three(7, pieces),
+        cost_estimate=lasting(70),
         compiler_params=pltpu.CompilerParams(collective_id=next(ids), has_side_effects=True),
-    )(tile)
-
-
-def small_scatter_kernel(seqs, x_ref, o_ref, got, total, late, send_sem, recv_sem):
+    )(tile, shard, hat, rows, query, zgate, channels, mixed, gate, up)
+
+
+def small_scatter_steps(seqs, x_ref, o_ref, mine_ref, got, total, late, own_sem, send_sem, recv_sem):
     me, mine = lax.axis_index(CTX), lax.axis_index(FSDP)
-    others = [(FSDP, (mine + j) % seqs) for j in range(1, seqs)]
-    greet(others + [(CTX, (me + j) % PLANE) for j in range(1, PLANE)])
+    load = pltpu.make_async_copy(x_ref.at[me], mine_ref, own_sem)
+    load.start()
     copies = []
-    for j in range(1, PLANE):
-        to = (me + j) % PLANE
-        copy = remote(x_ref.at[to], got.at[j - 1], send_sem.at[j], recv_sem.at[j], CTX, to)
+    for j, (axis, to) in enumerate(other_places(CTX, PLANE)):
+        copy = remote(x_ref.at[to], got.at[j], send_sem.at[j], recv_sem.at[j], axis, to)
         copy.start()
         copies.append(copy)
-    acc = x_ref[me]
+    yield True
+    load.wait()
+    acc = mine_ref[...]
     for j, copy in enumerate(copies):
         copy.wait_recv()
         acc = acc + got[j]
     total[...] = acc
     first = len(copies)
-    for j, (_, other) in enumerate(others):
+    for j, (axis, other) in enumerate(other_places(FSDP, seqs)):
         k = PLANE + j
-        copy = remote(total.at[other], late.at[j], send_sem.at[k], recv_sem.at[k], FSDP, other)
+        copy = remote(total.at[other], late.at[j], send_sem.at[k], recv_sem.at[k], axis, other)
         copy.start()
         copies.append(copy)
+    yield True
     out = total[mine]
     for j, copy in enumerate(copies[first:]):
         copy.wait_recv()
@@ -932,24 +1176,253 @@
         copy.wait_send()
 
 
-def small_scatter(tiles, ids):
-    seqs = tiles.shape[1]
-    tile = tiles.shape[2:]
+def scatter_two_kernel(p_ref, q_ref, o_ref, oq_ref, *scratch):
+    me, sibling, by_x, by_y = plane()
+    greet([(CTX, sibling), (CTX, by_x), (CTX, by_y)])
+    together(
+        scatter_steps(0, p_ref, o_ref, *scratch[:10]),
+        scatter_steps(0, q_ref, oq_ref, *scratch[10:]),
+    )
+
+
+def scatter_two(first, second, ids, waits=()):
+    near = pl.BlockSpec(memory_space=pltpu.VMEM)
+    shapes = [(x.shape[0] // PLANE, x.shape[1]) for x in (first, second)]
     return pl.pallas_call(
-        partial(small_scatter_kernel, seqs),
-        out_shape=jax.ShapeDtypeStruct(tile, F32),
-        in_specs=[pl.BlockSpec(memory_space=pltpu.VMEM)],
-        out_specs=pl.BlockSpec(memory_space=pltpu.VMEM),
+        unused(scatter_two_kernel, 2, len(waits)),
+        out_shape=tuple(jax.ShapeDtypeStruct(shape, F32) for shape in shapes),
+        in_specs=[pl.BlockSpec(memory_space=pl.ANY)] * (2 + len(waits)),
+        out_specs=(near, near),
+        scratch_shapes=scatter_scratch(*shapes[0]) + scatter_scratch(*shapes[1]),
+        cost_estimate=lasting(28),
+        compiler_params=pltpu.CompilerParams(
+            collective_id=next(ids), has_side_effects=True, vmem_limit_bytes=40 * 2**20
+        ),
+    )(first, second, *waits)
+
+
+def closing_kernel(
+    seqs, g1, g2, g3, w1, w2, w3, rest, ffn, hat, o_ref, norm_ref, query, zgate, gate, up, p_ref, *scratch
+):
+    factors, own, sems = (g1, g2, g3, w1, w2, w3), scratch[:6], scratch[6]
+    scratch = scratch[7:]
+    loads = [
+        pltpu.make_async_copy(factors[k], own[k], sems.at[k]) for k in range(len(factors))
+    ]
+    for load in loads:
+        load.start()
+    greet(other_places(CTX, PLANE))
+    head = query.shape[1] // PLANE
+    inner = zgate.shape[1] // PLANE
+    half = gate.shape[1] // PLANE
+    pair = 2 * o_ref.shape[0]
+
+    def make(chip):
+        rows = pl.ds(pl.multiple_of(chip * pair, pair), pair)
+        total = 0.0
+        for g, w in zip(own[:3], own[3:]):
+            total = total + lax.dot_general(
+                g[rows, :], w[...], (((1,), (1,)), ((), ())), preferred_element_type=F32
+            )
+        p_ref[rows, :] = total.astype(BF)
+
+    from_rest = [
+        (lambda to: rest.at[to, :, :head], lambda at: columns(query, at, head)),
+        (lambda to: rest.at[to, :, head:], lambda at: columns(zgate, at, inner)),
+    ]
+    from_ffn = [
+        (lambda to: ffn.at[to, :, :half], lambda at: columns(gate, at, half)),
+        (lambda to: ffn.at[to, :, half:], lambda at: columns(up, at, half)),
+    ]
+    for load in loads:
+        load.wait()
+    together(
+        swap_steps(0, 8, from_rest, *scratch[10:13]),
+        swap_steps(0, 8, from_ffn, *scratch[13:]),
+        scatter_steps(seqs, p_ref, o_ref, *scratch[:10], make=make),
+    )
+    total = jnp.sum(o_ref[...] * hat[...], axis=0, keepdims=True)
+    norm_ref[...] = jnp.zeros_like(norm_ref)
+    part = total.shape[1] // (PLANE * seqs)
+    for k in range(PLANE * seqs):
+        norm_ref[k // seqs, k % seqs, 0:1, 0:part] = total[:, k * part : (k + 1) * part]
+
+
+def closing(grads, weights, rest, ffn, hat, head, seqs, ids, waits=()):
+    anywhere = pl.BlockSpec(memory_space=pl.ANY)
+    near = pl.BlockSpec(memory_space=pltpu.VMEM)
+    length, cols = grads[0].shape[0], weights[0].shape[0]
+    rows = length // PLANE
+    _, krows, rest_cols = rest.shape
+    half = ffn.shape[2] // 2
+
+    def wide(count):
+        return jax.ShapeDtypeStruct((krows, PLANE * count), BF)
+
+    return pl.pallas_call(
+        unused(partial(closing_kernel, seqs), 9, len(waits)),
+        out_shape=(
+            jax.ShapeDtypeStruct((rows, cols), F32),
+            jax.ShapeDtypeStruct((PLANE, seqs, 8, 128), F32),
+            wide(head),
+            wide(rest_cols - head),
+            wide(half),
+            wide(half),
+        ),
+        in_specs=[anywhere] * 8 + [near] + [anywhere] * len(waits),
+        out_specs=(near, near) + (anywhere,) * 4,
+        scratch_shapes=[pltpu.VMEM((length, cols), BF)]
+        + [pltpu.VMEM(x.shape, BF) for x in (*grads, *weights)]
+        + [pltpu.SemaphoreType.DMA((6,))]
+        + scatter_scratch(rows, cols)
+        + swap_scratch(2)
+        + swap_scratch(2),
+        cost_estimate=lasting(35),
+        compiler_params=pltpu.CompilerParams(
+            collective_id=next(ids), has_side_effects=True, vmem_limit_bytes=60 * 2**20
+        ),
+    )(*grads, *weights, rest, ffn, hat, *waits)
+
+
+def step_sum_steps(seqs, x_ref, o_ref, land, got, own_sem, send_sem, recv_sem):
+    me, mine = lax.axis_index(CTX), lax.axis_index(FSDP)
+    keep = pltpu.make_async_copy(x_ref.at[me], land.at[me], own_sem)
+    keep.start()
+    copies = []
+    for j, (axis, to) in enumerate(other_places(CTX, PLANE)):
+        copy = remote(x_ref.at[to], land.at[me], send_sem.at[j], recv_sem.at[j], axis, to)
+        copy.start()
+        copies.append(copy)
+    yield True
+    keep.wait()
+    for copy in copies:
+        copy.wait_recv()
+    first = len(copies)
+    for j, (axis, other) in enumerate(other_places(FSDP, seqs)):
+        k = PLANE + j
+        copy = remote(land.at[:, other], got.at[j], send_sem.at[k], recv_sem.at[k], axis, other)
+        copy.start()
+        copies.append(copy)
+    yield True
+    total = land[:, mine]
+    for j, copy in enumerate(copies[first:]):
+        copy.wait_recv()
+        total = total + got[j]
+    o_ref[...] = total
+    for copy in copies:
+        copy.wait_send()
+
+
+def last_kernel(
+    seqs, norm, ffn_gain, mixer_gain, channel, by_head, step, conv,
+    small_ref, step_ref, channels, key, value,
+    mixed, x_ref, st_ref, full, *scratch
+):
+    me = lax.axis_index(CTX)
+    given = (norm, ffn_gain, mixer_gain, channel, by_head, step)
+    near, sems, scratch = scratch[:6], scratch[6], scratch[7:]
+    loads = [pltpu.make_async_copy(given[k], near[k], sems.at[k]) for k in range(len(given))]
+    for load in loads:
+        load.start()
+    norm, ffn_gain, mixer_gain, channel, by_head, step = near
+    devices = PLANE * seqs
+    krows = conv.shape[1]
+    bc = 2 * STATE // PLANE
+    total = channels.shape[1] - 2 * STATE
+    inner = total // PLANE
+    kv = value.shape[1] // PLANE
+    from_conv = [
+        (lambda to: conv.at[to, :, :inner], lambda at: columns(channels, at, inner)),
+        (lambda to: conv.at[to, :, inner:], lambda at: mixed.at[at]),
+    ]
+    x_ref[...] = jnp.zeros_like(x_ref)
+    full[...] = jnp.zeros_like(full)
+    st_ref[...] = jnp.zeros_like(st_ref)
+    for load in loads:
+        load.wait()
+    kinds = channel.shape[0]
+    full[0:kinds, pl.ds(pl.multiple_of(me * inner, 128), inner)] = channel[:, :inner]
+    for k in range(PLANE):
+        full[0:kinds, total + k * bc : total + (k + 1) * bc] = jnp.where(
+            me == k, channel[:, inner:], 0.0
+        )
+    heads = by_head.shape[1]
+    mine_only = [jnp.where(me == k, by_head[...], 0.0) for k in range(PLANE)]
+    spread = jnp.concatenate(mine_only, axis=1)
+    part, wide = ffn_gain.shape[1] // devices, full.shape[1] // devices
+    for n in range(devices):
+        c, f = n // seqs, n % seqs
+        x_ref[c, f, 0:1, 0:part] = ffn_gain[:, n * part : (n + 1) * part]
+        x_ref[c, f, 1:2, :] = norm[c, f, 0:1, :]
+        x_ref[c, f, 3 : 3 + kinds, 0:wide] = full[0:kinds, n * wide : (n + 1) * wide]
+        x_ref[c, f, 8:11, 0 : PLANE * heads] = spread
+        at = (f * PLANE + c) * krows
+        st_ref[c, f, 0:heads, 0:krows] = step[:, at : at + krows]
+    part = inner // seqs
+    for f in range(seqs):
+        x_ref[me, f, 2:3, 0:part] = mixer_gain[:, f * part : (f + 1) * part]
+    greet(other_places(FSDP, seqs) + other_places(CTX, PLANE))
+    together(
+        small_scatter_steps(seqs, x_ref, small_ref, *scratch[:7]),
+        step_sum_steps(seqs, st_ref, step_ref, *scratch[7:12]),
+        swap_steps(0, 2, from_conv, *scratch[12:]),
+    )
+    blocks = [mixed[k].astype(F32) for k in range(PLANE)]
+    channels[:, total:] = jnp.concatenate([b[:, :bc] for b in blocks], axis=1).astype(BF)
+    value[...] = jnp.concatenate([b[:, bc + kv :] for b in blocks], axis=1)
+    half = kv // 2
+    group = PLANE // KEY_VALUE_HEADS
+    turned = []
+    for k in range(0, PLANE, group):
+        for at in (bc, bc + half):
+            turned += [b[:, at : at + half] for b in blocks[k : k + group]]
+    key[...] = jnp.concatenate(turned, axis=1)
+
+
+def last_exchange(small, conv, inner, kv, seqs, ids):
+    anywhere = pl.BlockSpec(memory_space=pl.ANY)
+    near = pl.BlockSpec(memory_space=pltpu.VMEM)
+    _, krows, cols = conv.shape
+
+    def room(*shape):
+        return pltpu.VMEM(shape, F32)
+
+    two = [pltpu.SemaphoreType.DMA((PLANE + seqs,)), pltpu.SemaphoreType.DMA((PLANE + seqs,))]
+    return pl.pallas_call(
+        partial(last_kernel, seqs),
+        out_shape=(
+            jax.ShapeDtypeStruct((16, 128), F32),
+            jax.ShapeDtypeStruct((PLANE, 8, 128), F32),
+            jax.ShapeDtypeStruct((krows, PLANE * inner + 2 * STATE), BF),
+            jax.ShapeDtypeStruct((krows, PLANE * kv), F32),
+            jax.ShapeDtypeStruct((krows, PLANE * kv), F32),
+        ),
+        in_specs=[anywhere] * 7,
+        out_specs=(near,) * 5,
         scratch_shapes=[
-            pltpu.VMEM((PLANE - 1,) + tiles.shape[1:], F32),
-            pltpu.VMEM(tiles.shape[1:], F32),
-            pltpu.VMEM((seqs - 1,) + tile, F32),
-            pltpu.SemaphoreType.DMA((PLANE + seqs,)),
-            pltpu.SemaphoreType.DMA((PLANE + seqs,)),
-        ],
-        cost_estimate=lasting(8),
-        compiler_params=pltpu.CompilerParams(collective_id=next(ids), has_side_effects=True),
-    )(tiles)
+            pltpu.VMEM((PLANE, krows, cols - inner), BF),
+            room(PLANE, seqs, 16, 128),
+            room(PLANE, seqs, 8, 128),
+            room(8, PLANE * inner + 2 * STATE),
+            *[room(*x.shape) for x in small],
+            pltpu.SemaphoreType.DMA((6,)),
+            room(seqs, 16, 128),
+            room(PLANE - 1, seqs, 16, 128),
+            room(seqs, 16, 128),
+            room(seqs - 1, 16, 128),
+            pltpu.SemaphoreType.DMA,
+            *two,
+            room(PLANE, seqs, 8, 128),
+            room(seqs - 1, PLANE, 8, 128),
+            pltpu.SemaphoreType.DMA,
+            *two,
+        ]
+        + swap_scratch(2),
+        cost_estimate=lasting(15),
+        compiler_params=pltpu.CompilerParams(
+            collective_id=next(ids), has_side_effects=True, vmem_limit_bytes=40 * 2**20
+        ),
+    )(*small, conv)
 
 
 def gather_rows(shard):
@@ -960,21 +1433,39 @@
     return lax.psum_scatter(partial_sum.astype(BF), FSDP, scatter_dimension=0, tiled=False)
 
 
-def after(value, *earlier):
-    return lax.optimization_barrier((value, *earlier))[0]
+def hold_kernel(*refs):
+    pass
+
+
+def hold(value, *earlier):
+    anywhere = pl.BlockSpec(memory_space=pl.ANY)
+    return pl.pallas_call(
+        hold_kernel,
+        out_shape=jax.ShapeDtypeStruct(value.shape, value.dtype),
+        in_specs=[anywhere] * (1 + len(earlier)),
+        out_specs=anywhere,
+        input_output_aliases={0: 0},
+    )(value, *earlier)
 
 
 def lasting(us):
-    return pl.CostEstimate(flops=int(us * 1e9), bytes_accessed=int(us * 3e6), transcendentals=0)
-
-
-def swap_columns(packed):
-    return lax.all_to_all(packed, CTX, split_axis=0, concat_axis=0, tiled=True)
+    return pl.CostEstimate(flops=int(us * 0.3e9), bytes_accessed=int(us * 0.3e6), transcendentals=0)
 
 
 def same_document(documents):
     places = jnp.arange(documents.shape[0])
     return (documents[:, None] == documents[None, :]) & (places[:, None] >= places[None, :])
+
+
+def rotate_some(values, places, first_pair, pairs):
+    half = values.shape[-1] // 2
+    freqs = ROPE_BASE ** (-(first_pair + jnp.arange(half)).astype(F32) / pairs)
+    angles = places[:, None] * freqs[None, :]
+    cosine, sine = jnp.cos(angles), jnp.sin(angles)
+    first, second = values[:, :half], values[:, half:]
+    return jnp.concatenate(
+        [first * cosine - second * sine, second * cosine + first * sine], axis=-1
+    )
 
 
 def ssm_terms(step, rate, documents, chunks):
@@ -991,11 +1482,15 @@
     entry = jnp.where((docs_c == prior[:, None])[:, None], jnp.exp(level), 0.0)
     tail = jnp.where((docs_c == last[:, None])[:, None], jnp.exp(level[:, :, -1:] - level), 0.0)
     carry = jnp.exp(level[:, :, -1]) * (last == prior).astype(F32)[:, None]
-    return step_c, pair, entry, tail, carry
+    k, j, i = (jnp.arange(chunks).reshape(shape) for shape in ((-1, 1, 1), (1, -1, 1), (1, 1, -1)))
+    between = ((j < i) & (i < k))[..., None]
+    reach = jnp.prod(jnp.where(between, carry[None, None], 1.0), axis=2)
+    reach = jnp.where((j < k), reach, 0.0)
+    return step_c, pair, entry, tail, carry, reach
 
 
 def ssm_forward(xin, write, read, terms, skip):
-    step_c, pair, entry, tail, carry = terms
+    step_c, pair, entry, tail, carry, reach = terms
     chunks, heads, rows = step_c.shape
     x_c = xin.reshape(chunks, rows, heads, HP)
     write_c = write.reshape(chunks, rows, STATE)
@@ -1006,12 +1501,7 @@
     weight = (tail * step_c).transpose(0, 2, 1)
     weighted = (x_c.astype(F32) * weight[..., None]).astype(BF)
     local = jnp.einsum("kthp,ktn->khpn", weighted, write_c, preferred_element_type=F32)
-    state = jnp.zeros_like(local[0])
-    entering = []
-    for k in range(chunks):
-        entering.append(state)
-        state = carry[k][:, None, None] * state + local[k]
-    entering = jnp.stack(entering)
+    entering = jnp.sum(reach[:, :, :, None, None] * local[None], axis=1)
     reached = jnp.einsum(
         "ktn,khpn->kthp", read_c, entering.astype(BF), preferred_element_type=F32
     )
@@ -1024,7 +1514,7 @@
 
 
 def ssm_backward(grad, xin, write, read, terms, skip, rate, saved):
-    step_c, pair, entry, tail, carry = terms
+    step_c, pair, entry, tail, carry, reach = terms
     gram, mixing, entering, reached = saved
     chunks, heads, rows = step_c.shape
     x_c = xin.reshape(chunks, rows, heads, HP)
@@ -1054,12 +1544,7 @@
         "kthp,khpn->ktn", g_reached, entering.astype(BF), preferred_element_type=F32
     )
     g_enter = jnp.einsum("kthp,ktn->khpn", g_reached, read_c, preferred_element_type=F32)
-    state = jnp.zeros_like(g_enter[0])
-    leaving = [None] * chunks
-    for k in reversed(range(chunks)):
-        leaving[k] = state
-        state = carry[k][:, None, None] * state + g_enter[k]
-    leaving = jnp.stack(leaving)
+    leaving = jnp.sum(reach.transpose(1, 0, 2)[:, :, :, None, None] * g_enter[None], axis=1)
     g_carry = jnp.sum(entering * leaving, axis=(2, 3))
     leaving_low = leaving.astype(BF)
     weight = tail * step_c
@@ -1128,9 +1613,14 @@
     ff = gate_weight.shape[1] // ctx
     head = HEAD_SIZE * QUERY_HEADS // ctx
     taps = CONV - 1
-    step_pad = 128 - bc % 128
 
     ids = itertools.count(1)
+
+    def to_shards(x):
+        return x.reshape(-1, ctx, seqs, krows).transpose(0, 2, 1, 3).reshape(-1, width)
+
+    def from_shards(x):
+        return x.reshape(-1, seqs, ctx, krows).transpose(0, 2, 1, 3).reshape(-1, width)
 
     small = jnp.concatenate(
         [
@@ -1140,15 +1630,51 @@
             conv_bias,
             conv_weight.reshape(-1),
             doc_ids[0].astype(BF),
+            step_weight.reshape(-1),
         ]
     )
     small_size = small.size
     tile_rows = -(-small_size // 2048) * 16
     small = jnp.pad(small, (0, tile_rows * 128 - small_size)).reshape(tile_rows, 128)
-    small = small_gather(small, seqs, ids).reshape(ctx * seqs, -1)
+
+    def by_column(weight, n):
+        return weight.reshape(krows, ctx, n).transpose(1, 0, 2)
+
+    kv_repeat = ctx // KEY_VALUE_HEADS
+    kv = HEAD_SIZE // kv_repeat
+    half = kv // 2
+    key_pack = (
+        key_matrix.reshape(krows, KEY_VALUE_HEADS, 2, kv_repeat, half)
+        .transpose(1, 3, 0, 2, 4)
+        .reshape(ctx, krows, kv)
+    )
+    mixed_pack = jnp.concatenate(
+        [by_column(conv_in_weight[:, dssm:], bc), key_pack, by_column(value_matrix, kv)], axis=2
+    )
+    conv_cols = inner + bc + 2 * kv
+    rest_cols = head + inner
+    resid = hidden_in[0].astype(F32)
+    scale_one = lax.rsqrt(jnp.mean(resid * resid, axis=-1, keepdims=True) + EPSILON)
+    hat_one = resid * scale_one
+    small, out_own, normed, grad_all, _, rest_pack, ffn_pack, conv_in_own = opening(
+        small,
+        jnp.concatenate([attn_out_weight, mamba_out_weight]),
+        to_shards(hat_one.astype(BF)),
+        out_grad[0],
+        query_weight,
+        mixer_gate_weight,
+        conv_in_weight,
+        mixed_pack,
+        gate_weight,
+        up_weight,
+        seqs,
+        ids,
+    )
+    conv_in_own = conv_in_own.reshape(width, conv_cols)
+    small = small.reshape(ctx * seqs, -1)
     cuts = []
     at = 0
-    for n in (norm_gain.size, ffn_gain.size, mixer_gain.size, conv_bias.size, conv_weight.size, tokens):
+    for n in (norm_gain.size, ffn_gain.size, mixer_gain.size, conv_bias.size, conv_weight.size, tokens, step_weight.size):
         cuts.append(small[:, at : at + n])
         at += n
     gain_one = cuts[0].reshape(-1).astype(F32)
@@ -1175,69 +1701,31 @@
     decay_own = lax.dynamic_slice_in_dim(log_decay, me * heads, heads)
     skip_own = lax.dynamic_slice_in_dim(skip_gain, me * heads, heads)
 
-    def by_column(weight, n):
-        return weight.reshape(krows, ctx, n).transpose(1, 0, 2)
-
-    kv_repeat = ctx // KEY_VALUE_HEADS
-    conv_pack = jnp.concatenate(
-        [
-            by_column(conv_in_weight[:, :dssm], inner),
-            by_column(conv_in_weight[:, dssm:], bc),
-            jnp.pad(by_column(step_weight, heads), ((0, 0), (0, 0), (0, step_pad - heads))),
-        ],
-        axis=2,
-    )
-    rest_pack = jnp.concatenate(
-        [
-            by_column(query_weight, head),
-            jnp.repeat(
-                key_matrix.reshape(krows, KEY_VALUE_HEADS, HEAD_SIZE).transpose(1, 0, 2),
-                kv_repeat,
-                axis=0,
-            ),
-            jnp.repeat(
-                value_matrix.reshape(krows, KEY_VALUE_HEADS, HEAD_SIZE).transpose(1, 0, 2),
-                kv_repeat,
-                axis=0,
-            ),
-            by_column(mixer_gate_weight, inner),
-        ],
-        axis=2,
-    )
-    ffn_pack = jnp.concatenate([by_column(gate_weight, ff), by_column(up_weight, ff)], axis=2)
-    conv_cols = conv_pack.shape[2]
-    rest_cols = rest_pack.shape[2]
-    mixer_pack = swap_columns(jnp.concatenate([conv_pack, rest_pack], axis=2))
-    ffn_pack = swap_columns(after(ffn_pack, mixer_pack))
-    conv_in_own = gather_rows(mixer_pack[:, :, :conv_cols])
-    rest_own = gather_rows(after(mixer_pack[:, :, conv_cols:], conv_in_own))
-    out_own = gather_rows(after(jnp.concatenate([attn_out_weight, mamba_out_weight]), rest_own))
-    ffn_own = gather_rows(after(ffn_pack, out_own))
-    down_own = gather_rows(after(down_weight, ffn_own)).reshape(ff, width)
-    conv_in_own = conv_in_own.reshape(width, conv_cols)
-    rest_own = rest_own.reshape(width, rest_cols)
+    rest_own = gather_rows(rest_pack).reshape(width, rest_cols)
     out_rows = attn_out_weight.shape[0]
-    attn_out_own = out_own[:, :out_rows].reshape(head, width)
-    mamba_out_own = out_own[:, out_rows:].reshape(inner, width)
-    ffn_own = ffn_own.reshape(width, 2 * ff)
-
-    def to_shards(x):
-        return x.reshape(-1, ctx, seqs, krows).transpose(0, 2, 1, 3).reshape(-1, width)
-
-    def from_shards(x):
-        return x.reshape(-1, seqs, ctx, krows).transpose(0, 2, 1, 3).reshape(-1, width)
-
-    resid = hidden_in[0].astype(F32)
-    scale_one = lax.rsqrt(jnp.mean(resid * resid, axis=-1, keepdims=True) + EPSILON)
-    normed = gather_tokens(to_shards((resid * scale_one * gain_one).astype(BF)), ids)
+    out_own = jnp.concatenate(
+        [out_own[:, :out_rows].reshape(head, width), out_own[:, out_rows:].reshape(inner, width)]
+    )
+    ffn_own = gather_rows(ffn_pack).reshape(width, 2 * ff)
+    down_own = gather_rows(down_weight).reshape(ff, width)
+    step_own = lax.dynamic_slice_in_dim(
+        cuts[6].reshape(ctx, seqs, krows, HS).transpose(1, 0, 2, 3).reshape(width, HS),
+        me * heads,
+        heads,
+        1,
+    )
+    step_room = ((0, 0), (0, 128 - heads))
+    step_wide = jnp.pad(step_own, step_room)
+
+    normed = (normed.astype(F32) * to_shards(gain_one[None])).astype(BF)
     conv_all = mm(normed, conv_in_own)
     rest_all = mm(normed, rest_own)
     conv_lin = conv_all[:, : inner + bc].astype(BF).astype(F32)
-    step_lin = conv_all[:, inner + bc : inner + bc + heads]
+    k_lin = conv_all[:, inner + bc : inner + bc + kv]
+    v_lin = conv_all[:, inner + bc + kv :]
+    step_lin = mm(normed, step_own)
     q_lin = rest_all[:, :head]
-    k_lin = rest_all[:, head : head + HEAD_SIZE]
-    value = rest_all[:, head + HEAD_SIZE : head + 2 * HEAD_SIZE].astype(BF)
-    zgate = rest_all[:, head + 2 * HEAD_SIZE :]
+    zgate = rest_all[:, head:]
 
     widened = jnp.concatenate([jnp.zeros((taps, inner + bc), F32), conv_lin], axis=0)
     widened_docs = jnp.concatenate([jnp.full((taps,), -1, jnp.int32), documents])
@@ -1248,19 +1736,33 @@
         conv_shift,
     )
     conv_act = conv_act.astype(BF)
-    shared = gather_tokens(conv_act[:, inner:].T, ids, 2).T
-    write, read = shared[:, :STATE], shared[:, STATE:]
+    places = jnp.arange(length).astype(F32)
+    first_pair = (me % kv_repeat) * half
+    key_turned, unturn_key = jax.vjp(
+        lambda lin: rotate_some(lin, places, first_pair, HEAD_SIZE // 2), k_lin
+    )
+    shared = jnp.concatenate(
+        [conv_act[:, inner:], key_turned.astype(BF), v_lin.astype(BF)], axis=1
+    ).T
+    shared = gather_tokens(shared, ids, 2).reshape(ctx, bc + 2 * kv, length)
+    write_read = shared[:, :bc].reshape(2 * STATE, length).T
+    write, read = write_read[:, :STATE], write_read[:, STATE:]
+    group = me // kv_repeat * kv_repeat
+    own_kv = lax.dynamic_slice_in_dim(shared[:, bc:], group, kv_repeat, 0)
+    key = (
+        own_kv[:, :kv]
+        .reshape(kv_repeat, 2, half, length)
+        .transpose(1, 0, 2, 3)
+        .reshape(HEAD_SIZE, length)
+        .T
+    )
+    value = own_kv[:, kv:].reshape(HEAD_SIZE, length).T
     xin = conv_act[:, :inner]
 
-    places = jnp.arange(length).astype(F32)
     query_turned, unturn = jax.vjp(
         partial(rotate, places=places), q_lin.reshape(length, head // HEAD_SIZE, HEAD_SIZE)
     )
-    key_turned, unturn_key = jax.vjp(
-        partial(rotate, places=places), k_lin.reshape(length, 1, HEAD_SIZE)
-    )
     query = query_turned.astype(BF)
-    key = key_turned.astype(BF)[:, 0]
     visible = same_document(documents)
     scores = jnp.einsum("thd,ud->htu", query, key, preferred_element_type=F32) * HEAD_SIZE**-0.5
     scores = jnp.where(visible[None], scores, NEGATIVE_FLOOR)
@@ -1283,11 +1785,11 @@
     scale_mix = lax.rsqrt(mean_square + EPSILON)[:, None]
     ymix = (gated * scale_mix * gain_mix).astype(BF)
 
-    branch = scatter_tokens(mm(attn_low, attn_out_own) + mm(ymix, mamba_out_own), ids)
+    mixed = jnp.concatenate([attn_low, ymix], axis=1)
+    branch = scatter_tokens(mm(mixed, out_own), ids)
     mid = resid + branch
     scale_two = lax.rsqrt(jnp.mean(mid * mid, axis=-1, keepdims=True) + EPSILON)
     normed_two = gather_tokens(to_shards((mid * scale_two * gain_two).astype(BF)), ids)
-    grad_all = gather_tokens(out_grad[0], ids)
 
     gate_up = mm(normed_two, ffn_own)
     gate_lin, up_lin = gate_up[:, :ff], gate_up[:, ff:]
@@ -1300,31 +1802,31 @@
     ).astype(BF)
     grad_up = (grad_hidden * silu_gate).astype(BF)
     grad_gu = jnp.concatenate([grad_gate, grad_up], axis=1)
-    grad_n2 = from_shards(scatter_tokens(mm_nt(grad_gu, ffn_own), ids))
-    block_out = (mid + scatter_tokens(mm(hidden, down_own), ids)).astype(BF)
     down_grad = scatter_rows(mm_tn(hidden, grad_all).reshape(seqs, ff // seqs, width))
     ffn_grad = mm_tn(normed_two, grad_gu).reshape(seqs, ctx, krows, 2 * ff).astype(BF)
-    ffn_grad = scatter_rows(after(ffn_grad, down_grad))
+    grad_n2 = scatter_tokens(mm_nt(grad_gu, ffn_own), ids, (ffn_grad,), seqs=seqs)
+    ffn_grad = scatter_rows(ffn_grad)
 
     turned = grad_n2 * gain_two
     hat_two = mid * scale_two
-    ffn_gain_grad = jnp.sum(grad_n2 * hat_two, axis=0)
+    ffn_gain_grad = jnp.sum(grad_n2 * hat_two, axis=0, keepdims=True)
     grad_mid = out_grad[0].astype(F32) + scale_two * (
         turned - hat_two * jnp.mean(turned * hat_two, axis=-1, keepdims=True)
     )
-    branch_grad = gather_tokens(grad_mid.astype(BF), ids)
-
-    out_grad_own = jnp.concatenate(
+    branch_grad = hold(gather_tokens(grad_mid.astype(BF), ids), down_grad)
+
+    out_grad_own = mm_tn(mixed, branch_grad).astype(BF)
+    out_part = jnp.concatenate(
         [
-            mm_tn(attn_low, branch_grad).reshape(seqs, -1, width),
-            mm_tn(ymix, branch_grad).reshape(seqs, -1, width),
+            out_grad_own[:head].reshape(seqs, -1, width),
+            out_grad_own[head:].reshape(seqs, -1, width),
         ],
         axis=1,
-    ).astype(BF)
-    out_grad_own = scatter_rows(after(out_grad_own, ffn_grad)).astype(F32)
-    attn_out_grad, mamba_out_grad = out_grad_own[:out_rows], out_grad_own[out_rows:]
-    grad_attn = mm_nt(branch_grad, attn_out_own).astype(BF).reshape(length, -1, HEAD_SIZE)
-    grad_ymix = mm_nt(branch_grad, mamba_out_own)
+    )
+    out_grad_own = scatter_rows(hold(out_part, ffn_grad))
+    grad_mixed = mm_nt(branch_grad, out_own)
+    grad_attn = grad_mixed[:, :head].astype(BF).reshape(length, -1, HEAD_SIZE)
+    grad_ymix = grad_mixed[:, head:]
 
     grad_prob = jnp.einsum("thd,ud->htu", grad_attn, value, preferred_element_type=F32)
     delta = jnp.sum(probs * grad_prob, axis=-1, keepdims=True)
@@ -1337,129 +1839,112 @@
     )
     grad_value = jnp.einsum("htu,thd->ud", probs_low, grad_attn, preferred_element_type=F32)
     grad_q_lin = unturn(grad_query)[0].reshape(length, head).astype(BF)
-    grad_k_lin = unturn_key(grad_key[:, None])[0].reshape(length, HEAD_SIZE).astype(BF)
 
     hat = gated * scale_mix
     turned_mix = grad_ymix * gain_mix
-    mixer_gain_grad = jnp.sum(grad_ymix * hat, axis=0)
-    along = row_sum(jnp.sum(turned_mix * hat, axis=-1), ids)[:, None] / dssm
+    mixer_gain_grad = jnp.sum(grad_ymix * hat, axis=0, keepdims=True)
+    along = row_sum(jnp.sum(turned_mix * hat, axis=-1), ids, (down_grad,))[:, None] / dssm
     grad_gated = scale_mix * (turned_mix - hat * along)
     grad_y, grad_zgate = gated_back(grad_gated)
 
+    grad_rest = jnp.concatenate([grad_q_lin, grad_zgate.astype(BF)], axis=1)
+    rest_part = mm_tn(normed, grad_rest).reshape(seqs, ctx, krows, rest_cols).astype(BF)
+
     grad_xin, grad_write, grad_read, grad_step, grad_rate, skip_grad = ssm_backward(
         grad_y, xin, write, read, terms, skip_own, rate, saved
     )
+    grad_key = (
+        grad_key.T.reshape(2, kv_repeat, half, length)
+        .transpose(1, 0, 2, 3)
+        .reshape(kv_repeat, kv, length)
+    )
+    grad_kv = jnp.concatenate([grad_key, grad_value.T.reshape(kv_repeat, kv, length)], axis=1)
+    grad_kv = lax.dynamic_update_slice_in_dim(
+        jnp.zeros((ctx, 2 * kv, length), BF), grad_kv.astype(BF), group, 0
+    )
     grad_shared = jnp.concatenate([grad_write, grad_read], axis=1).astype(BF)
-    grad_shared = scatter_tokens(grad_shared.T, ids).T
+    grad_shared = jnp.concatenate([grad_shared.T.reshape(ctx, bc, length), grad_kv], axis=1)
+    grad_shared, last = scatter_two(
+        grad_shared.reshape(ctx * (bc + 2 * kv), length),
+        mm(hidden, down_own).astype(BF),
+        ids,
+        (ffn_grad, rest_part),
+    )
+    block_out = (mid + last).astype(BF)
+    grad_shared = grad_shared.T
+    grad_k_lin = unturn_key(grad_shared[:, bc : bc + kv])[0].astype(BF)
+    grad_v_lin = grad_shared[:, bc + kv :].astype(BF)
+    grad_shared = grad_shared[:, :bc]
     grad_widened, taps_grad, shift_grad = conv_back(
         jnp.concatenate([grad_xin, grad_shared], axis=1)
     )
     grad_step_lin, step_bias_grad = step_back(grad_step)
     log_decay_grad = grad_rate * rate
     grad_conv = jnp.concatenate(
-        [
-            grad_widened[taps:].astype(BF),
-            jnp.pad(grad_step_lin.astype(BF), ((0, 0), (0, step_pad - heads))),
-        ],
-        axis=1,
-    )
-    grad_rest = jnp.concatenate(
-        [grad_q_lin, grad_k_lin, grad_value.astype(BF), grad_zgate.astype(BF)], axis=1
-    )
-
-    grad_normed = from_shards(
-        scatter_tokens(mm_nt(grad_conv, conv_in_own) + mm_nt(grad_rest, rest_own), ids)
-    )
-    rest_grad = mm_tn(normed, grad_rest).reshape(seqs, ctx, krows, rest_cols).astype(BF)
-    rest_grad = scatter_rows(after(rest_grad, out_grad_own))
-    conv_grad = mm_tn(normed, grad_conv).reshape(seqs, ctx, krows, conv_cols).astype(BF)
-    conv_grad = scatter_rows(after(conv_grad, rest_grad))
-    ffn_grad = swap_columns(ffn_grad).astype(F32)
-    mixer_grad = swap_columns(jnp.concatenate([conv_grad, rest_grad], axis=2)).astype(F32)
+        [grad_widened[taps:].astype(BF), grad_k_lin, grad_v_lin], axis=1
+    )
+    grad_step_low = grad_step_lin.astype(BF)
+    step_grad = mm_tn(grad_step_low, normed)
+    rest_grad = scatter_rows(rest_part)
+    conv_grad = mm_tn(normed, grad_conv).reshape(seqs, ctx, krows, conv_cols)
+    conv_grad = scatter_rows(conv_grad)
+    grad_normed, norm_rows, query_grad, zgate_grad, gate_grad, up_grad = closing(
+        (grad_conv, grad_rest, jnp.pad(grad_step_low, step_room)),
+        (conv_in_own, rest_own, step_wide),
+        rest_grad,
+        ffn_grad,
+        hat_one,
+        head,
+        seqs,
+        ids,
+        (out_grad_own,),
+    )
+
+    sums, step_sums, channels_grad, key_grad, value_grad = last_exchange(
+        (
+            norm_rows,
+            ffn_gain_grad,
+            mixer_gain_grad,
+            jnp.concatenate([shift_grad[None], taps_grad]),
+            jnp.stack([step_bias_grad, log_decay_grad, skip_grad]),
+            step_grad,
+        ),
+        conv_grad,
+        inner,
+        kv,
+        seqs,
+        ids,
+    )
+    step_grad = step_sums[:, :heads, :krows].reshape(HS, krows).T
+
     turned_one = grad_normed * gain_one
-    hat_one = resid * scale_one
-    norm_gain_grad = jnp.sum(grad_normed * hat_one, axis=0)
     input_grad = (
         grad_mid
         + scale_one
         * (turned_one - hat_one * jnp.mean(turned_one * hat_one, axis=-1, keepdims=True))
     ).astype(BF)
 
-    def spread_out(own, at, total):
-        return lax.dynamic_update_slice_in_dim(
-            jnp.zeros(own.shape[:-1] + (total,), F32), own, at, own.ndim - 1
-        )
-
-    def spread_channels(own):
-        full = spread_out(own[..., :inner], me * inner, dssm + 2 * STATE)
-        return lax.dynamic_update_slice_in_dim(full, own[..., inner:], dssm + me * bc, own.ndim - 1)
-
-    parts = (
-        norm_gain_grad,
-        ffn_gain_grad,
-        spread_out(mixer_gain_grad, me * inner, dssm),
-        spread_channels(shift_grad),
-        spread_channels(taps_grad).reshape(-1),
-        spread_out(step_bias_grad, me * heads, HS),
-        spread_out(log_decay_grad, me * heads, HS),
-        spread_out(skip_grad, me * heads, HS),
-    )
-    place = (ctx, seqs)
-    tiles = [part.reshape(place + (-1,)) for part in parts[:4]]
-    tiles.append(parts[4].reshape((CONV,) + place + (-1,)).transpose(1, 2, 0, 3).reshape(place + (-1,)))
-    tiles.append(
-        jnp.broadcast_to(jnp.concatenate(parts[5:]), place + (3 * HS,))
-    )
-    sizes = [tile.shape[-1] for tile in tiles]
-    tile_rows = -(-sum(sizes) // 1024) * 8
-    tiles = jnp.concatenate(tiles, axis=-1)
-    tiles = jnp.pad(tiles, ((0, 0), (0, 0), (0, tile_rows * 128 - sum(sizes))))
-    sums = small_scatter(tiles.reshape(place + (tile_rows, 128)), ids).reshape(-1)
-    pieces = []
-    at = 0
-    for size in sizes:
-        pieces.append(sums[at : at + size])
-        at += size
-    per_head = pieces[5].reshape(3, HS)
-
-    def by_row(packed, start, n):
-        return packed[:, :, start : start + n].transpose(1, 0, 2).reshape(krows, -1)
-
-    base = conv_cols
-    key_grad = mixer_grad[:, :, base + head : base + head + HEAD_SIZE]
-    value_grad = mixer_grad[:, :, base + head + HEAD_SIZE : base + head + 2 * HEAD_SIZE]
-
-    def over_queries(packed):
-        return (
-            packed.reshape(KEY_VALUE_HEADS, kv_repeat, krows, HEAD_SIZE)
-            .sum(axis=1)
-            .transpose(1, 0, 2)
-            .reshape(krows, -1)
-        )
-
     return (
         block_out[None],
         input_grad[None],
-        pieces[0],
-        by_row(mixer_grad, base, head),
-        over_queries(key_grad),
-        over_queries(value_grad),
-        attn_out_grad,
-        by_row(mixer_grad, base + head + 2 * HEAD_SIZE, inner),
-        jnp.concatenate(
-            [by_row(mixer_grad, 0, inner), by_row(mixer_grad, inner, bc)], axis=1
-        ),
-        by_row(mixer_grad, inner + bc, heads),
-        pieces[4].reshape(CONV, -1),
-        pieces[3],
-        per_head[0],
-        per_head[1],
-        per_head[2],
-        pieces[2],
-        mamba_out_grad,
-        pieces[1],
-        by_row(ffn_grad, 0, ff),
-        by_row(ffn_grad, ff, ff),
+        sums[1, :krows],
+        query_grad.astype(F32),
+        key_grad,
+        value_grad,
+        out_grad_own[:out_rows].astype(F32),
+        zgate_grad.astype(F32),
+        channels_grad.astype(F32),
+        step_grad,
+        sums[4 : 4 + CONV, : conv_weight.shape[1]],
+        sums[3, : conv_bias.size],
+        sums[8, :HS],
+        sums[9, :HS],
+        sums[10, :HS],
+        sums[2, : mixer_gain.size],
+        out_grad_own[out_rows:].astype(F32),
+        sums[0, :krows],
+        gate_grad.astype(F32),
+        up_grad.astype(F32),
         down_grad.astype(F32),
     )
 

time: 696 us -> 593 us (0.85)
  waiting for transfers between devices: 115 us -> 19.6 us
  Pallas kernels: 238 us -> 283 us
  blocking collectives: 41.6 us -> 0 us
  other arithmetic: 60.7 us -> 83 us
  matrix products: 121 us -> 110 us
  starting transfers between devices: 9.2 us -> 0.71 us
  local copies, waits for them, and re-layouts: 82.9 us -> 75.3 us
    reduce_scatter x5, waiting for transfers between devices: 88.9 us -> 0.08 us  [scatter_rows(): lax.psum_scatter(partial_sum.astype(BF), FSDP, scatter_dimension=0, tiled...]
    pallas_call x14 -> x13, Pallas kernels: 238 us -> 283 us  [the longest x1 80.6 us: opening(): pl.pallas_call(partial(opening_kernel, seqs, pieces), out_shape=(shape(PL...]
    all_to_all x2 -> x0, blocking collectives: 41.6 us -> none  [swap_columns(): return lax.all_to_all(packed, CTX, split_axis=0, concat_axis=0, tiled=True)]
    reshape x28 -> x9, local copies, waits for them, and re-layouts: 28.1 us -> 6.7 us  [the longest x1 3.01 us: ssm_backward(): gx.reshape(length, heads * HP)]
    all_to_all x2 -> x0, starting transfers between devices: 8.55 us -> none  [swap_columns(): return lax.all_to_all(packed, CTX, split_axis=0, concat_axis=0, tiled=True)]
    all_gather x5 -> x3, waiting for transfers between devices: 25.5 us -> 18.1 us  [gather_rows(): return lax.all_gather(shard, FSDP, axis=0, tiled=False)]
    dot_general x18 -> x15, matrix products: 88 us -> 81.6 us  [dotf(): lax.dot_general(left, right, (dims, ((), ())), preferred_element_type=F32)]
    unnamed x350 -> x342, local copies, waits for them, and re-layouts: 25.1 us -> 29.1 us
  transfers between devices with their start and end apart: 12 -> 8, of which waited for: 4 -> 1; matrix products, arithmetic and copies ran while one was open for 28% -> 36% of each run, Pallas kernels for 27% -> 32%
where the time goes in v3:
time: 593 us; the launch traced here: 588 us
  Pallas kernels  283 us (48%)
  matrix products  110 us (19%)
  other arithmetic  83 us (14%)
  local copies, waits for them, and re-layouts  75.3 us (13%)
  waiting for transfers between devices  19.6 us (3%)
  between operations  16.7 us (3%)
    dot_general x15, matrix products, dotf(): lax.dot_general(left, right, (dims, ((), ())), preferred_element_type=F32)  81.6 us
    pallas_call x1, Pallas kernels, opening(): pl.pallas_call(partial(opening_kernel, seqs, pieces), out_shape=(shape(PL...  80.6 us
    pallas_call x3, Pallas kernels, gather_tokens(): pl.pallas_call(unused(partial(gather_kernel, pieces), 1, len(waits)), out...  57.7 us
    pallas_call x2, Pallas kernels, scatter_tokens(): pl.pallas_call(unused(partial(scatter_kernel, seqs), 1, len(waits)), out_...  45.2 us
    pallas_call x1, Pallas kernels, closing(): pl.pallas_call(unused(partial(closing_kernel, seqs), 9, len(waits)), out_...  41.9 us
    pallas_call x1, Pallas kernels, scatter_two(): pl.pallas_call(unused(scatter_two_kernel, 2, len(waits)), out_shape=tuple...  30.7 us
    unnamed x342, local copies, waits for them, and re-layouts  29.1 us
    all_gather x3, waiting for transfers between devices, gather_rows(): return lax.all_gather(shard, FSDP, axis=0, tiled=False)  18.1 us
  transfers between devices with their start and end apart: 8, of which 1 were waited for; matrix products, arithmetic and copies ran while one was open for 36% of the time, Pallas kernels for 32%

profile of v3, /device:TPU:0, one launch (start us, length us, event | category | flops | bytes accessed | tf_op | source)
XLA Modules:
  0.0 588.0 jit_solution(7946689218201506512)
XLA Ops:
  14.6 80.6 %shard_map.373 = (bf16[8,4,32,128]{3,2,1,0:T(8,128)(2,1)}, bf16[4,128,2048]{2,1,0:T(8,128)(2,1)}, bf16[1024,2048]{1,0:T(8,128)(2,1)}, bf16[1024,2048]{1,0:T(8,12...) custom-call(bf16[32,128]{1,0:T(8,128)(2,1)} %pad_bitcast_fusion.refs, ...), custom_call_target="tpu_custom_call" | custom-call | flops 20999999488 | bytes 21000000 | tf_op jit(solution)/shard_map/pallas_call | solution.py:1120
  98.1 6.8 %fusion.138 = (bf16[1024,512]{1,0:T(8,128)(2,1)S(1)}, f32[1024,512]{1,0:T(8,128)}) fusion(bf16[2048,512]{1,0:T(8,128)(2,1)} %bitcast.490, bf16[1024,2048]{1,0:T(8,128)(2,1)} %get-tuple-element.54, f32[2048]{0:T(1024)S(1)} %reshape.800), kind=kOutput, calls=%fused_computation.303 | convolution fusion | flops 2154299392 | bytes 9445376 | tf_op jit(solution)/shard_map/dot_general | solution.py:611
  108.6 3.2 multiply_convert_fusion.5
  113.9 4.5 compare_select_fusion.2
  118.8 1.7 reduce_window_sum.17
  126.0 3.8 fusion.74
  132.0 13.5 %shard_map.374 = bf16[1024,1024]{1,0:T(8,128)(2,1)} custom-call(bf16[128,1024]{1,0:T(8,128)(2,1)} %copy.377.refs_0_), custom_call_target="tpu_custom_call" | custom-call | flops 2400000000 | bytes 2400000 | tf_op jit(solution)/shard_map/pallas_call | solution.py:818
  145.5 2.0 fusion.135
  156.8 3.1 multiply_reduce_fusion.1
  161.6 1.5 fusion.22
  165.1 5.6 fusion.19
  172.8 6.1 %shard_map.375 = f32[8,128]{1,0:T(8,128)} custom-call(f32[8,128]{1,0:T(8,128)} %bitcast.482), custom_call_target="tpu_custom_call" | custom-call | flops 1500000000 | bytes 1500000 | tf_op jit(solution)/shard_map/pallas_call | solution.py:978
  179.6 2.8 fusion.98
  183.7 1.8 fusion.7
  185.7 1.6 fusion.41
  187.6 1.5 copy-done.54
  189.2 2.4 convolution_convert_fusion.1.refs_0_
  191.6 22.2 %shard_map.376 = f32[128,2048]{1,0:T(8,128)S(1)} custom-call(bf16[1024,2048]{1,0:T(8,128)(2,1)S(1)} %convolution_convert_fusion.1.refs_0_), custom_call_target="tpu_custom_call" | custom-call | flops 6600000000 | bytes 6600000 | tf_op jit(solution)/shard_map/pallas_call | solution.py:944
  216.7 21.9 %shard_map.377 = bf16[1024,2048]{1,0:T(8,128)(2,1)} custom-call(bf16[128,2048]{1,0:T(8,128)(2,1)} %copy.406.refs_0_), custom_call_target="tpu_custom_call" | custom-call | flops 6600000000 | bytes 6600000 | tf_op jit(solution)/shard_map/pallas_call | solution.py:818
  238.6 10.1 %fusion.141 = f32[1024,1024]{0,1:T(8,128)} fusion(bf16[1024,2048]{1,0:T(8,128)(2,1)} %shard_map.377, bf16[2048,1024]{1,0:T(8,128)(2,1)} %bitcast.485), kind=kOutput, calls=%fused_computation.306 | convolution fusion | flops 4294967296 | bytes 12582912 | tf_op jit(solution)/shard_map/dot_general | solution.py:611
  248.7 18.0 %all-gather.9.cloned.1.call-done = bf16[512,2048]{1,0:T(8,128)(2,1)} async-done(((bf16[128,2048]{1,0:T(8,128)(2,1)}), bf16[512,2048]{1,0:T(8,128)(2,1)}) %all-gather.9.cloned.1.call-update) | async-done | bytes 2097168 | tf_op jit(solution)/shard_map/all_gather | solution.py:1429
  266.7 8.1 %multiply_convert_fusion.4 = (bf16[1024,512]{0,1:T(8,128)(2,1)S(1)}, bf16[1024,512]{0,1:T(8,128)(2,1)}, bf16[1024,512]{0,1:T(8,128)(2,1)S(1)}) fusion(f32[1024,1024]{0,1:T(8,128)} %fusion.141, bf16[1024,2048]{1,0:T(8,128)(2,1)} %get-tuple-element.58, bf16[512,2048]{1,0:T(8,128)(2,1)} %all-gather.9.cloned.1.call-done), kind=kOutput, calls=%fused_computation.57 | convolution fusion | flops 2154823680 | bytes 13631488 | tf_op jit(solution)/shard_map/dot_general | solution.py:611
  274.9 3.6 convolution_convert_fusion.7
  279.3 9.0 %convolution_convert_fusion.2 = bf16[2048,1024]{1,0:T(8,128)(2,1)} fusion(bf16[1024,2048]{1,0:T(8,128)(2,1)} %shard_map.377, bf16[1024,512]{0,1:T(8,128)(2,1)} %get-tuple-element.97, bf16[1024,512]{0,1:T(8,128)(2,1)S(1)} %get-tuple-element.96), kind=kOutput, calls=%fused_computation.14 | convolution fusion | flops 4301258752 | bytes 10485760 | tf_op jit(solution)/shard_map/dot_general | solution.py:611
  288.4 7.3 %convolution_convert_fusion.3.refs_0_ = bf16[1024,2048]{1,0:T(8,128)(2,1)S(1)} fusion(bf16[2048,1024]{1,0:T(8,128)(2,1)} %bitcast.486, bf16[1024,512]{0,1:T(8,128)(2,1)} %get-tuple-element.97, bf16[1024,512]{0,1:T(8,128)(2,1)S(1)} %get-tuple-element.96), kind=kOutput, calls=%fused_computation.15 | convolution fusion | flops 4301258752 | bytes 10485760 | tf_op jit(solution)/shard_map/dot_general | solution.py:611
  295.7 23.0 %shard_map.378 = f32[128,2048]{1,0:T(8,128)S(1)} custom-call(bf16[1024,2048]{1,0:T(8,128)(2,1)S(1)} %convolution_convert_fusion.3.refs_0_, bf16[4,8,64,1024]{3,2,1,0:T(8,128)(2,1)S(1)} %bitcast.363), custom_call_target="tpu_custom_call" | custom-call | flops 6600000000 | bytes 6600000 | tf_op jit(solution)/shard_map/pallas_call | solution.py:944
  320.3 4.5 convolution_convert_fusion.refs_1_
  325.9 22.3 %shard_map.379.refs_0_ = bf16[1024,2048]{1,0:T(8,128)(2,1)} custom-call(bf16[128,2048]{1,0:T(8,128)(2,1)} %fusion.129.refs_0_), custom_call_target="tpu_custom_call" | custom-call | flops 6600000000 | bytes 6600000 | tf_op jit(solution)/shard_map/pallas_call | solution.py:818
  348.2 1.4 copy-done.55
  349.6 4.5 fusion.29
  355.7 1.6 copy.455
  357.3 4.0 fusion
  361.4 2.4 fusion.10
  364.8 2.4 fusion.83
  368.6 6.0 %shard_map.381 = f32[8,128]{1,0:T(8,128)} custom-call(f32[8,128]{1,0:T(8,128)} %bitcast.481, bf16[128,2048]{1,0:T(8,128)(2,1)} %bitcast.406), custom_call_target="tpu_custom_call" | custom-call | flops 1500000000 | bytes 1500000 | tf_op jit(solution)/shard_map/pallas_call | solution.py:978
  375.3 4.8 multiply_reduce_fusion.10
  380.1 3.7 convolution_convert_fusion.6
  385.0 4.6 convolution_convert_fusion.5
  389.6 2.2 slice.400
  393.8 1.6 copy.408
  395.4 1.8 copy.459
  397.9 3.1 multiply_reduce_fusion
  402.7 1.4 fusion.27
  405.1 1.5 copy.505
  406.6 3.0 copy.425
  409.6 2.8 convolution_bitcast_fusion.1
  412.4 4.1 multiply_reduce_fusion.5
  418.8 2.3 copy.414
  421.0 3.2 fusion.40
  426.0 3.0 pad_maximum_fusion.4.refs_0_
  430.0 3.6 fusion.37
  435.0 1.4 copy-done.1
  436.7 30.7 %shard_map.382 = (f32[128,1024]{1,0:T(8,128)S(1)}, f32[128,2048]{1,0:T(8,128)S(1)}) custom-call(bf16[1024,1024]{1,0:T(8,128)(2,1)S(1)} %bitcast.366, bf16[1024,2048]{1,0:T(8,128)(2,1)S(1)} %copy-done.6, bf16[8,64,1024]{2,1,0:T(8,128)(2,1)S(1)} %bitcast.369, bf16[4,8,64,512]{3,2,1,0:T(8,128)(2,1)S(1)} %bitcast.365), custom_call_target="tpu_custom_call" | custom-call | flops 8400000000 | bytes 8400000 | tf_op jit(solution)/shard_map/pallas_call | solution.py:1191
  470.8 3.8 fusion.77
  474.9 5.1 multiply_reduce_fusion.8
  483.1 3.8 convolution_convert_fusion.4
  488.9 3.2 multiply_reduce_fusion.2
  492.9 1.9 multiply_reduce_fusion.12
  497.4 1.9 reduce_window_sum.18
  503.9 3.1 fusion.17.step
  508.1 41.9 %shard_map.384 = (f32[128,2048]{1,0:T(8,128)}, f32[8,4,8,128]{3,2,1,0:T(8,128)}, bf16[64,1024]{1,0:T(8,128)(2,1)}, bf16[64,3072]{1,0:T(8,128)(2,1)}, bf16[64,4096]{1,0:T(8,128)(2,1)}, /*index=5*/bf16[64,4096]{1,0:T(8,128)(2,1)}) custom-call(bf16[1024,512]{1,0:T(8,128)(2,1)} %copy-done.59, bf16[1024,512]{1,0:T(8,128)(2,1)} %pad_maximum_fusion.10.refs_1_, ...), custom_call_target="tpu_custom_call" | custom-call | flops 10499999744 | bytes 10500000 | tf_op jit(solution)/shard_map/pallas_call | solution.py:1262
  552.0 14.9 %shard_map.385 = (f32[16,128]{1,0:T(8,128)S(1)}, f32[8,8,128]{2,1,0:T(8,128)S(1)}, bf16[64,3584]{1,0:T(8,128)(2,1)S(1)}, f32[64,256]{1,0:T(8,128)S(1)}, f32[64,256]{1,0:T(8,128)S(1)}) custom-call(f32[8,4,8,128]{3,2,1,0:T(8,128)S(1)} %copy-done.7, f32[1,2048]{1,0:T(1,128)S(1)} %bitcast.371, f32[1,384]{1,0:T(1,128)S(1)} %broadcast_in_dim.216.mixer_gain, ...), custom_call_target="tpu_custom_call" | custom-call | flops 4499999744 | bytes 4500000 | tf_op jit(solution)/shard_map/pallas_call | solution.py:1391
  571.6 2.2 convert_element_type.408
  576.5 1.5 fusion.87
  (540 shorter events, 94.4 us)
Async XLA Ops:
  7.2 157.9 %all-gather.7.cloned.1.call-start = ((), (), s32[]{:S(2)}) async-start(), calls=%async_computation.10 | async-start | bytes 2621440 | tf_op jit(solution)/shard_map/all_gather | solution.py:1429
  95.2 143.4 %all-gather.11.cloned.1.call-start = ((), (), s32[]{:S(2)}) async-start(), calls=%async_computation.12 | async-start | bytes 5242880 | tf_op jit(solution)/shard_map/all_gather | solution.py:1429
  96.0 170.7 %all-gather.9.cloned.1.call-start = ((), (), s32[]{:S(2)}) async-start(), calls=%async_computation.11 | async-start | bytes 2621440 | tf_op jit(solution)/shard_map/all_gather | solution.py:1429
  96.7 251.4 %reduce-scatter.6.cloned.1.call-start = ((), (), s32[]{:S(2)}) async-start(), calls=%async_computation.5 | async-start | bytes 2621440 | tf_op jit(solution)/shard_map/reduce_scatter | solution.py:1433
  97.1 11.2 %copy-start.58 = (bf16[4,8,32,128]{3,1,2,0:T(8,128)(2,1)}, bf16[4,8,32,128]{3,1,2,0:T(8,128)(2,1)S(1)}, u32[]{:S(2)}) copy-start(bf16[4,8,32,128]{3,1,2,0:T(8,128)(2,1)S(1)} %copy.507) | copy-start | bytes 786436
  97.9 6.9 %copy-start.86 = (f32[32,64]{1,0:T(8,128)}, f32[32,64]{1,0:T(8,128)S(1)}, u32[]{:S(2)}) copy-start(f32[32,64]{1,0:T(8,128)S(1)} %get-tuple-element.122) | copy-start | bytes 24580
  98.1 15.9 %copy-start.95 = (f32[2048]{0:T(1024)}, f32[2048]{0:T(1024)S(1)}, u32[]{:S(2)}) copy-start(f32[2048]{0:T(1024)S(1)} %reshape.800) | copy-start | bytes 24580
  105.8 6.0 %copy-start.15 = (f32[1024,448]{1,0:T(8,128)}, f32[1024,448]{1,0:T(8,128)S(1)}, u32[]{:S(2)}) copy-start(f32[1024,448]{1,0:T(8,128)S(1)} %slice_convert_fusion) | copy-start | bytes 5505028
  113.9 10.0 %copy-start.47 = (bf16[4,128,2048]{2,1,0:T(8,128)(2,1)S(1)}, bf16[4,128,2048]{2,1,0:T(8,128)(2,1)}, u32[]{:S(2)}) copy-start(bf16[4,128,2048]{2,1,0:T(8,128)(2,1)} %get-tuple-element.57) | copy-start | bytes 6291460
  118.7 31.5 %copy-start.68 = (f32[8,128,6]{1,0,2:T(8,128)}, f32[8,128,6]{1,0,2:T(8,128)S(1)}, u32[]{:S(2)}) copy-start(f32[8,128,6]{1,0,2:T(8,128)S(1)} %copy.384) | copy-start | bytes 73732
  120.5 34.8 %copy-start.56 = (f32[8,6,128]{2,0,1:T(8,128)}, f32[8,6,128]{2,0,1:T(8,128)S(1)}, u32[]{:S(2)}) copy-start(f32[8,6,128]{2,0,1:T(8,128)S(1)} %reduce_window_sum.17) | copy-start | bytes 73732
  120.7 29.4 %copy-start.93 = (f32[8,6,1]{0,1,2:T(8,128)}, f32[8,6,1]{0,1,2:T(8,128)S(1)}, u32[]{:S(2)}) copy-start(f32[8,6,1]{0,1,2:T(8,128)S(1)} %copy.449) | copy-start | bytes 580
  126.0 19.5 %copy-start.141 = (f32[16]{0:T(128)}, f32[16]{0:T(128)S(1)}, u32[]{:S(2)}) copy-start(f32[16]{0:T(128)S(1)} %multiply_power_fusion.1) | copy-start | bytes 196
  149.9 6.4 %copy-start.23 = (bf16[1024,256]{1,0:T(8,128)(2,1)}, bf16[1024,256]{1,0:T(8,128)(2,1)S(1)}, u32[]{:S(2)}) copy-start(bf16[1024,256]{1,0:T(8,128)(2,1)S(1)} %get-tuple-element.112) | copy-start | bytes 1572868
  149.9 10.0 %copy-start.25 = (bf16[1024,256]{1,0:T(8,128)(2,1)}, bf16[1024,256]{1,0:T(8,128)(2,1)S(1)}, u32[]{:S(2)}) copy-start(bf16[1024,256]{1,0:T(8,128)(2,1)S(1)} %get-tuple-element.113) | copy-start | bytes 1572868
  150.1 5.3 copy-start.124
  153.4 7.1 %copy-start.28 = (bf16[48,8,8,128]{3,2,1,0:T(8,128)(2,1)}, bf16[48,8,8,128]{3,2,1,0:T(8,128)(2,1)S(1)}, u32[]{:S(2)}) copy-start(bf16[48,8,8,128]{3,2,1,0:T(8,128)(2,1)S(1)} %copy.457) | copy-start | bytes 2359300
  155.6 4.9 copy-start.100
  164.9 6.8 %copy-start.20 = (f32[1024,384]{1,0:T(8,128)}, f32[1024,384]{1,0:T(8,128)S(1)}, u32[]{:S(2)}) copy-start(f32[1024,384]{1,0:T(8,128)S(1)} %copy.403) | copy-start | bytes 4718596
  172.8 14.5 %copy-start.13 = (f32[1024,384]{1,0:T(8,128)}, f32[1024,384]{1,0:T(8,128)S(1)}, u32[]{:S(2)}) copy-start(f32[1024,384]{1,0:T(8,128)S(1)} %get-tuple-element.93) | copy-start | bytes 4718596
  172.8 6.8 %copy-start.39 = (f32[1024,1,128]{2,0,1:T(8,128)S(1)}, f32[1024,1,128]{2,0,1:T(8,128)}, u32[]{:S(2)}) copy-start(f32[1024,1,128]{2,0,1:T(8,128)} %slice_bitcast_fusion) | copy-start | bytes 1572868
  172.8 6.8 %copy-start.145 = (f32[64]{0:T(128)S(1)}, f32[64]{0:T(128)}, u32[]{:S(2)}) copy-start(f32[64]{0:T(128)} %multiply_power_fusion) | copy-start | bytes 772
  172.8 9.7 %copy-start.63 = (bf16[2,4,16,1024]{3,2,1,0:T(8,128)(2,1)S(1)}, bf16[2,4,16,1024]{3,2,1,0:T(8,128)(2,1)}, u32[]{:S(2)}) copy-start(bf16[2,4,16,1024]{3,2,1,0:T(8,128)(2,1)} %copy.378) | copy-start | bytes 786436
  185.5 175.8 %copy-start.115 = (f32[1024]{0:T(1024)}, f32[1024]{0:T(1024)S(1)}, u32[]{:S(2)}) copy-start(f32[1024]{0:T(1024)S(1)} %fusion.7) | copy-start | bytes 12292
  191.6 22.3 %copy-start.21 = (bf16[1,128,2048]{2,1,0:T(8,128)(2,1)S(1)}, bf16[1,128,2048]{2,1,0:T(8,128)(2,1)}, u32[]{:S(2)}) copy-start(bf16[1,128,2048]{2,1,0:T(8,128)(2,1)} %param.24) | copy-start | bytes 1572868
  191.6 22.3 %copy-start.126 = (f32[128]{0:T(128)S(1)}, f32[128]{0:T(128)}, u32[]{:S(2)}) copy-start(f32[128]{0:T(128)} %copy-done.125) | copy-start | bytes 1540
  215.2 109.5 %copy-start.11 = (f32[128,2048]{1,0:T(8,128)}, f32[128,2048]{1,0:T(8,128)S(1)}, u32[]{:S(2)}) copy-start(f32[128,2048]{1,0:T(8,128)S(1)} %get-tuple-element.91) | copy-start | bytes 3145732
  215.2 109.5 %copy-start.129 = (f32[128]{0:T(128)}, f32[128]{0:T(128)S(1)}, u32[]{:S(2)}) copy-start(f32[128]{0:T(128)S(1)} %add_rsqrt_fusion) | copy-start | bytes 1540
  266.7 8.1 %copy-start.160 = (bf16[1024,2048]{1,0:T(8,128)(2,1)S(1)}, bf16[1024,2048]{1,0:T(8,128)(2,1)}, u32[]{:S(2)}) copy-start(bf16[1024,2048]{1,0:T(8,128)(2,1)} %get-tuple-element.58) | copy-start | bytes 12582916
  278.5 150.5 %reduce-scatter.8.cloned.1.call-start = ((), (), s32[]{:S(2)}) async-start(), calls=%async_computation.6 | async-start | bytes 5242880 | tf_op jit(solution)/shard_map/reduce_scatter | solution.py:1433
  288.3 219.7 %reduce-scatter.10.cloned.1.call-start = ((), (), s32[]{:S(2)}) async-start(), calls=%async_computation.7 | async-start | bytes 2621440 | tf_op jit(solution)/shard_map/reduce_scatter | solution.py:1433
  288.4 7.3 %copy-start = (bf16[2048,1024]{1,0:T(8,128)(2,1)S(1)}, bf16[2048,1024]{1,0:T(8,128)(2,1)}, u32[]{:S(2)}) copy-start(bf16[2048,1024]{1,0:T(8,128)(2,1)} %convolution_convert_fusion.2) | copy-start | bytes 12582916
  295.7 23.4 %copy-start.162 = (bf16[1024,512]{0,1:T(8,128)(2,1)S(1)}, bf16[1024,512]{0,1:T(8,128)(2,1)}, u32[]{:S(2)}) copy-start(bf16[1024,512]{0,1:T(8,128)(2,1)} %copy-done.161) | copy-start | bytes 3145732
  367.4 12.7 %copy-start.61 = (bf16[1024,128]{1,0:T(8,128)(2,1)}, bf16[1024,128]{1,0:T(8,128)(2,1)S(1)}, u32[]{:S(2)}) copy-start(bf16[1024,128]{1,0:T(8,128)(2,1)S(1)} %fusion.96) | copy-start | bytes 786436
  375.3 4.8 copy-start.40
  375.3 4.8 copy-start.97
  383.9 124.2 %reduce-scatter.12.cloned.1.call-start = ((), (), s32[]{:S(2)}) async-start(), calls=%async_computation.8 | async-start | bytes 2621440 | tf_op jit(solution)/shard_map/reduce_scatter | solution.py:1433
  397.3 5.4 copy-start.66
  421.0 5.0 slice-start
  429.0 121.0 %reduce-scatter.14.cloned.1.call-start = ((), (), s32[]{:S(2)}) async-start(), calls=%async_computation.9 | async-start | bytes 2621440 | tf_op jit(solution)/shard_map/reduce_scatter | solution.py:1433
  430.0 5.1 copy-start.6
  436.7 34.1 %copy-start.142 = (f32[16]{0:T(128)S(1)}, f32[16]{0:T(128)}, u32[]{:S(2)}) copy-start(f32[16]{0:T(128)} %copy-done.141) | copy-start | bytes 196
  469.4 5.4 copy-start.16
  469.4 5.4 copy-start.31
  469.4 5.4 copy-start.38
  469.4 5.4 copy-start.118
  469.4 5.4 copy-start.120
  469.5 5.4 copy-start.122
  474.9 5.1 copy-start.105
  474.9 5.1 copy-start.107
  474.9 5.1 copy-start.109
  474.9 5.1 copy-start.111
  492.9 8.5 %copy-start.70 = (f32[1024,6]{1,0:T(8,128)S(1)}, f32[1024,6]{1,0:T(8,128)}, u32[]{:S(2)}) copy-start(f32[1024,6]{1,0:T(8,128)} %get-tuple-element.146) | copy-start | bytes 73732
  494.8 7.8 %copy-start.128 = (f32[384]{0:T(512)S(1)}, f32[384]{0:T(512)}, u32[]{:S(2)}) copy-start(f32[384]{0:T(512)} %get-tuple-element.79) | copy-start | bytes 4612
  494.9 7.8 %copy-start.153 = (f32[48]{0:T(128)S(1)}, f32[48]{0:T(128)}, u32[]{:S(2)}) copy-start(f32[48]{0:T(128)} %param.38) | copy-start | bytes 580
  494.9 7.9 %copy-start.45 = (bf16[1024,384]{1,0:T(8,128)(2,1)S(1)}, bf16[1024,384]{1,0:T(8,128)(2,1)}, u32[]{:S(2)}) copy-start(bf16[1024,384]{1,0:T(8,128)(2,1)} %copy-done.44) | copy-start | bytes 2359300
  494.9 7.8 %copy-start.62 = (bf16[1024,128]{1,0:T(8,128)(2,1)S(1)}, bf16[1024,128]{1,0:T(8,128)(2,1)}, u32[]{:S(2)}) copy-start(bf16[1024,128]{1,0:T(8,128)(2,1)} %copy-done.61) | copy-start | bytes 786436
  552.0 19.2 %copy-start.22 = (bf16[1,128,2048]{2,1,0:T(8,128)(2,1)S(1)}, bf16[1,128,2048]{2,1,0:T(8,128)(2,1)}, u32[]{:S(2)}) copy-start(bf16[1,128,2048]{2,1,0:T(8,128)(2,1)} %param.24) | copy-start | bytes 1572868
  552.0 19.2 %copy-start.127 = (f32[128]{0:T(128)S(1)}, f32[128]{0:T(128)}, u32[]{:S(2)}) copy-start(f32[128]{0:T(128)} %copy-done.125) | copy-start | bytes 1540
  571.5 5.0 copy-start.4
  571.5 5.0 copy-start.12
  571.5 5.0 copy-start.50
  571.6 5.0 copy-start.130
  571.6 5.0 copy-start.144
  (111 other events, 286.5 us)
Sparse Core Ops, SparseCore 0:
  95.4 44.1 all-gather.6
  141.1 79.4 all-gather.10
  222.2 44.4 all-gather.8
  278.7 42.5 reduce-scatter.5
  323.5 76.0 reduce-scatter.7
  401.8 44.3 reduce-scatter.9
  448.6 43.1 reduce-scatter.11
  494.1 43.1 reduce-scatter.13

commit v4 on v3

--- a/solution.py
+++ b/solution.py
@@ -1174,6 +1174,110 @@
     o_ref[...] = out
     for copy in copies:
         copy.wait_send()
+
+
+def product_steps(kind, block, rounds, a_any, b_any, o_any, a, b, o, sems):
+    loads = [
+        pltpu.make_async_copy(src, dst, sems.at[k])
+        for k, (src, dst) in enumerate(((a_any, a), (b_any, b)))
+    ]
+    for load in loads:
+        load.start()
+    yield True
+    for load in loads:
+        load.wait()
+    count = o.shape[0] // block
+    per = -(-count // rounds)
+    for first in range(0, count, per):
+
+        def one(k, carry):
+            rows = pl.ds(pl.multiple_of(k * block, 128), block)
+            if kind:
+                part = lax.dot_general(
+                    a[:, rows], b[...], (((0,), (0,)), ((), ())), preferred_element_type=F32
+                )
+            else:
+                part = jnp.dot(a[rows, :], b[...], preferred_element_type=F32)
+            o[rows, :] = part.astype(BF)
+            return carry
+
+        lax.fori_loop(first, min(first + per, count), one, 0)
+        yield True
+    store = pltpu.make_async_copy(o, o_any, sems.at[2])
+    store.start()
+    yield True
+    store.wait()
+
+
+def product_scratch(kind, a, b):
+    rows = a.shape[1] if kind else a.shape[0]
+    return [
+        pltpu.VMEM(a.shape, BF),
+        pltpu.VMEM(b.shape, BF),
+        pltpu.VMEM((rows, b.shape[1]), BF),
+        pltpu.SemaphoreType.DMA((3,)),
+    ]
+
+
+def scatter_beside_kernel(seqs, p_ref, a, b, o_ref, o, *scratch):
+    me, sibling, by_x, by_y = plane()
+    greet([(CTX, sibling), (CTX, by_x), (CTX, by_y)])
+    together(
+        scatter_steps(seqs, p_ref, o_ref, *scratch[:10]),
+        product_steps(1, 256, 3, a, b, o, *scratch[10:]),
+    )
+
+
+def scatter_beside(partial_sum, a, b, seqs, ids, waits=()):
+    anywhere = pl.BlockSpec(memory_space=pl.ANY)
+    rows, cols = partial_sum.shape[0] // PLANE, partial_sum.shape[1]
+    return pl.pallas_call(
+        unused(partial(scatter_beside_kernel, seqs), 3, len(waits)),
+        out_shape=(
+            jax.ShapeDtypeStruct((rows, cols), F32),
+            jax.ShapeDtypeStruct((a.shape[1], b.shape[1]), BF),
+        ),
+        in_specs=[anywhere] * (3 + len(waits)),
+        out_specs=(pl.BlockSpec(memory_space=pltpu.VMEM), anywhere),
+        scratch_shapes=scatter_scratch(rows, cols) + product_scratch(1, a, b),
+        cost_estimate=lasting(25),
+        compiler_params=pltpu.CompilerParams(
+            collective_id=next(ids), has_side_effects=True, vmem_limit_bytes=40 * 2**20
+        ),
+    )(partial_sum.astype(BF), a, b, *waits)
+
+
+def gather_beside_kernel(pieces, x_ref, a, b, o_ref, o, *scratch):
+    me, sibling, by_x, by_y = plane()
+    greet([(CTX, sibling), (CTX, by_x), (CTX, by_y)])
+    together(
+        gather_steps(pieces, x_ref, o_ref, *scratch[:3]),
+        product_steps(0, 256, 4, a, b, o, *scratch[3:]),
+    )
+
+
+def gather_beside(block, a, b, ids, pieces=4):
+    anywhere = pl.BlockSpec(memory_space=pl.ANY)
+    rows, cols = block.shape
+    return pl.pallas_call(
+        partial(gather_beside_kernel, pieces),
+        out_shape=(
+            jax.ShapeDtypeStruct((PLANE * rows, cols), BF),
+            jax.ShapeDtypeStruct((a.shape[0], b.shape[1]), BF),
+        ),
+        in_specs=[anywhere] * 3,
+        out_specs=(anywhere, anywhere),
+        scratch_shapes=[
+            pltpu.SemaphoreType.DMA,
+            pltpu.SemaphoreType.DMA((7, pieces)),
+            pltpu.SemaphoreType.DMA((7, pieces)),
+        ]
+        + product_scratch(0, a, b),
+        cost_estimate=lasting(22),
+        compiler_params=pltpu.CompilerParams(
+            collective_id=next(ids), has_side_effects=True, vmem_limit_bytes=40 * 2**20
+        ),
+    )(block, a, b)
 
 
 def scatter_two_kernel(p_ref, q_ref, o_ref, oq_ref, *scratch):
@@ -1796,16 +1900,17 @@
     sigmoid_gate = jax.nn.sigmoid(gate_lin)
     silu_gate = gate_lin * sigmoid_gate
     hidden = (silu_gate * up_lin).astype(BF)
+    down_part = mm_tn(hidden, grad_all).astype(BF).reshape(seqs, ff // seqs, width)
+    down_own = hold(down_own, down_part)
     grad_hidden = mm_nt(grad_all, down_own)
     grad_gate = (
         grad_hidden * up_lin * (sigmoid_gate + silu_gate * (1.0 - sigmoid_gate))
     ).astype(BF)
     grad_up = (grad_hidden * silu_gate).astype(BF)
     grad_gu = jnp.concatenate([grad_gate, grad_up], axis=1)
-    down_grad = scatter_rows(mm_tn(hidden, grad_all).reshape(seqs, ff // seqs, width))
-    ffn_grad = mm_tn(normed_two, grad_gu).reshape(seqs, ctx, krows, 2 * ff).astype(BF)
-    grad_n2 = scatter_tokens(mm_nt(grad_gu, ffn_own), ids, (ffn_grad,), seqs=seqs)
-    ffn_grad = scatter_rows(ffn_grad)
+    down_grad = scatter_rows(down_part)
+    grad_n2, ffn_grad = scatter_beside(mm_nt(grad_gu, ffn_own), normed_two, grad_gu, seqs, ids)
+    ffn_grad = scatter_rows(ffn_grad.reshape(seqs, ctx, krows, 2 * ff))
 
     turned = grad_n2 * gain_two
     hat_two = mid * scale_two
@@ -1813,7 +1918,8 @@
     grad_mid = out_grad[0].astype(F32) + scale_two * (
         turned - hat_two * jnp.mean(turned * hat_two, axis=-1, keepdims=True)
     )
-    branch_grad = hold(gather_tokens(grad_mid.astype(BF), ids), down_grad)
+    branch_grad, last = gather_beside(grad_mid.astype(BF), hidden, down_own, ids)
+    branch_grad = hold(branch_grad, down_grad)
 
     out_grad_own = mm_tn(mixed, branch_grad).astype(BF)
     out_part = jnp.concatenate(
@@ -1824,9 +1930,8 @@
         axis=1,
     )
     out_grad_own = scatter_rows(hold(out_part, ffn_grad))
-    grad_mixed = mm_nt(branch_grad, out_own)
-    grad_attn = grad_mixed[:, :head].astype(BF).reshape(length, -1, HEAD_SIZE)
-    grad_ymix = grad_mixed[:, head:]
+    grad_attn = mm_nt(branch_grad, out_own[:head]).astype(BF).reshape(length, -1, HEAD_SIZE)
+    grad_ymix = mm_nt(branch_grad, out_own[head:])
 
     grad_prob = jnp.einsum("thd,ud->htu", grad_attn, value, preferred_element_type=F32)
     delta = jnp.sum(probs * grad_prob, axis=-1, keepdims=True)
@@ -1866,7 +1971,7 @@
     grad_shared = jnp.concatenate([grad_shared.T.reshape(ctx, bc, length), grad_kv], axis=1)
     grad_shared, last = scatter_two(
         grad_shared.reshape(ctx * (bc + 2 * kv), length),
-        mm(hidden, down_own).astype(BF),
+        last,
         ids,
         (ffn_grad, rest_part),
     )

time: 593 us -> 576 us (0.971)
  matrix products: 110 us -> 90.3 us
    pallas_call x0 -> x2, Pallas kernels: none -> 46.9 us  [the longest x1 25.2 us: scatter_beside(): pl.pallas_call(unused(partial(scatter_beside_kernel, seqs), 3, len(waits)...]
    pallas_call x2 -> x1, Pallas kernels: 45.2 us -> 22.3 us  [scatter_tokens(): pl.pallas_call(unused(partial(scatter_kernel, seqs), 1, len(waits)), out_...]
    pallas_call x3 -> x2, Pallas kernels: 57.7 us -> 35.4 us  [gather_tokens(): pl.pallas_call(unused(partial(gather_kernel, pieces), 1, len(waits)), out...]
    dot_general x15 -> x14, matrix products: 81.6 us -> 65.5 us  [dotf(): lax.dot_general(left, right, (dims, ((), ())), preferred_element_type=F32)]
    unnamed x342 -> x345, local copies, waits for them, and re-layouts: 29.1 us -> 38.9 us
  transfers between devices with their start and end apart: 8 -> 8, of which waited for: 1 -> 1; matrix products, arithmetic and copies ran while one was open for 36% -> 35% of each run, Pallas kernels for 32% -> 33%
where the time goes in v4:
time: 576 us; the launch traced here: 571 us
  Pallas kernels  285 us (49%)
  matrix products  90.3 us (16%)
  other arithmetic  83.9 us (15%)
  local copies, waits for them, and re-layouts  80.7 us (14%)
  between operations  16.8 us (3%)
  waiting for transfers between devices  13.7 us (2%)
    pallas_call x1, Pallas kernels, opening(): pl.pallas_call(partial(opening_kernel, seqs, pieces), out_shape=(shape(PL...  80.6 us
    dot_general x14, matrix products, dotf(): lax.dot_general(left, right, (dims, ((), ())), preferred_element_type=F32)  65.5 us
    pallas_call x1, Pallas kernels, closing(): pl.pallas_call(unused(partial(closing_kernel, seqs), 9, len(waits)), out_...  42.3 us
    unnamed x345, local copies, waits for them, and re-layouts  38.9 us
    pallas_call x2, Pallas kernels, gather_tokens(): pl.pallas_call(unused(partial(gather_kernel, pieces), 1, len(waits)), out...  35.4 us
    pallas_call x1, Pallas kernels, scatter_two(): pl.pallas_call(unused(scatter_two_kernel, 2, len(waits)), out_shape=tuple...  30.5 us
    pallas_call x1, Pallas kernels, scatter_beside(): pl.pallas_call(unused(partial(scatter_beside_kernel, seqs), 3, len(waits)...  25.2 us
    pallas_call x1, Pallas kernels, scatter_tokens(): pl.pallas_call(unused(partial(scatter_kernel, seqs), 1, len(waits)), out_...  22.3 us
  transfers between devices with their start and end apart: 8, of which 1 were waited for; matrix products, arithmetic and copies ran while one was open for 35% of the time, Pallas kernels for 33%

profile of v4, /device:TPU:0, one launch (start us, length us, event | category | flops | bytes accessed | tf_op | source)
XLA Modules:
  0.0 571.0 jit_solution(16887863897717127952)
XLA Ops:
  14.7 80.6 %shard_map.373 = (bf16[8,4,32,128]{3,2,1,0:T(8,128)(2,1)}, bf16[4,128,2048]{2,1,0:T(8,128)(2,1)}, bf16[1024,2048]{1,0:T(8,128)(2,1)}, bf16[1024,2048]{1,0:T(8,12...) custom-call(bf16[32,128]{1,0:T(8,128)(2,1)} %pad_bitcast_fusion.refs, ...), custom_call_target="tpu_custom_call" | custom-call | flops 20999999488 | bytes 21000000 | tf_op jit(solution)/shard_map/pallas_call | solution.py:1120
  98.1 6.8 %fusion.137 = (bf16[1024,512]{1,0:T(8,128)(2,1)S(1)}, f32[1024,512]{1,0:T(8,128)}) fusion(bf16[2048,512]{1,0:T(8,128)(2,1)} %bitcast.489, bf16[1024,2048]{1,0:T(8,128)(2,1)} %get-tuple-element.58, f32[2048]{0:T(1024)S(1)} %reshape.804), kind=kOutput, calls=%fused_computation.299 | convolution fusion | flops 2154299392 | bytes 9445376 | tf_op jit(solution)/shard_map/dot_general | solution.py:611
  108.7 3.2 multiply_convert_fusion.5
  114.0 4.5 compare_select_fusion.2
  118.9 1.7 reduce_window_sum.17
  126.7 3.8 fusion.76
  132.8 13.5 %shard_map.374 = bf16[1024,1024]{1,0:T(8,128)(2,1)} custom-call(bf16[128,1024]{1,0:T(8,128)(2,1)} %copy.393.refs_0_), custom_call_target="tpu_custom_call" | custom-call | flops 2400000000 | bytes 2400000 | tf_op jit(solution)/shard_map/pallas_call | solution.py:818
  146.3 2.0 fusion.134
  157.5 3.1 multiply_reduce_fusion.1
  162.3 1.5 fusion.25
  166.0 5.3 fusion.22
  173.5 6.1 %shard_map.375 = f32[8,128]{1,0:T(8,128)} custom-call(f32[8,128]{1,0:T(8,128)} %bitcast.481), custom_call_target="tpu_custom_call" | custom-call | flops 1500000000 | bytes 1500000 | tf_op jit(solution)/shard_map/pallas_call | solution.py:978
  180.3 2.8 fusion.100
  184.4 1.8 fusion.7
  186.4 1.6 fusion.43
  189.9 2.3 convolution_convert_fusion.refs_0_
  192.3 22.3 %shard_map.376 = f32[128,2048]{1,0:T(8,128)S(1)} custom-call(bf16[1024,2048]{1,0:T(8,128)(2,1)S(1)} %convolution_convert_fusion.refs_0_), custom_call_target="tpu_custom_call" | custom-call | flops 6600000000 | bytes 6600000 | tf_op jit(solution)/shard_map/pallas_call | solution.py:944
  217.4 21.9 %shard_map.377.refs_1_ = bf16[1024,2048]{1,0:T(8,128)(2,1)} custom-call(bf16[128,2048]{1,0:T(8,128)(2,1)} %copy.422.refs_0_), custom_call_target="tpu_custom_call" | custom-call | flops 6600000000 | bytes 6600000 | tf_op jit(solution)/shard_map/pallas_call | solution.py:818
  239.3 7.7 %fusion.139 = f32[1024,1024]{1,0:T(8,128)S(1)} fusion(bf16[1024,2048]{1,0:T(8,128)(2,1)} %shard_map.377.refs_1_, bf16[2048,1024]{1,0:T(8,128)(2,1)} %bitcast.484), kind=kOutput, calls=%fused_computation.301 | convolution fusion | flops 4294967296 | bytes 12582912 | tf_op jit(solution)/shard_map/dot_general | solution.py:611
  249.2 1.6 copy-done.164
  250.8 3.8 convolution_convert_fusion.5
  254.6 12.1 %all-gather.9.cloned.1.call-done.refs_0_ = bf16[512,2048]{1,0:T(8,128)(2,1)} async-done(((bf16[128,2048]{1,0:T(8,128)(2,1)}), bf16[512,2048]{1,0:T(8,128)(2,1)}) %all-gather.9.cloned.1.call-update) | async-done | bytes 2097168 | tf_op jit(solution)/shard_map/all_gather | solution.py:1533
  266.8 7.0 %multiply_convert_fusion.3 = (bf16[1024,512]{1,0:T(8,128)(2,1)S(1)}, bf16[1024,512]{1,0:T(8,128)(2,1)S(1)}) fusion(f32[1024,1024]{1,0:T(8,128)} %copy-done.41, bf16[1024,2048]{1,0:T(8,128)(2,1)} %get-tuple-element.62, bf16[512,2048]{1,0:T(8,128)(2,1)} %shard_map.378.b), kind=kOutput, calls=%fused_computation.56 | convolution fusion | flops 2153775104 | bytes 12582912 | tf_op jit(solution)/shard_map/dot_general | solution.py:611
  274.1 1.9 copy-done.156
  276.0 4.8 convolution_convert_fusion.1.refs_0_
  280.8 25.2 %shard_map.379 = (f32[128,2048]{1,0:T(8,128)S(1)}, bf16[2048,1024]{1,0:T(8,128)(2,1)S(1)}) custom-call(bf16[1024,2048]{1,0:T(8,128)(2,1)S(1)} %convolution_convert_fusion.1.refs_0_, bf16[1024,2048]{1,0:T(8,128)(2,1)} %shard_map.377.refs_1_, bf16[1024,1024]{1,0:T(8,128)(2,1)S(1)} %pad_maximum_fusion.refs_2_), custom_call_target="tpu_custom_call" | custom-call | flops 7500000256 | bytes 7500000 | tf_op jit(solution)/shard_map/pallas_call | solution.py:1234
  306.0 2.0 copy-done
  312.8 21.8 %shard_map.380 = (bf16[1024,2048]{1,0:T(8,128)(2,1)S(1)}, bf16[1024,2048]{1,0:T(8,128)(2,1)S(1)}) custom-call(bf16[128,2048]{1,0:T(8,128)(2,1)S(1)} %fusion.128.x_ref, bf16[1024,512]{1,0:T(8,128)(2,1)S(1)} %multiply_convert_fusion.4.a, bf16[512,2048]{1,0:T(8,128)(2,1)S(1)} %copy-done.3), custom_call_target="tpu_custom_call" | custom-call | flops 6600000000 | bytes 6600000 | tf_op jit(solution)/shard_map/pallas_call | solution.py:1262
  334.6 2.0 copy-done.1
  336.6 2.1 copy-done.9
  339.8 3.8 convolution_convert_fusion.6
  345.1 2.4 fusion.10
  349.9 2.2 fusion.85
  352.4 4.2 multiply_reduce_fusion.11
  356.6 6.1 %shard_map.382 = f32[8,128]{1,0:T(8,128)} custom-call(f32[8,128]{1,0:T(8,128)} %bitcast.492, bf16[128,2048]{1,0:T(8,128)(2,1)} %bitcast.408), custom_call_target="tpu_custom_call" | custom-call | flops 1500000000 | bytes 1500000 | tf_op jit(solution)/shard_map/pallas_call | solution.py:978
  363.4 5.6 multiply_reduce_fusion.10
  369.0 3.7 convolution_convert_fusion.4
  373.9 4.6 convolution_convert_fusion.3
  380.3 3.1 copy.427
  383.4 1.8 copy.479
  386.0 3.1 multiply_reduce_fusion
  390.8 1.4 fusion.30
  393.2 1.5 copy.525
  394.6 3.0 copy.444
  397.7 3.1 convolution_bitcast_fusion.1
  400.8 3.9 multiply_reduce_fusion.5
  408.4 2.5 fusion.42
  411.0 3.0 pad_maximum_fusion.3.refs_0_
  414.9 3.7 fusion.39
  421.7 30.5 %shard_map.383 = (f32[128,1024]{1,0:T(8,128)S(1)}, f32[128,2048]{1,0:T(8,128)S(1)}) custom-call(bf16[1024,1024]{1,0:T(8,128)(2,1)S(1)} %bitcast.366, bf16[1024,2048]{1,0:T(8,128)(2,1)S(1)} %copy-done.10, bf16[8,64,1024]{2,1,0:T(8,128)(2,1)S(1)} %bitcast.369, bf16[4,8,64,512]{3,2,1,0:T(8,128)(2,1)S(1)} %bitcast.365), custom_call_target="tpu_custom_call" | custom-call | flops 8400000000 | bytes 8400000 | tf_op jit(solution)/shard_map/pallas_call | solution.py:1295
  453.7 2.2 fusion.79
  456.2 5.1 multiply_reduce_fusion.8
  464.4 3.8 convolution_convert_fusion.2
  470.3 3.2 multiply_reduce_fusion.2
  473.7 2.3 multiply_reduce_fusion.12
  477.1 1.9 reduce_window_sum.18
  480.4 1.7 fusion.129
  484.1 3.1 fusion.20.step
  488.4 42.3 %shard_map.385 = (f32[128,2048]{1,0:T(8,128)}, f32[8,4,8,128]{3,2,1,0:T(8,128)}, bf16[64,1024]{1,0:T(8,128)(2,1)}, bf16[64,3072]{1,0:T(8,128)(2,1)}, bf16[64,4096]{1,0:T(8,128)(2,1)}, /*index=5*/bf16[64,4096]{1,0:T(8,128)(2,1)}) custom-call(bf16[1024,512]{1,0:T(8,128)(2,1)} %copy-done.60, bf16[1024,512]{1,0:T(8,128)(2,1)} %pad_maximum_fusion.5.refs_1_, ...), custom_call_target="tpu_custom_call" | custom-call | flops 10499999744 | bytes 10500000 | tf_op jit(solution)/shard_map/pallas_call | solution.py:1366
  532.6 14.9 %shard_map.386 = (f32[16,128]{1,0:T(8,128)S(1)}, f32[8,8,128]{2,1,0:T(8,128)S(1)}, bf16[64,3584]{1,0:T(8,128)(2,1)S(1)}, f32[64,256]{1,0:T(8,128)S(1)}, f32[64,256]{1,0:T(8,128)S(1)}) custom-call(f32[8,4,8,128]{3,2,1,0:T(8,128)S(1)} %copy-done.11, f32[1,2048]{1,0:T(1,128)S(1)} %bitcast.371, f32[1,384]{1,0:T(1,128)S(1)} %broadcast_in_dim.216.mixer_gain, ...), custom_call_target="tpu_custom_call" | custom-call | flops 4499999744 | bytes 4500000 | tf_op jit(solution)/shard_map/pallas_call | solution.py:1495
  551.8 1.6 multiply_reduce_fusion.16
  553.4 2.2 convert_element_type.401
  555.7 2.1 convert_element_type.402
  559.4 1.6 fusion.89
  (542 shorter events, 96.3 us)
Async XLA Ops:
  7.2 158.9 %all-gather.7.cloned.1.call-start = ((), (), s32[]{:S(2)}) async-start(), calls=%async_computation.10 | async-start | bytes 2621440 | tf_op jit(solution)/shard_map/all_gather | solution.py:1533
  95.3 144.0 %all-gather.11.cloned.1.call-start = ((), (), s32[]{:S(2)}) async-start(), calls=%async_computation.12 | async-start | bytes 5242880 | tf_op jit(solution)/shard_map/all_gather | solution.py:1533
  96.1 170.7 %all-gather.9.cloned.1.call-start = ((), (), s32[]{:S(2)}) async-start(), calls=%async_computation.11 | async-start | bytes 2621440 | tf_op jit(solution)/shard_map/all_gather | solution.py:1533
  96.8 241.9 %reduce-scatter.6.cloned.1.call-start = ((), (), s32[]{:S(2)}) async-start(), calls=%async_computation.5 | async-start | bytes 2621440 | tf_op jit(solution)/shard_map/reduce_scatter | solution.py:1537
  97.1 11.2 %copy-start.59 = (bf16[4,8,32,128]{3,1,2,0:T(8,128)(2,1)}, bf16[4,8,32,128]{3,1,2,0:T(8,128)(2,1)S(1)}, u32[]{:S(2)}) copy-start(bf16[4,8,32,128]{3,1,2,0:T(8,128)(2,1)S(1)} %copy.527) | copy-start | bytes 786436
  98.0 6.9 %copy-start.84 = (f32[32,64]{1,0:T(8,128)}, f32[32,64]{1,0:T(8,128)S(1)}, u32[]{:S(2)}) copy-start(f32[32,64]{1,0:T(8,128)S(1)} %get-tuple-element.129) | copy-start | bytes 24580
  105.9 6.0 %copy-start.17 = (f32[1024,448]{1,0:T(8,128)}, f32[1024,448]{1,0:T(8,128)S(1)}, u32[]{:S(2)}) copy-start(f32[1024,448]{1,0:T(8,128)S(1)} %slice_convert_fusion) | copy-start | bytes 5505028
  113.9 4.6 copy-start.53
  114.0 4.7 copy-start.154
  114.0 10.7 %copy-start.49 = (bf16[4,128,2048]{2,1,0:T(8,128)(2,1)S(1)}, bf16[4,128,2048]{2,1,0:T(8,128)(2,1)}, u32[]{:S(2)}) copy-start(bf16[4,128,2048]{2,1,0:T(8,128)(2,1)} %get-tuple-element.61) | copy-start | bytes 6291460
  118.7 32.2 %copy-start.68 = (f32[8,128,6]{1,0,2:T(8,128)}, f32[8,128,6]{1,0,2:T(8,128)S(1)}, u32[]{:S(2)}) copy-start(f32[8,128,6]{1,0,2:T(8,128)S(1)} %copy.400) | copy-start | bytes 73732
  120.6 35.5 %copy-start.57 = (f32[8,6,128]{2,0,1:T(8,128)}, f32[8,6,128]{2,0,1:T(8,128)S(1)}, u32[]{:S(2)}) copy-start(f32[8,6,128]{2,0,1:T(8,128)S(1)} %reduce_window_sum.17) | copy-start | bytes 73732
  120.8 30.1 %copy-start.92 = (f32[8,6,1]{0,1,2:T(8,128)}, f32[8,6,1]{0,1,2:T(8,128)S(1)}, u32[]{:S(2)}) copy-start(f32[8,6,1]{0,1,2:T(8,128)S(1)} %copy.470) | copy-start | bytes 580
  126.7 19.5 %copy-start.142 = (f32[16]{0:T(128)}, f32[16]{0:T(128)S(1)}, u32[]{:S(2)}) copy-start(f32[16]{0:T(128)S(1)} %multiply_power_fusion.1) | copy-start | bytes 196
  150.6 6.3 %copy-start.26 = (bf16[1024,256]{1,0:T(8,128)(2,1)}, bf16[1024,256]{1,0:T(8,128)(2,1)S(1)}, u32[]{:S(2)}) copy-start(bf16[1024,256]{1,0:T(8,128)(2,1)S(1)} %get-tuple-element.119) | copy-start | bytes 1572868
  150.6 10.0 %copy-start.28 = (bf16[1024,256]{1,0:T(8,128)(2,1)}, bf16[1024,256]{1,0:T(8,128)(2,1)S(1)}, u32[]{:S(2)}) copy-start(bf16[1024,256]{1,0:T(8,128)(2,1)S(1)} %get-tuple-element.120) | copy-start | bytes 1572868
  150.9 5.2 copy-start.122
  151.6 4.8 copy-start.159
  151.6 4.8 copy-start.91
  154.1 7.1 %copy-start.30 = (bf16[48,8,8,128]{3,2,1,0:T(8,128)(2,1)}, bf16[48,8,8,128]{3,2,1,0:T(8,128)(2,1)S(1)}, u32[]{:S(2)}) copy-start(bf16[48,8,8,128]{3,2,1,0:T(8,128)(2,1)S(1)} %copy.477) | copy-start | bytes 2359300
  156.3 4.9 copy-start.96
  156.4 4.8 copy-start.162
  156.6 4.6 copy-start.87
  156.9 4.3 copy-start.70
  165.6 6.7 %copy-start.21 = (f32[1024,384]{1,0:T(8,128)}, f32[1024,384]{1,0:T(8,128)S(1)}, u32[]{:S(2)}) copy-start(f32[1024,384]{1,0:T(8,128)S(1)} %copy.419) | copy-start | bytes 4718596
  173.5 14.5 %copy-start.22 = (f32[1024,384]{1,0:T(8,128)}, f32[1024,384]{1,0:T(8,128)S(1)}, u32[]{:S(2)}) copy-start(f32[1024,384]{1,0:T(8,128)S(1)} %get-tuple-element.101) | copy-start | bytes 4718596
  173.5 6.8 %copy-start.40 = (f32[1024,1,128]{2,0,1:T(8,128)S(1)}, f32[1024,1,128]{2,0,1:T(8,128)}, u32[]{:S(2)}) copy-start(f32[1024,1,128]{2,0,1:T(8,128)} %slice_bitcast_fusion) | copy-start | bytes 1572868
  173.5 6.8 %copy-start.146 = (f32[64]{0:T(128)S(1)}, f32[64]{0:T(128)}, u32[]{:S(2)}) copy-start(f32[64]{0:T(128)} %multiply_power_fusion) | copy-start | bytes 772
  173.5 9.7 %copy-start.63 = (bf16[2,4,16,1024]{3,2,1,0:T(8,128)(2,1)S(1)}, bf16[2,4,16,1024]{3,2,1,0:T(8,128)(2,1)}, u32[]{:S(2)}) copy-start(bf16[2,4,16,1024]{3,2,1,0:T(8,128)(2,1)} %copy.394) | copy-start | bytes 786436
  186.2 158.9 %copy-start.113 = (f32[1024]{0:T(1024)}, f32[1024]{0:T(1024)S(1)}, u32[]{:S(2)}) copy-start(f32[1024]{0:T(1024)S(1)} %fusion.7) | copy-start | bytes 12292
  192.3 22.3 %copy-start.24 = (bf16[1,128,2048]{2,1,0:T(8,128)(2,1)S(1)}, bf16[1,128,2048]{2,1,0:T(8,128)(2,1)}, u32[]{:S(2)}) copy-start(bf16[1,128,2048]{2,1,0:T(8,128)(2,1)} %param.24) | copy-start | bytes 1572868
  192.3 22.3 %copy-start.125 = (f32[128]{0:T(128)S(1)}, f32[128]{0:T(128)}, u32[]{:S(2)}) copy-start(f32[128]{0:T(128)} %copy-done.124) | copy-start | bytes 1540
  254.6 159.4 %reduce-scatter.8.cloned.1.call-start = ((), (), s32[]{:S(2)}) async-start(), calls=%async_computation.6 | async-start | bytes 5242880 | tf_op jit(solution)/shard_map/reduce_scatter | solution.py:1537
  307.9 180.4 %reduce-scatter.10.cloned.1.call-start = ((), (), s32[]{:S(2)}) async-start(), calls=%async_computation.7 | async-start | bytes 2621440 | tf_op jit(solution)/shard_map/reduce_scatter | solution.py:1537
  345.1 4.8 copy-start.147
  345.1 7.2 %copy-start.56 = (bf16[4,96,2048]{2,1,0:T(8,128)(2,1)S(1)}, bf16[4,96,2048]{2,1,0:T(8,128)(2,1)}, u32[]{:S(2)}) copy-start(bf16[4,96,2048]{2,1,0:T(8,128)(2,1)} %slice.246) | copy-start | bytes 4718596
  352.4 16.6 %copy-start.61 = (bf16[1024,128]{1,0:T(8,128)(2,1)}, bf16[1024,128]{1,0:T(8,128)(2,1)S(1)}, u32[]{:S(2)}) copy-start(bf16[1024,128]{1,0:T(8,128)(2,1)S(1)} %fusion.98) | copy-start | bytes 786436
  356.6 6.8 %copy-start.35 = (bf16[1024,448]{1,0:T(8,128)(2,1)S(1)}, bf16[1024,448]{1,0:T(8,128)(2,1)}, u32[]{:S(2)}) copy-start(bf16[1024,448]{1,0:T(8,128)(2,1)} %copy-done.34) | copy-start | bytes 2752516
  363.4 5.6 copy-start.42
  372.7 115.6 %reduce-scatter.12.cloned.1.call-start = ((), (), s32[]{:S(2)}) async-start(), calls=%async_computation.8 | async-start | bytes 2621440 | tf_op jit(solution)/shard_map/reduce_scatter | solution.py:1537
  385.3 5.5 copy-start.15
  385.4 5.4 copy-start.66
  414.0 116.7 %reduce-scatter.14.cloned.1.call-start = ((), (), s32[]{:S(2)}) async-start(), calls=%async_computation.9 | async-start | bytes 2621440 | tf_op jit(solution)/shard_map/reduce_scatter | solution.py:1537
  414.9 5.2 copy-start.10
  421.7 31.9 %copy-start.143 = (f32[16]{0:T(128)S(1)}, f32[16]{0:T(128)}, u32[]{:S(2)}) copy-start(f32[16]{0:T(128)} %copy-done.142) | copy-start | bytes 196
  456.2 5.1 copy-start.103
  456.2 5.1 copy-start.105
  456.2 5.1 copy-start.107
  456.2 5.1 copy-start.109
  473.6 5.5 copy-start.141
  473.7 6.5 %copy-start.127 = (f32[384]{0:T(512)S(1)}, f32[384]{0:T(512)}, u32[]{:S(2)}) copy-start(f32[384]{0:T(512)} %get-tuple-element.95) | copy-start | bytes 4612
  476.0 6.8 %copy-start.148 = (f32[384]{0:T(512)S(1)}, f32[384]{0:T(512)}, u32[]{:S(2)}) copy-start(f32[384]{0:T(512)} %get-tuple-element.87) | copy-start | bytes 4612
  476.1 6.8 %copy-start.155 = (f32[48]{0:T(128)S(1)}, f32[48]{0:T(128)}, u32[]{:S(2)}) copy-start(f32[48]{0:T(128)} %param.38) | copy-start | bytes 580
  476.1 6.9 %copy-start.47 = (bf16[1024,384]{1,0:T(8,128)(2,1)S(1)}, bf16[1024,384]{1,0:T(8,128)(2,1)}, u32[]{:S(2)}) copy-start(bf16[1024,384]{1,0:T(8,128)(2,1)} %copy-done.46) | copy-start | bytes 2359300
  476.1 6.9 %copy-start.62 = (bf16[1024,128]{1,0:T(8,128)(2,1)S(1)}, bf16[1024,128]{1,0:T(8,128)(2,1)}, u32[]{:S(2)}) copy-start(bf16[1024,128]{1,0:T(8,128)(2,1)} %copy-done.61) | copy-start | bytes 786436
  532.6 19.1 %copy-start.25 = (bf16[1,128,2048]{2,1,0:T(8,128)(2,1)S(1)}, bf16[1,128,2048]{2,1,0:T(8,128)(2,1)}, u32[]{:S(2)}) copy-start(bf16[1,128,2048]{2,1,0:T(8,128)(2,1)} %param.24) | copy-start | bytes 1572868
  532.6 19.1 %copy-start.126 = (f32[128]{0:T(128)S(1)}, f32[128]{0:T(128)}, u32[]{:S(2)}) copy-start(f32[128]{0:T(128)} %copy-done.124) | copy-start | bytes 1540
  551.8 6.0 %copy-start.77 = (bf16[64,3072]{1,0:T(8,128)(2,1)S(1)}, bf16[64,3072]{1,0:T(8,128)(2,1)}, u32[]{:S(2)}) copy-start(bf16[64,3072]{1,0:T(8,128)(2,1)} %get-tuple-element.76) | copy-start | bytes 1179652
  553.4 5.3 copy-start.86
  553.4 6.0 %copy-start.7 = (f32[128,2048]{1,0:T(8,128)S(1)}, f32[128,2048]{1,0:T(8,128)}, u32[]{:S(2)}) copy-start(f32[128,2048]{1,0:T(8,128)} %copy-done.6) | copy-start | bytes 3145732
  553.4 6.0 %copy-start.44 = (f32[128,2048]{1,0:T(8,128)S(1)}, f32[128,2048]{1,0:T(8,128)}, u32[]{:S(2)}) copy-start(f32[128,2048]{1,0:T(8,128)} %get-tuple-element.70) | copy-start | bytes 3145732
  553.4 6.0 %copy-start.52 = (bf16[1,128,2048]{2,1,0:T(8,128)(2,1)S(1)}, bf16[1,128,2048]{2,1,0:T(8,128)(2,1)}, u32[]{:S(2)}) copy-start(bf16[1,128,2048]{2,1,0:T(8,128)(2,1)} %param.25) | copy-start | bytes 1572868
  553.4 6.0 %copy-start.129 = (f32[128]{0:T(128)S(1)}, f32[128]{0:T(128)}, u32[]{:S(2)}) copy-start(f32[128]{0:T(128)} %copy-done.128) | copy-start | bytes 1540
  553.4 6.0 %copy-start.145 = (f32[128]{0:T(128)S(1)}, f32[128]{0:T(128)}, u32[]{:S(2)}) copy-start(f32[128]{0:T(128)} %copy-done.144) | copy-start | bytes 1540
  (113 other events, 250.9 us)
Sparse Core Ops, SparseCore 0:
  95.4 44.1 all-gather.6
  141.2 79.4 all-gather.10
  222.3 44.4 all-gather.8
  268.9 42.5 reduce-scatter.5
  313.8 76.0 reduce-scatter.7
  392.0 44.4 reduce-scatter.9
  438.9 43.0 reduce-scatter.11
  484.3 43.1 reduce-scatter.13

commit v5 on v4

--- a/solution.py
+++ b/solution.py
@@ -954,16 +954,14 @@
     )(partial_sum.astype(BF), *waits)
 
 
-def row_sum_kernel(x_ref, o_ref, got, send_sem, recv_sem):
-    me = lax.axis_index(CTX)
-    greet([(CTX, (me + j) % PLANE) for j in range(1, PLANE)])
+def row_sum_steps(x_ref, o_ref, got, send_sem, recv_sem):
     copies = []
-    for j in range(1, PLANE):
-        copy = remote(
-            x_ref, got.at[j - 1], send_sem.at[j - 1], recv_sem.at[j - 1], CTX, (me + j) % PLANE
-        )
+    for j, (axis, other) in enumerate(other_places(CTX, PLANE)):
+        copy = remote(x_ref, got.at[j], send_sem.at[j], recv_sem.at[j], axis, other)
         copy.start()
         copies.append(copy)
+    for _ in range(3):
+        yield True
     total = x_ref[...]
     for j, copy in enumerate(copies):
         copy.wait_recv()
@@ -971,6 +969,56 @@
     o_ref[...] = total
     for copy in copies:
         copy.wait_send()
+
+
+def row_sum_kernel(*refs):
+    greet(other_places(CTX, PLANE))
+    together(row_sum_steps(*refs))
+
+
+def row_sum_beside_kernel(seqs, head, x_ref, a, b, o_ref, o, *scratch):
+    first = head // seqs
+    second = o.shape[1] - first
+
+    def stores(made):
+        return [
+            (made.at[pl.ds(f * first, first)], o.at[f, pl.ds(0, first)]) for f in range(seqs)
+        ] + [
+            (made.at[pl.ds(head + f * second, second)], o.at[f, pl.ds(first, second)])
+            for f in range(seqs)
+        ]
+
+    greet(other_places(CTX, PLANE))
+    together(
+        row_sum_steps(x_ref, o_ref, *scratch[:3]),
+        product_steps(1, 256, 1, stores, a, b, *scratch[3:]),
+    )
+
+
+def row_sum_beside(rows, a, b, head, seqs, ids, waits=()):
+    anywhere = pl.BlockSpec(memory_space=pl.ANY)
+    near = pl.BlockSpec(memory_space=pltpu.VMEM)
+    tile = rows.reshape(8, -1)
+    total, product = pl.pallas_call(
+        unused(partial(row_sum_beside_kernel, seqs, head), 3, len(waits)),
+        out_shape=(
+            jax.ShapeDtypeStruct(tile.shape, F32),
+            jax.ShapeDtypeStruct((seqs, a.shape[1] // seqs, b.shape[1]), BF),
+        ),
+        in_specs=[near] + [anywhere] * (2 + len(waits)),
+        out_specs=(near, anywhere),
+        scratch_shapes=[
+            pltpu.VMEM((PLANE - 1,) + tile.shape, F32),
+            pltpu.SemaphoreType.DMA((PLANE - 1,)),
+            pltpu.SemaphoreType.DMA((PLANE - 1,)),
+        ]
+        + product_scratch(1, a, b, 2 * seqs),
+        cost_estimate=lasting(8),
+        compiler_params=pltpu.CompilerParams(
+            collective_id=next(ids), has_side_effects=True, vmem_limit_bytes=40 * 2**20
+        ),
+    )(tile, a, b, *waits)
+    return total.reshape(rows.shape), product
 
 
 def row_sum(rows, ids, waits=()):
@@ -1176,7 +1224,7 @@
         copy.wait_send()
 
 
-def product_steps(kind, block, rounds, a_any, b_any, o_any, a, b, o, sems):
+def product_steps(kind, block, rounds, stores, a_any, b_any, a, b, o, sems):
     loads = [
         pltpu.make_async_copy(src, dst, sems.at[k])
         for k, (src, dst) in enumerate(((a_any, a), (b_any, b)))
@@ -1203,19 +1251,23 @@
 
         lax.fori_loop(first, min(first + per, count), one, 0)
         yield True
-    store = pltpu.make_async_copy(o, o_any, sems.at[2])
-    store.start()
+    copies = [
+        pltpu.make_async_copy(src, dst, sems.at[2 + k]) for k, (src, dst) in enumerate(stores(o))
+    ]
+    for copy in copies:
+        copy.start()
     yield True
-    store.wait()
-
-
-def product_scratch(kind, a, b):
+    for copy in copies:
+        copy.wait()
+
+
+def product_scratch(kind, a, b, stores=1):
     rows = a.shape[1] if kind else a.shape[0]
     return [
         pltpu.VMEM(a.shape, BF),
         pltpu.VMEM(b.shape, BF),
         pltpu.VMEM((rows, b.shape[1]), BF),
-        pltpu.SemaphoreType.DMA((3,)),
+        pltpu.SemaphoreType.DMA((2 + stores,)),
     ]
 
 
@@ -1224,7 +1276,7 @@
     greet([(CTX, sibling), (CTX, by_x), (CTX, by_y)])
     together(
         scatter_steps(seqs, p_ref, o_ref, *scratch[:10]),
-        product_steps(1, 256, 3, a, b, o, *scratch[10:]),
+        product_steps(1, 256, 3, lambda made: [(made, o)], a, b, *scratch[10:]),
     )
 
 
@@ -1252,7 +1304,7 @@
     greet([(CTX, sibling), (CTX, by_x), (CTX, by_y)])
     together(
         gather_steps(pieces, x_ref, o_ref, *scratch[:3]),
-        product_steps(0, 256, 4, a, b, o, *scratch[3:]),
+        product_steps(0, 256, 4, lambda made: [(made, o)], a, b, *scratch[3:]),
     )
 
 
@@ -1483,7 +1535,7 @@
     key[...] = jnp.concatenate(turned, axis=1)
 
 
-def last_exchange(small, conv, inner, kv, seqs, ids):
+def last_exchange(small, conv, inner, kv, seqs, ids, waits=()):
     anywhere = pl.BlockSpec(memory_space=pl.ANY)
     near = pl.BlockSpec(memory_space=pltpu.VMEM)
     _, krows, cols = conv.shape
@@ -1493,7 +1545,7 @@
 
     two = [pltpu.SemaphoreType.DMA((PLANE + seqs,)), pltpu.SemaphoreType.DMA((PLANE + seqs,))]
     return pl.pallas_call(
-        partial(last_kernel, seqs),
+        unused(partial(last_kernel, seqs), 7, len(waits)),
         out_shape=(
             jax.ShapeDtypeStruct((16, 128), F32),
             jax.ShapeDtypeStruct((PLANE, 8, 128), F32),
@@ -1501,7 +1553,7 @@
             jax.ShapeDtypeStruct((krows, PLANE * kv), F32),
             jax.ShapeDtypeStruct((krows, PLANE * kv), F32),
         ),
-        in_specs=[anywhere] * 7,
+        in_specs=[anywhere] * (7 + len(waits)),
         out_specs=(near,) * 5,
         scratch_shapes=[
             pltpu.VMEM((PLANE, krows, cols - inner), BF),
@@ -1526,7 +1578,7 @@
         compiler_params=pltpu.CompilerParams(
             collective_id=next(ids), has_side_effects=True, vmem_limit_bytes=40 * 2**20
         ),
-    )(*small, conv)
+    )(*small, conv, *waits)
 
 
 def gather_rows(shard):
@@ -1921,15 +1973,6 @@
     branch_grad, last = gather_beside(grad_mid.astype(BF), hidden, down_own, ids)
     branch_grad = hold(branch_grad, down_grad)
 
-    out_grad_own = mm_tn(mixed, branch_grad).astype(BF)
-    out_part = jnp.concatenate(
-        [
-            out_grad_own[:head].reshape(seqs, -1, width),
-            out_grad_own[head:].reshape(seqs, -1, width),
-        ],
-        axis=1,
-    )
-    out_grad_own = scatter_rows(hold(out_part, ffn_grad))
     grad_attn = mm_nt(branch_grad, out_own[:head]).astype(BF).reshape(length, -1, HEAD_SIZE)
     grad_ymix = mm_nt(branch_grad, out_own[head:])
 
@@ -1948,7 +1991,11 @@
     hat = gated * scale_mix
     turned_mix = grad_ymix * gain_mix
     mixer_gain_grad = jnp.sum(grad_ymix * hat, axis=0, keepdims=True)
-    along = row_sum(jnp.sum(turned_mix * hat, axis=-1), ids, (down_grad,))[:, None] / dssm
+    along, out_part = row_sum_beside(
+        jnp.sum(turned_mix * hat, axis=-1), mixed, branch_grad, head, seqs, ids, (down_grad,)
+    )
+    out_grad_own = scatter_rows(hold(out_part, ffn_grad))
+    along = along[:, None] / dssm
     grad_gated = scale_mix * (turned_mix - hat * along)
     grad_y, grad_zgate = gated_back(grad_gated)
 
@@ -1993,6 +2040,9 @@
     rest_grad = scatter_rows(rest_part)
     conv_grad = mm_tn(normed, grad_conv).reshape(seqs, ctx, krows, conv_cols)
     conv_grad = scatter_rows(conv_grad)
+    attn_out_grad = out_grad_own[:out_rows].astype(F32)
+    mamba_out_grad = out_grad_own[out_rows:].astype(F32)
+    down_grad = down_grad.astype(F32)
     grad_normed, norm_rows, query_grad, zgate_grad, gate_grad, up_grad = closing(
         (grad_conv, grad_rest, jnp.pad(grad_step_low, step_room)),
         (conv_in_own, rest_own, step_wide),
@@ -2002,8 +2052,10 @@
         head,
         seqs,
         ids,
-        (out_grad_own,),
-    )
+        (attn_out_grad, mamba_out_grad, down_grad),
+    )
+
+    gate_grad, up_grad = gate_grad.astype(F32), up_grad.astype(F32)
 
     sums, step_sums, channels_grad, key_grad, value_grad = last_exchange(
         (
@@ -2036,7 +2088,7 @@
         query_grad.astype(F32),
         key_grad,
         value_grad,
-        out_grad_own[:out_rows].astype(F32),
+        attn_out_grad,
         zgate_grad.astype(F32),
         channels_grad.astype(F32),
         step_grad,
@@ -2046,11 +2098,11 @@
         sums[9, :HS],
         sums[10, :HS],
         sums[2, : mixer_gain.size],
-        out_grad_own[out_rows:].astype(F32),
+        mamba_out_grad,
         sums[0, :krows],
-        gate_grad.astype(F32),
-        up_grad.astype(F32),
-        down_grad.astype(F32),
+        gate_grad,
+        up_grad,
+        down_grad,
     )
 
 

time: 576 us -> 570 us (0.990)
  other arithmetic: 83.9 us -> 76.8 us
    pallas_call x1 -> x2, Pallas kernels: 14.9 us -> 21.1 us  [the longest x1 14.9 us: last_exchange(): pl.pallas_call(unused(partial(last_kernel, seqs), 7, len(waits)), out_sha...]
    pallas_call x2 -> x1, Pallas kernels: 12.2 us -> 6.13 us  [row_sum(): pl.pallas_call(unused(row_sum_kernel, 1, len(waits)), out_shape=jax.Shape...]
    dot_general x14 -> x13, matrix products: 65.5 us -> 63.9 us  [dotf(): lax.dot_general(left, right, (dims, ((), ())), preferred_element_type=F32)]
    unnamed x345 -> x349, local copies, waits for them, and re-layouts: 38.9 us -> 38.1 us
  transfers between devices with their start and end apart: 8 -> 8, of which waited for: 1 -> 3; matrix products, arithmetic and copies ran while one was open for 35% -> 34% of each run, Pallas kernels for 33% -> 34%
where the time goes in v5:
time: 570 us; the launch traced here: 565 us
  Pallas kernels  286 us (50%)
  matrix products  91.2 us (16%)
  local copies, waits for them, and re-layouts  78.3 us (14%)
  other arithmetic  76.8 us (13%)
  between operations  16.9 us (3%)
  waiting for transfers between devices  15.4 us (3%)
    pallas_call x1, Pallas kernels, opening(): pl.pallas_call(partial(opening_kernel, seqs, pieces), out_shape=(shape(PL...  80.6 us
    dot_general x13, matrix products, dotf(): lax.dot_general(left, right, (dims, ((), ())), preferred_element_type=F32)  63.9 us
    pallas_call x1, Pallas kernels, closing(): pl.pallas_call(unused(partial(closing_kernel, seqs), 9, len(waits)), out_...  41.8 us
    unnamed x349, local copies, waits for them, and re-layouts  38.1 us
    pallas_call x2, Pallas kernels, gather_tokens(): pl.pallas_call(unused(partial(gather_kernel, pieces), 1, len(waits)), out...  35.4 us
    pallas_call x1, Pallas kernels, scatter_two(): pl.pallas_call(unused(scatter_two_kernel, 2, len(waits)), out_shape=tuple...  31.6 us
    pallas_call x1, Pallas kernels, scatter_beside(): pl.pallas_call(unused(partial(scatter_beside_kernel, seqs), 3, len(waits)...  25.1 us
    pallas_call x1, Pallas kernels, scatter_tokens(): pl.pallas_call(unused(partial(scatter_kernel, seqs), 1, len(waits)), out_...  22.3 us
  transfers between devices with their start and end apart: 8, of which 3 were waited for; matrix products, arithmetic and copies ran while one was open for 34% of the time, Pallas kernels for 34%

profile of v5, /device:TPU:0, one launch (start us, length us, event | category | flops | bytes accessed | tf_op | source)
XLA Modules:
  0.0 564.9 jit_solution(14172529227323257436)
XLA Ops:
  14.6 80.6 %shard_map.373 = (bf16[8,4,32,128]{3,2,1,0:T(8,128)(2,1)}, bf16[4,128,2048]{2,1,0:T(8,128)(2,1)}, bf16[1024,2048]{1,0:T(8,128)(2,1)}, bf16[1024,2048]{1,0:T(8,12...) custom-call(bf16[32,128]{1,0:T(8,128)(2,1)} %pad_bitcast_fusion.refs, ...), custom_call_target="tpu_custom_call" | custom-call | flops 20999999488 | bytes 21000000 | tf_op jit(solution)/shard_map/pallas_call | solution.py:1168
  98.7 6.9 %fusion.136 = (bf16[1024,512]{1,0:T(8,128)(2,1)S(1)}, f32[1024,512]{1,0:T(8,128)}) fusion(bf16[2048,512]{1,0:T(8,128)(2,1)} %bitcast.483, bf16[1024,2048]{1,0:T(8,128)(2,1)} %get-tuple-element.60, f32[2048]{0:T(1024)S(1)} %reshape.796), kind=kOutput, calls=%fused_computation.296 | convolution fusion | flops 2154299392 | bytes 9445376 | tf_op jit(solution)/shard_map/dot_general | solution.py:611
  109.4 3.2 multiply_convert_fusion.5
  114.6 4.5 compare_select_fusion.2
  119.5 1.7 reduce_window_sum.17
  127.3 3.8 fusion.76
  133.4 13.4 %shard_map.374 = bf16[1024,1024]{1,0:T(8,128)(2,1)} custom-call(bf16[128,1024]{1,0:T(8,128)(2,1)} %copy.393.refs_0_), custom_call_target="tpu_custom_call" | custom-call | flops 2400000000 | bytes 2400000 | tf_op jit(solution)/shard_map/pallas_call | solution.py:818
  146.8 2.1 fusion.133
  158.2 3.1 multiply_reduce_fusion.1
  166.7 5.3 fusion.22
  174.2 6.1 %shard_map.375 = f32[8,128]{1,0:T(8,128)} custom-call(f32[8,128]{1,0:T(8,128)} %bitcast.475), custom_call_target="tpu_custom_call" | custom-call | flops 1500000000 | bytes 1500000 | tf_op jit(solution)/shard_map/pallas_call | solution.py:1026
  181.0 2.8 fusion.100
  185.0 1.8 fusion.7
  187.1 1.6 fusion.43
  190.6 2.3 convolution_convert_fusion.refs_0_
  193.0 22.3 %shard_map.376 = f32[128,2048]{1,0:T(8,128)S(1)} custom-call(bf16[1024,2048]{1,0:T(8,128)(2,1)S(1)} %convolution_convert_fusion.refs_0_), custom_call_target="tpu_custom_call" | custom-call | flops 6600000000 | bytes 6600000 | tf_op jit(solution)/shard_map/pallas_call | solution.py:944
  219.1 21.9 %shard_map.377.refs_1_ = bf16[1024,2048]{1,0:T(8,128)(2,1)} custom-call(bf16[128,2048]{1,0:T(8,128)(2,1)} %copy.422.refs_0_), custom_call_target="tpu_custom_call" | custom-call | flops 6600000000 | bytes 6600000 | tf_op jit(solution)/shard_map/pallas_call | solution.py:818
  241.0 7.7 %fusion.138 = f32[1024,1024]{1,0:T(8,128)S(1)} fusion(bf16[1024,2048]{1,0:T(8,128)(2,1)} %shard_map.377.refs_1_, bf16[2048,1024]{1,0:T(8,128)(2,1)} %bitcast.478), kind=kOutput, calls=%fused_computation.298 | convolution fusion | flops 4294967296 | bytes 12582912 | tf_op jit(solution)/shard_map/dot_general | solution.py:611
  250.9 1.6 copy-done.168
  252.5 3.8 convolution_convert_fusion.4
  256.4 10.3 %all-gather.9.cloned.1.call-done.refs_0_ = bf16[512,2048]{1,0:T(8,128)(2,1)} async-done(((bf16[128,2048]{1,0:T(8,128)(2,1)}), bf16[512,2048]{1,0:T(8,128)(2,1)}) %all-gather.9.cloned.1.call-update) | async-done | bytes 2097168 | tf_op jit(solution)/shard_map/all_gather | solution.py:1585
  266.7 7.2 %multiply_convert_fusion.3 = (bf16[1024,512]{1,0:T(8,128)(2,1)S(1)}, bf16[1024,512]{1,0:T(8,128)(2,1)S(1)}) fusion(f32[1024,1024]{1,0:T(8,128)} %copy-done.52, bf16[1024,2048]{1,0:T(8,128)(2,1)} %get-tuple-element.64, bf16[512,2048]{1,0:T(8,128)(2,1)} %shard_map.378.b), kind=kOutput, calls=%fused_computation.54 | convolution fusion | flops 2153775104 | bytes 12582912 | tf_op jit(solution)/shard_map/dot_general | solution.py:611
  274.2 1.9 copy-done.161
  276.1 4.8 convolution_convert_fusion.1.refs_0_
  280.9 25.1 %shard_map.379 = (f32[128,2048]{1,0:T(8,128)S(1)}, bf16[2048,1024]{1,0:T(8,128)(2,1)S(1)}) custom-call(bf16[1024,2048]{1,0:T(8,128)(2,1)S(1)} %convolution_convert_fusion.1.refs_0_, bf16[1024,2048]{1,0:T(8,128)(2,1)} %shard_map.377.refs_1_, bf16[1024,1024]{1,0:T(8,128)(2,1)S(1)} %pad_maximum_fusion.refs_2_), custom_call_target="tpu_custom_call" | custom-call | flops 7500000256 | bytes 7500000 | tf_op jit(solution)/shard_map/pallas_call | solution.py:1286
  306.0 2.0 copy-done.1
  311.3 1.6 multiply_reduce_fusion.15
  314.5 21.9 %shard_map.380 = (bf16[1024,2048]{1,0:T(8,128)(2,1)S(1)}, bf16[1024,2048]{1,0:T(8,128)(2,1)S(1)}) custom-call(bf16[128,2048]{1,0:T(8,128)(2,1)S(1)} %fusion.127.x_ref, bf16[1024,512]{1,0:T(8,128)(2,1)S(1)} %multiply_convert_fusion.4.a, bf16[512,2048]{1,0:T(8,128)(2,1)S(1)} %copy-done.4), custom_call_target="tpu_custom_call" | custom-call | flops 6600000000 | bytes 6600000 | tf_op jit(solution)/shard_map/pallas_call | solution.py:1314
  336.4 2.0 copy-done.2
  338.5 2.0 copy-done.11
  340.5 6.3 %multiply_reduce_fusion.11 = (f32[384]{0:T(512)}, f32[1024]{0:T(1024)S(1)}, f32[1024,384]{1,0:T(8,128)S(1)}) fusion(f32[1024,384]{1,0:T(8,128)} %copy-done.29, f32[1024]{0:T(1024)S(1)} %rsqrt_bitcast_fusion, f32[384]{0:T(512)S(1)} %dynamic-slice_convert_fusion.1, bf16[1024,2048]{1,0:T(8,128)(2,1)} %shard_map.381.refs_2_, bf16[384,2048]{1,0:T(8,128)(2,1)} %bitcast.417), kind=kOutput, calls=%fused_computation.83 | convolution fusion | flops 1612970624 | bytes 8924160 | tf_op jit(solution)/shard_map/dot_general | solution.py:611
  346.9 6.2 %shard_map.382 = (f32[8,128]{1,0:T(8,128)S(1)}, bf16[4,128,2048]{2,1,0:T(8,128)(2,1)S(1)}) custom-call(f32[8,128]{1,0:T(8,128)S(1)} %bitcast.371, bf16[1024,512]{1,0:T(8,128)(2,1)S(1)} %pad_maximum_fusion.3.refs_1_, bf16[1024,2048]{1,0:T(8,128)(2,1)S(1)} %copy-done.3, bf16[128,2048]{1,0:T(8,128)(2,1)S(1)} %bitcast.361), custom_call_target="tpu_custom_call" | custom-call | flops 2400000000 | bytes 2400000 | tf_op jit(solution)/shard_map/pallas_call | solution.py:1002
  353.1 2.8 multiply_reduce_fusion.10
  355.9 1.7 copy.427
  357.6 1.8 copy.479
  360.1 3.1 multiply_reduce_fusion
  368.8 3.1 copy.444
  371.9 2.9 convolution_bitcast_fusion.1
  374.8 3.7 multiply_reduce_fusion.5
  381.3 2.3 copy.433
  383.5 4.6 convolution_convert_fusion.5
  388.1 1.7 reduce-scatter.8.cloned.1.call-done
  390.8 4.1 fusion
  394.9 2.4 fusion.10
  402.0 2.7 fusion.34
  404.8 2.2 fusion.85
  407.2 3.7 convolution_convert_fusion.3
  410.9 3.0 fusion.39
  415.9 1.6 pad_maximum_fusion.1
  421.3 31.6 %shard_map.383 = (f32[128,1024]{1,0:T(8,128)S(1)}, f32[128,2048]{1,0:T(8,128)S(1)}) custom-call(bf16[1024,1024]{1,0:T(8,128)(2,1)S(1)} %bitcast.364, bf16[1024,2048]{1,0:T(8,128)(2,1)S(1)} %copy-done.12, bf16[8,64,1024]{2,1,0:T(8,128)(2,1)S(1)} %bitcast.367, bf16[4,8,64,512]{3,2,1,0:T(8,128)(2,1)S(1)} %bitcast.363), custom_call_target="tpu_custom_call" | custom-call | flops 8400000000 | bytes 8400000 | tf_op jit(solution)/shard_map/pallas_call | solution.py:1347
  454.3 2.2 fusion.79
  456.8 4.5 multiply_reduce_fusion.8
  464.5 3.7 convolution_convert_fusion.2
  470.1 1.9 reduce_window_sum.18
  472.7 1.5 fusion.128
  476.1 3.0 fusion.20.refs_5_
  480.3 1.6 fusion.103.refs_9_
  481.9 1.9 fusion.97.refs_10_
  483.9 41.8 %shard_map.385 = (f32[128,2048]{1,0:T(8,128)}, f32[8,4,8,128]{3,2,1,0:T(8,128)}, bf16[64,1024]{1,0:T(8,128)(2,1)}, bf16[64,3072]{1,0:T(8,128)(2,1)}, bf16[64,4096]{1,0:T(8,128)(2,1)}, /*index=5*/bf16[64,4096]{1,0:T(8,128)(2,1)}) custom-call(bf16[1024,512]{1,0:T(8,128)(2,1)} %copy-done.68, bf16[1024,512]{1,0:T(8,128)(2,1)} %pad_maximum_fusion.4.refs_1_, ...), custom_call_target="tpu_custom_call" | custom-call | flops 10499999744 | bytes 10500000 | tf_op jit(solution)/shard_map/pallas_call | solution.py:1418
  525.6 1.9 reduce-scatter.14.cloned.1.call-done
  529.5 14.9 %shard_map.386 = (f32[16,128]{1,0:T(8,128)S(1)}, f32[8,8,128]{2,1,0:T(8,128)S(1)}, bf16[64,3584]{1,0:T(8,128)(2,1)S(1)}, f32[64,256]{1,0:T(8,128)S(1)}, f32[64,256]{1,0:T(8,128)S(1)}) custom-call(f32[8,4,8,128]{3,2,1,0:T(8,128)S(1)} %copy-done.13, f32[1,2048]{1,0:T(1,128)S(1)} %bitcast.369, f32[1,384]{1,0:T(1,128)S(1)} %broadcast_in_dim.216.refs_2_, ...), custom_call_target="tpu_custom_call" | custom-call | flops 4499999744 | bytes 4500000 | tf_op jit(solution)/shard_map/pallas_call | solution.py:1547
  549.0 2.2 convert_element_type.396
  551.3 2.1 convert_element_type.397
  555.0 1.5 fusion.89
  (542 shorter events, 96.4 us)
Async XLA Ops:
  7.2 159.5 %all-gather.7.cloned.1.call-start = ((), (), s32[]{:S(2)}) async-start(), calls=%async_computation.10 | async-start | bytes 2621440 | tf_op jit(solution)/shard_map/all_gather | solution.py:1585
  95.2 145.8 %all-gather.11.cloned.1.call-start = ((), (), s32[]{:S(2)}) async-start(), calls=%async_computation.12 | async-start | bytes 5242880 | tf_op jit(solution)/shard_map/all_gather | solution.py:1585
  96.0 170.7 %all-gather.9.cloned.1.call-start = ((), (), s32[]{:S(2)}) async-start(), calls=%async_computation.11 | async-start | bytes 2621440 | tf_op jit(solution)/shard_map/all_gather | solution.py:1585
  96.7 243.7 %reduce-scatter.6.cloned.1.call-start = ((), (), s32[]{:S(2)}) async-start(), calls=%async_computation.5 | async-start | bytes 2621440 | tf_op jit(solution)/shard_map/reduce_scatter | solution.py:1589
  97.1 12.0 %copy-start.67 = (bf16[4,8,32,128]{3,1,2,0:T(8,128)(2,1)}, bf16[4,8,32,128]{3,1,2,0:T(8,128)(2,1)S(1)}, u32[]{:S(2)}) copy-start(bf16[4,8,32,128]{3,1,2,0:T(8,128)(2,1)S(1)} %copy.527) | copy-start | bytes 786436
  98.7 68.0 %copy-start.100 = (f32[2048]{0:T(1024)}, f32[2048]{0:T(1024)S(1)}, u32[]{:S(2)}) copy-start(f32[2048]{0:T(1024)S(1)} %reshape.796) | copy-start | bytes 24580
  106.6 6.0 %copy-start.22 = (f32[1024,448]{1,0:T(8,128)}, f32[1024,448]{1,0:T(8,128)S(1)}, u32[]{:S(2)}) copy-start(f32[1024,448]{1,0:T(8,128)S(1)} %slice_convert_fusion) | copy-start | bytes 5505028
  114.5 4.6 copy-start.62
  114.6 4.7 copy-start.159
  114.6 10.6 %copy-start.59 = (bf16[4,128,2048]{2,1,0:T(8,128)(2,1)S(1)}, bf16[4,128,2048]{2,1,0:T(8,128)(2,1)}, u32[]{:S(2)}) copy-start(bf16[4,128,2048]{2,1,0:T(8,128)(2,1)} %get-tuple-element.63) | copy-start | bytes 6291460
  119.4 32.1 %copy-start.75 = (f32[8,128,6]{1,0,2:T(8,128)}, f32[8,128,6]{1,0,2:T(8,128)S(1)}, u32[]{:S(2)}) copy-start(f32[8,128,6]{1,0,2:T(8,128)S(1)} %copy.400) | copy-start | bytes 73732
  121.2 35.5 %copy-start.65 = (f32[8,6,128]{2,0,1:T(8,128)}, f32[8,6,128]{2,0,1:T(8,128)S(1)}, u32[]{:S(2)}) copy-start(f32[8,6,128]{2,0,1:T(8,128)S(1)} %reduce_window_sum.17) | copy-start | bytes 73732
  121.4 30.1 %copy-start.98 = (f32[8,6,1]{0,1,2:T(8,128)}, f32[8,6,1]{0,1,2:T(8,128)S(1)}, u32[]{:S(2)}) copy-start(f32[8,6,1]{0,1,2:T(8,128)S(1)} %copy.470) | copy-start | bytes 580
  127.3 19.5 %copy-start.149 = (f32[16]{0:T(128)}, f32[16]{0:T(128)S(1)}, u32[]{:S(2)}) copy-start(f32[16]{0:T(128)S(1)} %multiply_power_fusion.1) | copy-start | bytes 196
  151.2 6.4 %copy-start.33 = (bf16[1024,256]{1,0:T(8,128)(2,1)}, bf16[1024,256]{1,0:T(8,128)(2,1)S(1)}, u32[]{:S(2)}) copy-start(bf16[1024,256]{1,0:T(8,128)(2,1)S(1)} %get-tuple-element.123) | copy-start | bytes 1572868
  151.2 10.0 %copy-start.36 = (bf16[1024,256]{1,0:T(8,128)(2,1)}, bf16[1024,256]{1,0:T(8,128)(2,1)S(1)}, u32[]{:S(2)}) copy-start(bf16[1024,256]{1,0:T(8,128)(2,1)S(1)} %get-tuple-element.124) | copy-start | bytes 1572868
  151.5 5.5 copy-start.132
  152.2 4.7 copy-start.164
  152.2 4.8 copy-start.97
  154.7 7.1 %copy-start.39 = (bf16[48,8,8,128]{3,2,1,0:T(8,128)(2,1)}, bf16[48,8,8,128]{3,2,1,0:T(8,128)(2,1)S(1)}, u32[]{:S(2)}) copy-start(bf16[48,8,8,128]{3,2,1,0:T(8,128)(2,1)S(1)} %copy.477) | copy-start | bytes 2359300
  157.0 4.9 copy-start.104
  157.1 4.8 copy-start.166
  157.3 4.6 copy-start.92
  157.6 4.3 copy-start.77
  166.3 6.7 %copy-start.27 = (f32[1024,384]{1,0:T(8,128)}, f32[1024,384]{1,0:T(8,128)S(1)}, u32[]{:S(2)}) copy-start(f32[1024,384]{1,0:T(8,128)S(1)} %copy.419) | copy-start | bytes 4718596
  174.1 14.6 %copy-start.29 = (f32[1024,384]{1,0:T(8,128)}, f32[1024,384]{1,0:T(8,128)S(1)}, u32[]{:S(2)}) copy-start(f32[1024,384]{1,0:T(8,128)S(1)} %get-tuple-element.105) | copy-start | bytes 4718596
  174.1 6.8 %copy-start.51 = (f32[1024,1,128]{2,0,1:T(8,128)S(1)}, f32[1024,1,128]{2,0,1:T(8,128)}, u32[]{:S(2)}) copy-start(f32[1024,1,128]{2,0,1:T(8,128)} %slice_bitcast_fusion) | copy-start | bytes 1572868
  174.2 6.8 %copy-start.147 = (f32[64]{0:T(128)S(1)}, f32[64]{0:T(128)}, u32[]{:S(2)}) copy-start(f32[64]{0:T(128)} %multiply_power_fusion) | copy-start | bytes 772
  174.2 9.7 %copy-start.72 = (bf16[2,4,16,1024]{3,2,1,0:T(8,128)(2,1)S(1)}, bf16[2,4,16,1024]{3,2,1,0:T(8,128)(2,1)}, u32[]{:S(2)}) copy-start(bf16[2,4,16,1024]{3,2,1,0:T(8,128)(2,1)} %copy.394) | copy-start | bytes 786436
  193.0 22.3 %copy-start.31 = (bf16[1,128,2048]{2,1,0:T(8,128)(2,1)S(1)}, bf16[1,128,2048]{2,1,0:T(8,128)(2,1)}, u32[]{:S(2)}) copy-start(bf16[1,128,2048]{2,1,0:T(8,128)(2,1)} %param.24) | copy-start | bytes 1572868
  193.0 22.3 %copy-start.135 = (f32[128]{0:T(128)S(1)}, f32[128]{0:T(128)}, u32[]{:S(2)}) copy-start(f32[128]{0:T(128)} %copy-done.134) | copy-start | bytes 1540
  216.6 96.3 %copy-start.138 = (f32[128]{0:T(128)}, f32[128]{0:T(128)S(1)}, u32[]{:S(2)}) copy-start(f32[128]{0:T(128)S(1)} %add_rsqrt_fusion) | copy-start | bytes 1540
  256.3 133.5 %reduce-scatter.8.cloned.1.call-start = ((), (), s32[]{:S(2)}) async-start(), calls=%async_computation.6 | async-start | bytes 5242880 | tf_op jit(solution)/shard_map/reduce_scatter | solution.py:1589
  308.0 172.3 %reduce-scatter.12.cloned.1.call-start = ((), (), s32[]{:S(2)}) async-start(), calls=%async_computation.8 | async-start | bytes 2621440 | tf_op jit(solution)/shard_map/reduce_scatter | solution.py:1589
  312.9 23.5 %copy-start.151 = (f32[128]{0:T(128)}, f32[128]{0:T(128)S(1)}, u32[]{:S(2)}) copy-start(f32[128]{0:T(128)S(1)} %broadcast_multiply_fusion.2) | copy-start | bytes 1540
  340.5 6.3 %copy-start.3 = (bf16[1024,2048]{1,0:T(8,128)(2,1)S(1)}, bf16[1024,2048]{1,0:T(8,128)(2,1)}, u32[]{:S(2)}) copy-start(bf16[1024,2048]{1,0:T(8,128)(2,1)} %shard_map.381.refs_2_) | copy-start | bytes 12582916
  340.5 6.3 %copy-start.5 = (bf16[1,128,2048]{2,1,0:T(8,128)(2,1)S(1)}, bf16[1,128,2048]{2,1,0:T(8,128)(2,1)}, u32[]{:S(2)}) copy-start(bf16[1,128,2048]{2,1,0:T(8,128)(2,1)} %reduce-scatter.6.cloned.1.call-done) | copy-start | bytes 1572868
  346.8 6.2 %copy-start.28 = (f32[1024,384]{1,0:T(8,128)S(1)}, f32[1024,384]{1,0:T(8,128)}, u32[]{:S(2)}) copy-start(f32[1024,384]{1,0:T(8,128)} %copy-done.27) | copy-start | bytes 4718596
  346.8 6.2 %copy-start.30 = (f32[1024,384]{1,0:T(8,128)S(1)}, f32[1024,384]{1,0:T(8,128)}, u32[]{:S(2)}) copy-start(f32[1024,384]{1,0:T(8,128)} %copy-done.29) | copy-start | bytes 4718596
  346.8 6.2 %copy-start.44 = (bf16[1024,448]{1,0:T(8,128)(2,1)S(1)}, bf16[1024,448]{1,0:T(8,128)(2,1)}, u32[]{:S(2)}) copy-start(bf16[1024,448]{1,0:T(8,128)(2,1)} %copy-done.43) | copy-start | bytes 2752516
  346.8 6.2 %copy-start.46 = (f32[1024,512]{1,0:T(8,128)S(1)}, f32[1024,512]{1,0:T(8,128)}, u32[]{:S(2)}) copy-start(f32[1024,512]{1,0:T(8,128)} %copy-done.45) | copy-start | bytes 6291460
  359.5 5.5 copy-start.73
  389.9 94.0 %reduce-scatter.10.cloned.1.call-start = ((), (), s32[]{:S(2)}) async-start(), calls=%async_computation.7 | async-start | bytes 2621440 | tf_op jit(solution)/shard_map/reduce_scatter | solution.py:1589
  400.2 4.6 copy-start.148
  402.0 5.2 copy-start.53
  413.9 113.6 %reduce-scatter.14.cloned.1.call-start = ((), (), s32[]{:S(2)}) async-start(), calls=%async_computation.9 | async-start | bytes 2621440 | tf_op jit(solution)/shard_map/reduce_scatter | solution.py:1589
  421.3 33.0 %copy-start.150 = (f32[16]{0:T(128)S(1)}, f32[16]{0:T(128)}, u32[]{:S(2)}) copy-start(f32[16]{0:T(128)} %copy-done.149) | copy-start | bytes 196
  456.8 4.5 copy-start.111
  456.8 4.5 copy-start.113
  456.8 4.5 copy-start.115
  456.8 4.5 copy-start.117
  468.3 6.7 %copy-start.153 = (f32[384]{0:T(512)S(1)}, f32[384]{0:T(512)}, u32[]{:S(2)}) copy-start(f32[384]{0:T(512)} %get-tuple-element.91) | copy-start | bytes 4612
  468.3 6.7 %copy-start.160 = (f32[48]{0:T(128)S(1)}, f32[48]{0:T(128)}, u32[]{:S(2)}) copy-start(f32[48]{0:T(128)} %param.38) | copy-start | bytes 580
  468.3 6.7 %copy-start.57 = (bf16[1024,384]{1,0:T(8,128)(2,1)S(1)}, bf16[1024,384]{1,0:T(8,128)(2,1)}, u32[]{:S(2)}) copy-start(bf16[1024,384]{1,0:T(8,128)(2,1)} %get-tuple-element.110) | copy-start | bytes 2359300
  468.3 6.7 %copy-start.71 = (bf16[1024,128]{1,0:T(8,128)(2,1)S(1)}, bf16[1024,128]{1,0:T(8,128)(2,1)}, u32[]{:S(2)}) copy-start(bf16[1024,128]{1,0:T(8,128)(2,1)} %copy-done.70) | copy-start | bytes 786436
  529.5 19.2 %copy-start.32 = (bf16[1,128,2048]{2,1,0:T(8,128)(2,1)S(1)}, bf16[1,128,2048]{2,1,0:T(8,128)(2,1)}, u32[]{:S(2)}) copy-start(bf16[1,128,2048]{2,1,0:T(8,128)(2,1)} %param.24) | copy-start | bytes 1572868
  529.5 19.2 %copy-start.136 = (f32[128]{0:T(128)S(1)}, f32[128]{0:T(128)}, u32[]{:S(2)}) copy-start(f32[128]{0:T(128)} %copy-done.134) | copy-start | bytes 1540
  548.7 4.7 copy-start.82
  549.0 5.3 copy-start.91
  549.0 6.0 %copy-start.9 = (f32[128,2048]{1,0:T(8,128)S(1)}, f32[128,2048]{1,0:T(8,128)}, u32[]{:S(2)}) copy-start(f32[128,2048]{1,0:T(8,128)} %copy-done.8) | copy-start | bytes 3145732
  549.0 6.0 %copy-start.21 = (f32[128,2048]{1,0:T(8,128)S(1)}, f32[128,2048]{1,0:T(8,128)}, u32[]{:S(2)}) copy-start(f32[128,2048]{1,0:T(8,128)} %copy-done.19) | copy-start | bytes 3145732
  549.0 6.0 %copy-start.61 = (bf16[1,128,2048]{2,1,0:T(8,128)(2,1)S(1)}, bf16[1,128,2048]{2,1,0:T(8,128)(2,1)}, u32[]{:S(2)}) copy-start(bf16[1,128,2048]{2,1,0:T(8,128)(2,1)} %param.25) | copy-start | bytes 1572868
  549.0 6.0 %copy-start.139 = (f32[128]{0:T(128)S(1)}, f32[128]{0:T(128)}, u32[]{:S(2)}) copy-start(f32[128]{0:T(128)} %copy-done.138) | copy-start | bytes 1540
  549.0 6.0 %copy-start.152 = (f32[128]{0:T(128)S(1)}, f32[128]{0:T(128)}, u32[]{:S(2)}) copy-start(f32[128]{0:T(128)} %copy-done.151) | copy-start | bytes 1540
  (114 other events, 247.1 us)
Sparse Core Ops, SparseCore 0:
  95.4 44.1 all-gather.6
  141.1 79.4 all-gather.10
  222.2 44.4 all-gather.8
  268.9 42.5 reduce-scatter.5
  313.7 76.0 reduce-scatter.7
  392.0 44.3 reduce-scatter.11
  438.8 43.1 reduce-scatter.9
  484.3 43.1 reduce-scatter.13
